TPU v7x, 32 devices: a whole 2x2x4 slice. The times are simulated.
32 devices in a mesh: fsdp: 4 (over z), ctx: 2 (over x), tp: 4 (over y, core).
Axes of the slice: x: 2, y: 2, z: 4, core: 2. Of those that a mesh axis runs over, the one named last changes fastest.
Arguments:
- mel_frames: bfloat16 [16, 2048, 80], P('fsdp', 'ctx'), may hold values from -6 to 6
- dec_ids: int32 [16, 512], P('fsdp', 'ctx'), may hold values from 0 to 51871
- targets: int32 [16, 512], P('fsdp', 'ctx'), may hold values from 0 to 51871
- teach_rows: int32 [16, 128], P('fsdp', 'ctx'), may hold values from 0 to 511, as said below
- teach_ids: int32 [16, 128, 64], P('fsdp', 'ctx'), may hold values from 0 to 51871
- teach_probs: float32 [16, 128, 64], P('fsdp', 'ctx'), may hold values from 0.002 to 0.03
- vocab_mask: int32 [51872], P('tp'), may hold values 0 or 1
- projections: float32 [9, 768, 768], P(None, ('fsdp', 'ctx'), 'tp'), may hold values from -0.21875 to 0.21875
- out_proj: float32 [3, 768, 768], P(None, ('fsdp', 'ctx'), 'tp'), may hold values from -0.875 to 0.875
- feed_forward: float32 [4, 768, 3072], P(None, ('fsdp', 'ctx'), 'tp'), may hold values from -0.21875 to 0.21875
- conv_kernels: float32 [2304, 768], P(('fsdp', 'ctx'), 'tp'), may hold values from -0.125 to 0.125
- embed_table: float32 [51872, 768], P('tp', ('fsdp', 'ctx')), may hold values from -0.625 to 0.625
- small_params: float32 [787, 768], replicated, may hold values from -2 to 2
- moment_projections: float32 [9, 768, 768], P(None, ('fsdp', 'ctx'), 'tp'), may hold values from -0.00061035156 to 0.00061035156
- moment_out_proj: float32 [3, 768, 768], P(None, ('fsdp', 'ctx'), 'tp'), may hold values from -0.00061035156 to 0.00061035156
- moment_feed_forward: float32 [4, 768, 3072], P(None, ('fsdp', 'ctx'), 'tp'), may hold values from -0.00061035156 to 0.00061035156
- moment_conv_kernels: float32 [2304, 768], P(('fsdp', 'ctx'), 'tp'), may hold values from -0.00061035156 to 0.00061035156
- moment_embed_table: float32 [51872, 768], P('tp', ('fsdp', 'ctx')), may hold values from -0.00061035156 to 0.00061035156
- moment_small_params: float32 [787, 768], replicated, may hold values from -0.00061035156 to 0.00061035156
- average_projections: float32 [9, 768, 768], P(None, ('fsdp', 'ctx'), 'tp'), may hold values from -0.21875 to 0.21875
- average_out_proj: float32 [3, 768, 768], P(None, ('fsdp', 'ctx'), 'tp'), may hold values from -0.875 to 0.875
- average_feed_forward: float32 [4, 768, 3072], P(None, ('fsdp', 'ctx'), 'tp'), may hold values from -0.21875 to 0.21875
- average_conv_kernels: float32 [2304, 768], P(('fsdp', 'ctx'), 'tp'), may hold values from -0.125 to 0.125
- average_embed_table: float32 [51872, 768], P('tp', ('fsdp', 'ctx')), may hold values from -0.625 to 0.625
- average_small_params: float32 [787, 768], replicated, may hold values from -2 to 2
Outputs:
- loss: float32 [], replicated
- grad_norm: float32 [], replicated
- update_projections: float32 [9, 768, 768], P(None, ('fsdp', 'ctx'), 'tp')
- update_out_proj: float32 [3, 768, 768], P(None, ('fsdp', 'ctx'), 'tp')
- update_feed_forward: float32 [4, 768, 3072], P(None, ('fsdp', 'ctx'), 'tp')
- update_conv_kernels: float32 [2304, 768], P(('fsdp', 'ctx'), 'tp')
- update_embed_table: float32 [51872, 768], P('tp', ('fsdp', 'ctx'))
- update_small_params: float32 [787, 768], replicated
- next_moment_projections: float32 [9, 768, 768], P(None, ('fsdp', 'ctx'), 'tp')
- next_moment_out_proj: float32 [3, 768, 768], P(None, ('fsdp', 'ctx'), 'tp')
- next_moment_feed_forward: float32 [4, 768, 3072], P(None, ('fsdp', 'ctx'), 'tp')
- next_moment_conv_kernels: float32 [2304, 768], P(('fsdp', 'ctx'), 'tp')
- next_moment_embed_table: float32 [51872, 768], P('tp', ('fsdp', 'ctx'))
- next_moment_small_params: float32 [787, 768], replicated
- next_average_projections: float32 [9, 768, 768], P(None, ('fsdp', 'ctx'), 'tp')
- next_average_out_proj: float32 [3, 768, 768], P(None, ('fsdp', 'ctx'), 'tp')
- next_average_feed_forward: float32 [4, 768, 3072], P(None, ('fsdp', 'ctx'), 'tp')
- next_average_conv_kernels: float32 [2304, 768], P(('fsdp', 'ctx'), 'tp')
- next_average_embed_table: float32 [51872, 768], P('tp', ('fsdp', 'ctx'))
- next_average_small_params: float32 [787, 768], replicated
Inputs may be any that keep to these rules, and one draw needn't show every extreme that they name: `teach_rows`: for each clip and each c, the 64 entries of columns c * 64 to (c + 1) * 64 - 1 are distinct positions between c * 256 and (c + 1) * 256 - 1.
All inputs are finite; a program needn't handle non-finite values. No bound on the sum of `vocab_mask` on one device may be relied on, other than what follows from the above.
Results may differ from a plain program's by a relative error of at most 0.0085.
The roundings to bfloat16 on the way count: a program that leaves them out, or rounds other values in their place, can miss the bound.
Values may be sent and summed in bfloat16 or wider, within the bound.
A program may use at most 576 MiB of HBM per device.

v0:
```python
import math

import jax
import jax.numpy as jnp
from jax import lax
from jax.sharding import PartitionSpec as P

D = 768
H = 12
FF = 3072
MEL = 80
KW = 3
DEC = 512
NVEC = 35


EPSILON = 1e-05
CLIP_NORM = 1.0
MOMENTUM = 0.9
LEARN_RATE = 20.0
AVERAGE_RATE = 0.1
NEG_FILL = -1e30


def padded(cells, sides, width):
    for axis, dim in sides:
        count = lax.axis_size(axis)
        ends = count - 1
        head = lax.slice_in_dim(cells, 0, width, axis=dim)
        tail = lax.slice_in_dim(cells, cells.shape[dim] - width, cells.shape[dim], axis=dim)
        cells = jnp.concatenate(
            [
                lax.ppermute(tail, axis, [(i, (i + 1) % count) for i in range(ends)]),
                cells,
                lax.ppermute(head, axis, [((i + 1) % count, i) for i in range(ends)]),
            ],
            axis=dim,
        )
    return cells


def merged(x, axis, combine):
    everything = jax.tree.map(lambda part: lax.all_gather(part, axis), x)
    first = jax.tree.map(lambda part: part[0], everything)

    def step(k, so_far):
        return combine(so_far, jax.tree.map(lambda part: part[k], everything))

    return lax.fori_loop(1, lax.axis_size(axis), step, first)


def to_low(values):
    return values.astype(jnp.bfloat16)


def product(pattern, left, right):
    return jnp.einsum(pattern, left, right, preferred_element_type=jnp.float32)


def layer_norm(values, scale_row, shift_row):
    center = values - jnp.mean(values, axis=-1, keepdims=True)
    spread = jnp.mean(center * center, axis=-1, keepdims=True)
    return center * lax.rsqrt(spread + EPSILON) * scale_row + shift_row


def norm_back(values, scale_row, shift_row, upstream):
    unused_out, pullback = jax.vjp(layer_norm, values, scale_row, shift_row)
    return pullback(upstream)


def gelu_exact(values):
    return jax.nn.gelu(values, approximate=False)


def gelu_back(values, upstream):
    unused_out, pullback = jax.vjp(gelu_exact, values)
    return pullback(upstream)[0]


def sinusoid(start, count, width):
    half_width = width // 2
    increment = math.log(10000.0) / (half_width - 1)
    inverse = jnp.exp(-increment * jnp.arange(half_width, dtype=jnp.int32).astype(jnp.float32))
    moments = (start + jnp.arange(count, dtype=jnp.int32)).astype(jnp.float32)
    angles = moments[:, None] * inverse[None, :]
    return jnp.concatenate([jnp.sin(angles), jnp.cos(angles)], axis=1)


def local_columns(values, width, index):
    return lax.dynamic_slice_in_dim(values, index * width, width, values.ndim - 1)


def place_columns(values, total_width, index):
    full_shape = values.shape[:-1] + (total_width,)
    return lax.dynamic_update_slice_in_dim(
        jnp.zeros(full_shape, jnp.float32), values, index * values.shape[-1], values.ndim - 1
    )


def gather_rows(values):
    return lax.all_gather(values, "tp", axis=1, tiled=True)


def sum_rows(values):
    return lax.psum_scatter(
        values.astype(jnp.bfloat16), "tp", scatter_dimension=1, tiled=True
    ).astype(jnp.float32)


def head_scores(queries, keys_all, causal, query_start, heads_local):
    clip_count, query_count, feature_count = queries.shape
    key_count = keys_all.shape[1]
    head_size = feature_count // heads_local
    query_heads = queries.reshape(clip_count, query_count, heads_local, head_size)
    key_heads = keys_all.reshape(clip_count, key_count, heads_local, head_size)
    scores = product("cqhd,ckhd->chqk", query_heads, key_heads) * head_size ** (-0.5)
    if causal:
        query_place = query_start + jnp.arange(query_count, dtype=jnp.int32)
        allowed = jnp.arange(key_count, dtype=jnp.int32)[None, :] <= query_place[:, None]
        scores = jnp.where(allowed[None, None], scores, NEG_FILL)
    return scores


def attend(queries, keys_local, values_local, causal, query_start, heads_local):
    keys_all, values_all = (
        lax.all_gather(keys_local, "ctx", axis=1, tiled=True),
        lax.all_gather(values_local, "ctx", axis=1, tiled=True),
    )
    scores = head_scores(queries, keys_all, causal, query_start, heads_local)
    row_top = jnp.max(scores, axis=-1, keepdims=True)
    raised = jnp.exp(scores - row_top)
    row_total = jnp.sum(raised, axis=-1, keepdims=True)
    weights_low = to_low(raised / row_total)
    clip_count, key_count, feature_count = values_all.shape
    value_heads = values_all.reshape(
        clip_count, key_count, heads_local, feature_count // heads_local
    )
    mixed = product("chqk,ckhd->cqhd", weights_low, value_heads)
    return (
        to_low(mixed.reshape(queries.shape)),
        row_top + jnp.log(row_total),
        keys_all,
        values_all,
    )


def attend_back(
    queries, keys_all, values_all, log_total, grad_mixed, causal, query_start, heads_local
):
    scores = head_scores(queries, keys_all, causal, query_start, heads_local)
    weights_full = jnp.exp(scores - log_total)
    clip_count, query_count, feature_count = queries.shape
    key_count = keys_all.shape[1]
    head_size = feature_count // heads_local
    query_heads = queries.reshape(clip_count, query_count, heads_local, head_size)
    key_heads = keys_all.reshape(clip_count, key_count, heads_local, head_size)
    value_heads = values_all.reshape(clip_count, key_count, heads_local, head_size)
    grad_heads = grad_mixed.reshape(clip_count, query_count, heads_local, head_size)
    grad_weights = product("cqhd,ckhd->chqk", grad_heads, value_heads)
    inner_sum = jnp.sum(weights_full * grad_weights, axis=-1, keepdims=True)
    grad_scores = to_low(weights_full * (grad_weights - inner_sum))
    factor = head_size ** (-0.5)
    grad_queries = product("chqk,ckhd->cqhd", grad_scores, key_heads) * factor
    grad_keys = product("chqk,cqhd->ckhd", grad_scores, query_heads) * factor
    grad_values = product("chqk,cqhd->ckhd", to_low(weights_full), grad_heads)
    grad_keys, grad_values = (
        lax.psum_scatter(
            grad_keys.reshape(clip_count, key_count, feature_count).astype(jnp.bfloat16),
            "ctx",
            scatter_dimension=1,
            tiled=True,
        ).astype(jnp.float32),
        lax.psum_scatter(
            grad_values.reshape(clip_count, key_count, feature_count).astype(jnp.bfloat16),
            "ctx",
            scatter_dimension=1,
            tiled=True,
        ).astype(jnp.float32),
    )
    return (
        to_low(grad_queries.reshape(clip_count, query_count, feature_count)),
        to_low(grad_keys),
        to_low(grad_values),
    )


def attention_forward(
    normed_q, normed_kv, weight_set, out_weight, bias_q, bias_v, causal, query_start, heads_local
):
    queries = to_low(product("cqd,dh->cqh", normed_q, weight_set[0]) + bias_q)
    keys_local = to_low(product("cqd,dh->cqh", normed_kv, weight_set[1]))
    values_local = to_low(product("cqd,dh->cqh", normed_kv, weight_set[2]) + bias_v)
    mixed, log_total, keys_all, values_all = attend(
        queries, keys_local, values_local, causal, query_start, heads_local
    )
    partial_value = product("cqh,oh->cqo", mixed, out_weight)
    return (sum_rows(partial_value), (queries, mixed, log_total, keys_all, values_all))


def attention_backward(
    normed_q,
    normed_kv,
    weight_set,
    out_weight,
    saved,
    grad_out_low,
    causal,
    query_start,
    heads_local,
):
    queries, mixed, log_total, keys_all, values_all = saved
    grad_full = gather_rows(grad_out_low)
    grad_out_weight = product("cqo,cqh->oh", grad_full, mixed)
    grad_mixed = to_low(product("cqo,oh->cqh", grad_full, out_weight))
    grad_q, grad_k, grad_v = attend_back(
        queries, keys_all, values_all, log_total, grad_mixed, causal, query_start, heads_local
    )
    grad_wq = product("cqd,cqh->dh", normed_q, grad_q)
    grad_wk = product("cqd,cqh->dh", normed_kv, grad_k)
    grad_wv = product("cqd,cqh->dh", normed_kv, grad_v)
    grad_bq = jnp.sum(grad_q, axis=(0, 1), dtype=jnp.float32)
    grad_bv = jnp.sum(grad_v, axis=(0, 1), dtype=jnp.float32)
    back_q = product("cqh,dh->cqd", grad_q, weight_set[0])
    back_kv = product("cqh,dh->cqd", grad_k, weight_set[1]) + product(
        "cqh,dh->cqd", grad_v, weight_set[2]
    )
    return ((grad_wq, grad_wk, grad_wv, grad_out_weight), (grad_bq, grad_bv), back_q, back_kv)


def feed_forward_pass(normed_full, weight_in, bias_in, weight_out):
    hidden = product("cqd,df->cqf", normed_full, weight_in) + bias_in
    active = to_low(gelu_exact(hidden))
    partial_value = product("cqf,of->cqo", active, weight_out)
    return (sum_rows(partial_value), (hidden, active))


def feed_backward(normed_full, weight_in, weight_out, saved, grad_out_low):
    hidden, active = saved
    grad_full = gather_rows(grad_out_low)
    grad_weight_out = product("cqo,cqf->of", grad_full, active)
    grad_active = product("cqo,of->cqf", grad_full, weight_out)
    grad_hidden = to_low(gelu_back(hidden, grad_active))
    grad_weight_in = product("cqd,cqf->df", normed_full, grad_hidden)
    grad_bias_in = jnp.sum(grad_hidden, axis=(0, 1), dtype=jnp.float32)
    back_in = sum_rows(product("cqf,df->cqd", grad_hidden, weight_in))
    return (grad_weight_in, grad_bias_in, grad_weight_out, back_in)


def nesterov(weight, grad, moment, average, factor):
    clipped = grad * factor
    moment_new = MOMENTUM * moment + clipped
    change = -LEARN_RATE * (clipped + MOMENTUM * moment_new)
    average_new = average + AVERAGE_RATE * (weight + change - average)
    return (change, moment_new, average_new)


def local(
    mel_frames,
    dec_ids,
    targets,
    teach_rows,
    teach_ids,
    teach_probs,
    vocab_mask,
    projections,
    out_proj,
    feed_forward,
    conv_kernels,
    embed_table,
    small_params,
    moment_projections,
    moment_out_proj,
    moment_feed_forward,
    moment_conv_kernels,
    moment_embed_table,
    moment_small_params,
    average_projections,
    average_out_proj,
    average_feed_forward,
    average_conv_kernels,
    average_embed_table,
    average_small_params,
):
    tp_count = lax.axis_size("tp")
    tp_index = lax.axis_index("tp")
    ctx_count = lax.axis_size("ctx")
    ctx_index = lax.axis_index("ctx")
    fsdp_count = lax.axis_size("fsdp")
    heads_local = H // tp_count
    width_local = D // tp_count
    hidden_local = FF // tp_count
    vocab_local = embed_table.shape[0]
    clip_count = mel_frames.shape[0]
    frame_count = mel_frames.shape[1]
    enc_rows = frame_count // 2
    enc_share = enc_rows // tp_count
    dec_rows = dec_ids.shape[1]
    dec_share = dec_rows // tp_count
    teach_count = teach_rows.shape[1]
    w_proj, w_out, w_feed, w_conv, w_table = (
        lax.all_gather(to_low(projections), ("fsdp", "ctx"), axis=1, tiled=True),
        lax.all_gather(to_low(out_proj), ("fsdp", "ctx"), axis=1, tiled=True),
        lax.all_gather(to_low(feed_forward), ("fsdp", "ctx"), axis=1, tiled=True),
        lax.all_gather(to_low(conv_kernels), ("fsdp", "ctx"), axis=0, tiled=True),
        lax.all_gather(to_low(embed_table), ("fsdp", "ctx"), axis=1, tiled=True),
    )

    def local_row(row_number):
        return local_columns(small_params[row_number], width_local, tp_index)

    hidden_bias = small_params[27:NVEC].reshape(2, FF)
    enc_bias_in = local_columns(hidden_bias[0], hidden_local, tp_index)
    dec_bias_in = local_columns(hidden_bias[1], hidden_local, tp_index)
    kernel_one = to_low(local_columns(small_params[NVEC : NVEC + KW * MEL], width_local, tp_index))
    mel_rim = padded(mel_frames, (("ctx", 1),), 2)
    taps_one = jnp.concatenate(
        [mel_rim[:, tap_index : tap_index + frame_count + 1] for tap_index in range(KW)], axis=2
    )
    first_pre = product("cfm,mo->cfo", taps_one, kernel_one) + local_row(14)
    frame_place = 2 * ctx_index * enc_rows - 1 + jnp.arange(frame_count + 1, dtype=jnp.int32)
    frame_open = (frame_place >= 0)[None, :, None]
    first_out = to_low(jnp.where(frame_open, gelu_exact(first_pre), 0.0))
    taps_two = jnp.concatenate(
        [first_out[:, tap_index : tap_index + frame_count : 2] for tap_index in range(KW)], axis=2
    )
    second_kernel = (
        w_conv.reshape(KW, D, width_local).transpose(0, 2, 1).reshape(KW * width_local, D)
    )
    second_pre = sum_rows(product("cjx,xo->cjo", taps_two, second_kernel)) + small_params[15]
    enc_start = ctx_index * enc_rows + tp_index * enc_share
    stream_zero = gelu_exact(second_pre) + sinusoid(enc_start, enc_share, D)[None]
    enc_full_one = gather_rows(to_low(layer_norm(stream_zero, small_params[0], small_params[1])))
    enc_attn_part, enc_attn_saved = attention_forward(
        enc_full_one,
        enc_full_one,
        (w_proj[0], w_proj[1], w_proj[2]),
        w_out[0],
        local_row(16),
        local_row(17),
        False,
        0,
        heads_local,
    )
    stream_one = stream_zero + enc_attn_part + small_params[18]
    enc_full_two = gather_rows(to_low(layer_norm(stream_one, small_params[2], small_params[3])))
    enc_feed_part, enc_feed_saved = feed_forward_pass(
        enc_full_two, w_feed[0], enc_bias_in, w_feed[1]
    )
    stream_two = stream_one + enc_feed_part + small_params[19]
    encoded_full = gather_rows(to_low(layer_norm(stream_two, small_params[4], small_params[5])))
    vocab_place = tp_index * vocab_local + jnp.arange(vocab_local, dtype=jnp.int32)
    id_hot = (dec_ids[:, :, None] == vocab_place[None, None, :]).astype(jnp.bfloat16)
    embedded = sum_rows(product("cqv,vd->cqd", id_hot, w_table))
    dec_start = ctx_index * dec_rows + tp_index * dec_share
    tokens_zero = (
        embedded
        + lax.dynamic_slice_in_dim(small_params, NVEC + KW * MEL + dec_start, dec_share, 0)[None]
    )
    dec_full_one = gather_rows(to_low(layer_norm(tokens_zero, small_params[6], small_params[7])))
    self_part, self_saved = attention_forward(
        dec_full_one,
        dec_full_one,
        (w_proj[3], w_proj[4], w_proj[5]),
        w_out[1],
        local_row(20),
        local_row(21),
        True,
        ctx_index * dec_rows,
        heads_local,
    )
    tokens_one = tokens_zero + self_part + small_params[22]
    dec_full_two = gather_rows(to_low(layer_norm(tokens_one, small_params[8], small_params[9])))
    cross_part, cross_saved = attention_forward(
        dec_full_two,
        encoded_full,
        (w_proj[6], w_proj[7], w_proj[8]),
        w_out[2],
        local_row(23),
        local_row(24),
        False,
        0,
        heads_local,
    )
    tokens_two = tokens_one + cross_part + small_params[25]
    dec_full_three = gather_rows(to_low(layer_norm(tokens_two, small_params[10], small_params[11])))
    dec_feed_part, dec_feed_saved = feed_forward_pass(
        dec_full_three, w_feed[2], dec_bias_in, w_feed[3]
    )
    tokens_three = tokens_two + dec_feed_part + small_params[26]
    final_full = gather_rows(to_low(layer_norm(tokens_three, small_params[12], small_params[13])))
    logits = product("cqd,vd->cqv", final_full, w_table)
    mask_open = (vocab_mask > 0)[None, None, :]
    masked = jnp.where(mask_open, logits, NEG_FILL)
    block_top = jnp.max(masked, axis=-1)
    block_total = jnp.sum(jnp.exp(masked - block_top[..., None]), axis=-1)
    target_local = targets - tp_index * vocab_local
    target_inside = jnp.logical_and(target_local >= 0, target_local < vocab_local)
    target_pick = jnp.take_along_axis(
        logits, jnp.clip(target_local, 0, vocab_local - 1)[..., None], axis=2
    )[..., 0]
    target_pick = jnp.where(target_inside, target_pick, 0.0)
    clip_index = jnp.arange(clip_count, dtype=jnp.int32)[:, None]
    teach_local_rows = teach_rows - ctx_index * dec_rows
    teach_rows_logits = logits[clip_index, teach_local_rows]
    teach_local = teach_ids - tp_index * vocab_local
    teach_inside = jnp.logical_and(teach_local >= 0, teach_local < vocab_local)
    teach_clipped = jnp.clip(teach_local, 0, vocab_local - 1)
    teach_pick = jnp.where(
        teach_inside, jnp.take_along_axis(teach_rows_logits, teach_clipped, axis=2), 0.0
    )

    def combine_stats(earlier_stats, later_stats):
        joint_top = jnp.maximum(earlier_stats[0], later_stats[0])
        joint_total = earlier_stats[1] * jnp.exp(earlier_stats[0] - joint_top) + later_stats[
            1
        ] * jnp.exp(later_stats[0] - joint_top)
        return (
            joint_top,
            joint_total,
            earlier_stats[2] + later_stats[2],
            earlier_stats[3] + later_stats[3],
        )

    joint_top, joint_total, target_logit, teach_logit = merged(
        (block_top, block_total, target_pick, teach_pick), "tp", combine_stats
    )
    log_total = joint_top + jnp.log(joint_total)
    token_total = clip_count * fsdp_count * dec_rows * ctx_count
    teach_total = clip_count * fsdp_count * teach_count * ctx_count
    teach_log_total = log_total[clip_index, teach_local_rows]
    cross_sum = jnp.sum(log_total - target_logit)
    teach_sum = jnp.sum(
        teach_probs * (jnp.log(teach_probs) - (teach_logit - teach_log_total[..., None]))
    )
    loss_term = (cross_sum / token_total + teach_sum / teach_total) / tp_count
    probs_open = jnp.where(mask_open, jnp.exp(logits - log_total[..., None]), 0.0)
    row_weight = (
        jnp.zeros((clip_count, dec_rows), jnp.float32)
        .at[clip_index, teach_local_rows]
        .add(jnp.sum(teach_probs, axis=-1) / teach_total)
    )
    grad_logits = probs_open * (1.0 / token_total + row_weight[..., None])
    target_hot = target_local[..., None] == jnp.arange(vocab_local, dtype=jnp.int32)[None, None, :]
    grad_logits = grad_logits - jnp.where(target_hot, 1.0 / token_total, 0.0)
    grad_logits = grad_logits.at[
        clip_index[..., None], teach_local_rows[..., None], teach_clipped
    ].add(jnp.where(teach_inside, -teach_probs / teach_total, 0.0))
    grad_logits_low = to_low(grad_logits)
    grad_table = product("cqv,cqd->vd", grad_logits_low, final_full)
    grad_final = sum_rows(product("cqv,vd->cqd", grad_logits_low, w_table))
    row_grads = {}
    grad_tokens_three, row_grads[12], row_grads[13] = norm_back(
        tokens_three, small_params[12], small_params[13], grad_final
    )
    grad_dec_feed = to_low(grad_tokens_three)
    row_grads[26] = jnp.sum(grad_dec_feed, axis=(0, 1), dtype=jnp.float32)
    dec_feed_grads = feed_backward(
        dec_full_three, w_feed[2], w_feed[3], dec_feed_saved, grad_dec_feed
    )
    back_three, row_grads[10], row_grads[11] = norm_back(
        tokens_two, small_params[10], small_params[11], dec_feed_grads[3]
    )
    grad_tokens_two = grad_tokens_three + back_three
    grad_cross = to_low(grad_tokens_two)
    row_grads[25] = jnp.sum(grad_cross, axis=(0, 1), dtype=jnp.float32)
    cross_weights, cross_biases, cross_back_q, cross_back_kv = attention_backward(
        dec_full_two,
        encoded_full,
        (w_proj[6], w_proj[7], w_proj[8]),
        w_out[2],
        cross_saved,
        grad_cross,
        False,
        0,
        heads_local,
    )
    back_two, row_grads[8], row_grads[9] = norm_back(
        tokens_one, small_params[8], small_params[9], sum_rows(cross_back_q)
    )
    grad_tokens_one = grad_tokens_two + back_two
    back_encoded = sum_rows(cross_back_kv)
    grad_self = to_low(grad_tokens_one)
    row_grads[22] = jnp.sum(grad_self, axis=(0, 1), dtype=jnp.float32)
    self_weights, self_biases, self_back_q, self_back_kv = attention_backward(
        dec_full_one,
        dec_full_one,
        (w_proj[3], w_proj[4], w_proj[5]),
        w_out[1],
        self_saved,
        grad_self,
        True,
        ctx_index * dec_rows,
        heads_local,
    )
    back_one, row_grads[6], row_grads[7] = norm_back(
        tokens_zero, small_params[6], small_params[7], sum_rows(self_back_q + self_back_kv)
    )
    grad_tokens_zero = grad_tokens_one + back_one
    grad_positions = jnp.sum(grad_tokens_zero, axis=0)
    grad_embed_full = gather_rows(to_low(grad_tokens_zero))
    grad_table = grad_table + product("cqv,cqd->vd", id_hot, grad_embed_full)
    grad_stream_two, row_grads[4], row_grads[5] = norm_back(
        stream_two, small_params[4], small_params[5], back_encoded
    )
    grad_enc_feed = to_low(grad_stream_two)
    row_grads[19] = jnp.sum(grad_enc_feed, axis=(0, 1), dtype=jnp.float32)
    enc_feed_grads = feed_backward(
        enc_full_two, w_feed[0], w_feed[1], enc_feed_saved, grad_enc_feed
    )
    back_enc_two, row_grads[2], row_grads[3] = norm_back(
        stream_one, small_params[2], small_params[3], enc_feed_grads[3]
    )
    grad_stream_one = grad_stream_two + back_enc_two
    grad_enc_attn = to_low(grad_stream_one)
    row_grads[18] = jnp.sum(grad_enc_attn, axis=(0, 1), dtype=jnp.float32)
    enc_weights, enc_biases, enc_back_q, enc_back_kv = attention_backward(
        enc_full_one,
        enc_full_one,
        (w_proj[0], w_proj[1], w_proj[2]),
        w_out[0],
        enc_attn_saved,
        grad_enc_attn,
        False,
        0,
        heads_local,
    )
    back_enc_one, row_grads[0], row_grads[1] = norm_back(
        stream_zero, small_params[0], small_params[1], sum_rows(enc_back_q + enc_back_kv)
    )
    grad_stream_zero = grad_stream_one + back_enc_one
    grad_second = to_low(gelu_back(second_pre, grad_stream_zero))
    row_grads[15] = jnp.sum(grad_second, axis=(0, 1), dtype=jnp.float32)
    grad_second_full = gather_rows(grad_second)
    grad_kernel_two = product("cjx,cjo->xo", taps_two, grad_second_full)
    grad_kernel_two = (
        grad_kernel_two.reshape(KW, width_local, D).transpose(0, 2, 1).reshape(KW * D, width_local)
    )
    grad_taps = product("cjo,xo->cjx", grad_second_full, second_kernel).reshape(
        clip_count, enc_rows, KW, width_local
    )
    even_part = jnp.pad(grad_taps[:, :, 0], ((0, 0), (0, 1), (0, 0))) + jnp.pad(
        grad_taps[:, :, 2], ((0, 0), (1, 0), (0, 0))
    )
    odd_part = jnp.pad(grad_taps[:, :, 1], ((0, 0), (0, 1), (0, 0)))
    grad_first = jnp.stack([even_part, odd_part], axis=2).reshape(
        clip_count, frame_count + 2, width_local
    )
    grad_first = grad_first[:, : frame_count + 1]
    grad_first_pre = to_low(jnp.where(frame_open, gelu_back(first_pre, grad_first), 0.0))
    row_grads[14] = place_columns(
        jnp.sum(grad_first_pre, axis=(0, 1), dtype=jnp.float32), D, tp_index
    )
    grad_kernel_one = product("cfm,cfo->mo", taps_one, grad_first_pre)
    row_grads[16] = place_columns(enc_biases[0], D, tp_index)
    row_grads[17] = place_columns(enc_biases[1], D, tp_index)
    row_grads[20] = place_columns(self_biases[0], D, tp_index)
    row_grads[21] = place_columns(self_biases[1], D, tp_index)
    row_grads[23] = place_columns(cross_biases[0], D, tp_index)
    row_grads[24] = place_columns(cross_biases[1], D, tp_index)
    vector_rows = jnp.stack([row_grads[row_number] for row_number in range(27)])
    bias_rows = place_columns(
        jnp.stack([enc_feed_grads[1], dec_feed_grads[1]]), FF, tp_index
    ).reshape(NVEC - 27, D)
    kernel_rows = place_columns(grad_kernel_one, D, tp_index)
    position_rows = lax.dynamic_update_slice_in_dim(
        jnp.zeros((DEC, D), jnp.float32), grad_positions, dec_start, 0
    )
    small_term = jnp.concatenate([vector_rows, bias_rows, kernel_rows, position_rows], axis=0)
    grad_proj = jnp.stack(
        [
            enc_weights[0],
            enc_weights[1],
            enc_weights[2],
            self_weights[0],
            self_weights[1],
            self_weights[2],
            cross_weights[0],
            cross_weights[1],
            cross_weights[2],
        ]
    )
    grad_out = jnp.stack([enc_weights[3], self_weights[3], cross_weights[3]])
    grad_feed = jnp.stack(
        [enc_feed_grads[0], enc_feed_grads[2], dec_feed_grads[0], dec_feed_grads[2]]
    )
    small_grad, loss_value = lax.psum((small_term, loss_term), ("fsdp", "ctx", "tp"))
    group_proj, group_out, group_feed, group_conv, group_table = (
        lax.psum_scatter(
            grad_proj.astype(jnp.bfloat16), "fsdp", scatter_dimension=1, tiled=True
        ).astype(jnp.float32),
        lax.psum_scatter(
            grad_out.astype(jnp.bfloat16), "fsdp", scatter_dimension=1, tiled=True
        ).astype(jnp.float32),
        lax.psum_scatter(
            grad_feed.astype(jnp.bfloat16), "fsdp", scatter_dimension=1, tiled=True
        ).astype(jnp.float32),
        lax.psum_scatter(
            grad_kernel_two.astype(jnp.bfloat16), "fsdp", scatter_dimension=0, tiled=True
        ).astype(jnp.float32),
        lax.psum_scatter(
            grad_table.astype(jnp.bfloat16), "fsdp", scatter_dimension=1, tiled=True
        ).astype(jnp.float32),
    )
    shard_proj, shard_out, shard_feed, shard_conv, shard_table = (
        lax.psum_scatter(
            group_proj.astype(jnp.bfloat16), "ctx", scatter_dimension=1, tiled=True
        ).astype(jnp.float32),
        lax.psum_scatter(
            group_out.astype(jnp.bfloat16), "ctx", scatter_dimension=1, tiled=True
        ).astype(jnp.float32),
        lax.psum_scatter(
            group_feed.astype(jnp.bfloat16), "ctx", scatter_dimension=1, tiled=True
        ).astype(jnp.float32),
        lax.psum_scatter(
            group_conv.astype(jnp.bfloat16), "ctx", scatter_dimension=0, tiled=True
        ).astype(jnp.float32),
        lax.psum_scatter(
            group_table.astype(jnp.bfloat16), "ctx", scatter_dimension=1, tiled=True
        ).astype(jnp.float32),
    )
    local_squares = (
        jnp.sum(shard_proj * shard_proj)
        + jnp.sum(shard_out * shard_out)
        + jnp.sum(shard_feed * shard_feed)
        + jnp.sum(shard_conv * shard_conv)
        + jnp.sum(shard_table * shard_table)
    )
    big_squares = lax.psum(local_squares, ("fsdp", "ctx", "tp"))
    grad_norm = jnp.sqrt(big_squares + jnp.sum(small_grad * small_grad))
    factor = jnp.minimum(1.0, CLIP_NORM / (grad_norm + 1e-06))
    next_proj = nesterov(projections, shard_proj, moment_projections, average_projections, factor)
    next_out = nesterov(out_proj, shard_out, moment_out_proj, average_out_proj, factor)
    next_feed = nesterov(
        feed_forward, shard_feed, moment_feed_forward, average_feed_forward, factor
    )
    next_conv = nesterov(
        conv_kernels, shard_conv, moment_conv_kernels, average_conv_kernels, factor
    )
    next_table = nesterov(embed_table, shard_table, moment_embed_table, average_embed_table, factor)
    next_small = nesterov(
        small_params, small_grad, moment_small_params, average_small_params, factor
    )
    return (
        loss_value,
        grad_norm,
        next_proj[0],
        next_out[0],
        next_feed[0],
        next_conv[0],
        next_table[0],
        next_small[0],
        next_proj[1],
        next_out[1],
        next_feed[1],
        next_conv[1],
        next_table[1],
        next_small[1],
        next_proj[2],
        next_out[2],
        next_feed[2],
        next_conv[2],
        next_table[2],
        next_small[2],
    )


def solution(mesh):
    in_specs = (
        P("fsdp", "ctx", None),
        P("fsdp", "ctx"),
        P("fsdp", "ctx"),
        P("fsdp", "ctx"),
        P("fsdp", "ctx", None),
        P("fsdp", "ctx", None),
        P("tp"),
        P(None, ("fsdp", "ctx"), "tp"),
        P(None, ("fsdp", "ctx"), "tp"),
        P(None, ("fsdp", "ctx"), "tp"),
        P(("fsdp", "ctx"), "tp"),
        P("tp", ("fsdp", "ctx")),
        P(),
        P(None, ("fsdp", "ctx"), "tp"),
        P(None, ("fsdp", "ctx"), "tp"),
        P(None, ("fsdp", "ctx"), "tp"),
        P(("fsdp", "ctx"), "tp"),
        P("tp", ("fsdp", "ctx")),
        P(),
        P(None, ("fsdp", "ctx"), "tp"),
        P(None, ("fsdp", "ctx"), "tp"),
        P(None, ("fsdp", "ctx"), "tp"),
        P(("fsdp", "ctx"), "tp"),
        P("tp", ("fsdp", "ctx")),
        P(),
    )
    out_specs = (
        P(),
        P(),
        P(None, ("fsdp", "ctx"), "tp"),
        P(None, ("fsdp", "ctx"), "tp"),
        P(None, ("fsdp", "ctx"), "tp"),
        P(("fsdp", "ctx"), "tp"),
        P("tp", ("fsdp", "ctx")),
        P(),
        P(None, ("fsdp", "ctx"), "tp"),
        P(None, ("fsdp", "ctx"), "tp"),
        P(None, ("fsdp", "ctx"), "tp"),
        P(("fsdp", "ctx"), "tp"),
        P("tp", ("fsdp", "ctx")),
        P(),
        P(None, ("fsdp", "ctx"), "tp"),
        P(None, ("fsdp", "ctx"), "tp"),
        P(None, ("fsdp", "ctx"), "tp"),
        P(("fsdp", "ctx"), "tp"),
        P("tp", ("fsdp", "ctx")),
        P(),
    )
    return jax.shard_map(local, mesh=mesh, in_specs=in_specs, out_specs=out_specs, check_vma=False)
```

profile of v0, /device:TPU:0, one launch (start us, length us, event | category | flops | bytes accessed | tf_op | source)
XLA Modules:
  0.0 3862.3 jit_solution(8682250978975709237)
XLA Ops:
  20.2 36.6 all_gather.105
  58.2 11.4 select_convert_fusion.1
  69.7 32.7 slice.233
  102.5 32.9 slice.234
  135.4 33.3 slice.235
  179.4 32.7 reduce-scatter.43.cloned.1.call-done
  219.5 56.6 %all-gather.33.cloned.1.call-done = bf16[9,768,192]{2,0,1:T(8,128)(2,1)} async-done(((bf16[9,96,192]{2,0,1:T(8,128)(2,1)}), bf16[9,768,192]{2,0,1:T(8,128)(2,1)}) %all-gather.33.cloned.1.call-update) | async-done | bytes 2654224 | tf_op jit(solution)/shard_map/all_gather | solution.py:301
  276.2 15.4 fusion.282
  310.0 47.6 %all_gather.104 = bf16[3,768,192]{2,0,1:T(4,128)(2,1)S(1)} all-gather(bf16[3,96,192]{2,0,1:T(4,128)(2,1)S(1)} %copy.154), channel_id=1, replica_groups=mesh['fsdp'=4,'ctx'=2,'tp'=4] {'fsdp','ctx'}, dimensions={1}, use_global_device_ids=true | all-gather | bytes 995328 | tf_op jit(solution)/shard_map/all_gather | solution.py:302
  372.0 11.9 multiply_reduce_fusion.1
  415.4 31.8 reduce-scatter.45.cloned.1.call-done
  450.3 383.6 %all-gather.29.cloned.1.call-done = bf16[12968,768]{0,1:T(8,128)(2,1)} async-done(((bf16[12968,96]{0,1:T(8,128)(2,1)}), bf16[12968,768]{0,1:T(8,128)(2,1)}) %all-gather.29.cloned.1.call-update) | async-done | bytes 19918864 | tf_op jit(solution)/shard_map/all_gather | solution.py:305
  833.9 32.3 fusion.77
  868.3 47.5 %all-gather.43.cloned.1.call-done = bf16[4,768,768]{2,1,0:T(8,128)(2,1)} async-done(((bf16[4,96,768]{2,1,0:T(8,128)(2,1)}), bf16[4,768,768]{2,1,0:T(8,128)(2,1)}) %all-gather.43.cloned.1.call-update) | async-done | bytes 4718608 | tf_op jit(solution)/shard_map/all_gather | solution.py:303
  915.9 28.9 all-gather.41.cloned.1.call-done
  958.3 16.6 multiply_convert_fusion.3
  993.8 11.9 all_gather.103
  1031.4 24.4 reduce-scatter.41.cloned.1.call-done
  1061.1 25.6 all-gather.45.cloned.1.call-done
  1110.7 27.2 all-gather.51.cloned.1.call-done
  1148.4 19.0 all-gather.47.cloned.1.call-done
  1175.9 28.3 reduce-scatter.49.cloned.1.call-done
  1206.9 19.7 all-gather.53.cloned.1.call-done
  1243.7 28.3 reduce-scatter.51.cloned.1.call-done
  1277.8 17.1 all-gather.55.cloned.1.call-done
  1294.9 33.3 select_reduce_fusion
  1328.2 52.0 %copy.171 = f32[4,256,12968]{2,1,0:T(8,128)} copy(f32[4,256,12968]{1,2,0:T(8,128)} %get-tuple-element.505) | data formatting | bytes 106233856 | tf_op jit(solution)/shard_map/cqd,vd->cqv/dot_general | solution.py:57
  1380.2 19.6 gather_fusion
  1399.8 577.1 %gather_fusion.3 = f32[16384]{0:T(1024)S(1)} fusion(f32[4,64,12968]{2,1,0:T(8,128)} %bitcast.564, s32[16384]{0:T(1024)S(1)} %reshape.602), kind=kCustom, calls=%fused_computation.3 | custom fusion | bytes 327680 | tf_op jit(solution)/shard_map/jit(take_along_axis)/gather | solution.py:409
  1988.1 36.9 gather_fusion.2
  2030.2 17.4 exponential_reduce_fusion
  2062.2 12.5 scatter_fusion
  2074.7 36.0 select_subtract_fusion
  2110.7 72.6 %copy.227 = f32[6484,2,8,128]{3,1,2,0:T(2,128)} copy(f32[6484,2,8,128]{3,2,1,0:T(8,128)} %bitcast.568) | data formatting | bytes 106233856
  2183.4 121.5 %scatter_fusion.1 = f32[13279232]{0:T(1024)} fusion(f32[13279232]{0:T(1024)} %bitcast.565, s32[16384]{0:T(1024)S(1)} %copy-done.114, f32[16384]{0:T(1024)S(1)} %reshape.616), kind=kCustom, calls=%fused_computation.5 | custom fusion | flops 16384 | bytes 262144
  2304.9 27.1 convert_element_type.614
  2332.0 38.5 reshape.581
  2370.5 27.9 fusion.72
  2398.5 28.8 reduce-scatter.53.cloned.1.call-done
  2434.0 19.8 all-gather.57.cloned.1.call-done
  2465.3 28.3 reduce-scatter.55.cloned.1.call-done
  2501.8 18.8 all-gather.59.cloned.1.call-done
  2522.8 11.5 multiply_reduce_fusion.2
  2551.4 18.7 reduce-scatter.57.cloned.1.call-done
  2574.9 24.1 reduce-scatter.59.cloned.1.call-done
  2604.8 38.1 reduce-scatter.61.cloned.1.call-done
  2658.4 20.1 all-gather.61.cloned.1.call-done
  2696.6 13.0 reduce-scatter.69.cloned.1.call-done
  2717.9 36.3 reduce-scatter.63.cloned.1.call-done
  2795.3 17.8 multiply_reduce_fusion
  2813.2 17.1 multiply_convert_fusion
  2835.4 12.7 fusion.83
  2897.8 23.0 reduce-scatter.85.cloned.1.call-done
  2928.4 36.0 reduce-scatter.79.cloned.1.call-done
  3028.9 29.7 fusion.2
  3064.6 35.7 fusion.4
  3101.2 16.7 reduce-scatter.95.cloned.1.call-done
  3118.0 55.6 %reduce-scatter.91.cloned.1.call-done = bf16[192,1728]{1,0:T(8,128)(2,1)} async-done(((bf16[768,1728]{1,0:T(8,128)(2,1)}), bf16[192,1728]{1,0:T(8,128)(2,1)}) %reduce-scatter.91.cloned.1.call-update) | async-done | bytes 663568
  3173.6 31.8 reduce-scatter.81.cloned.1.call-done
  3205.5 333.6 %reduce-scatter.87.cloned.1.call-done = bf16[12968,192]{0,1:T(8,128)(2,1)} async-done(((bf16[12968,768]{0,1:T(8,128)(2,1)}), bf16[12968,192]{0,1:T(8,128)(2,1)}) %reduce-scatter.87.cloned.1.call-update) | async-done | bytes 4979728 | tf_op jit(solution)/shard_map/reduce_scatter | solution.py:600
  3585.8 12.6 concatenate.35
  3617.5 60.4 %reduce-scatter.89.cloned.1.call-done = bf16[12968,96]{0,1:T(8,128)(2,1)} async-done(((bf16[12968,192]{0,1:T(8,128)(2,1)}), bf16[12968,96]{0,1:T(8,128)(2,1)}) %reduce-scatter.89.cloned.1.call-update) | async-done | bytes 2489872 | tf_op jit(solution)/shard_map/reduce_scatter | solution.py:617
  3682.2 91.0 %all-reduce.6.cloned.1.call-done = f32[787,768]{1,0:T(8,128)} async-done(((f32[787,768]{1,0:T(8,128)}), f32[787,768]{1,0:T(8,128)}) %all-reduce.6.cloned.1.call-update) | async-done | bytes 2417680 | tf_op jit(solution)/shard_map/psum | solution.py:586
  3776.1 39.4 %all-reduce.3 = (f32[]{:T(128)}, f32[]{:T(128)}) all-reduce(f32[]{:T(128)S(6)} %div.210, f32[]{:T(128)S(6)} %add.848), channel_id=1, replica_groups=mesh['fsdp'=4,'ctx'=2,'tp'=4] {'fsdp','ctx','tp'}, use_global_device_ids=true, to_apply=%region_33.34 | all-reduce | flops 2 | bytes 16 | tf_op jit(solution)/shard_map/psum | solution.py:586
  (1053 shorter events, 638.6 us)
Async XLA Ops:
  8.0 204.1 %reduce-scatter.43.cloned.1.call-start = ((), (), s32[]{:S(2)}) async-start(), calls=%async_computation.35 | async-start | bytes 3932160 | tf_op jit(solution)/shard_map/reduce_scatter | solution.py:105
  9.7 48.2 %collective-permute-start = (bf16[4,2,80]{2,1,0:T(2,128)(2,1)S(1)}, bf16[4,2,80]{2,1,0:T(2,128)(2,1)S(1)}, u32[]{:S(2)}, u32[]{:S(2)}) collective-permute-start(bf16[4,2,80]{2,1,0:T(2,128)(2,1)S(1)} %get-tuple-element.488), channel_id=1, source_target_pairs={{0,4},{1,5},{2,6},{3,7},{8,12},{9,13},{10,14},{11,15},{16,20},{17,... | collective-permute-start | bytes 3848 | tf_op jit(solution)/shard_map/ppermute | solution.py:33
  14.5 43.7 %collective-permute-start.1 = (bf16[4,2,80]{2,1,0:T(2,128)(2,1)S(1)}, bf16[4,2,80]{2,1,0:T(2,128)(2,1)S(1)}, u32[]{:S(2)}, u32[]{:S(2)}) collective-permute-start(bf16[4,2,80]{2,1,0:T(2,128)(2,1)S(1)} %get-tuple-element.489), channel_id=1, source_target_pairs={{4,0},{5,1},{6,2},{7,3},{12,8},{13,9},{14,10},{15,11},{20,16},{21,... | collective-permute-start | bytes 3848 | tf_op jit(solution)/shard_map/ppermute | solution.py:35
  174.1 102.0 %all-gather.33.cloned.1.call-start = ((), (), s32[]{:S(2)}) async-start(), calls=%async_computation.33 | async-start | bytes 7077888 | tf_op jit(solution)/shard_map/all_gather | solution.py:301
  176.5 128.3 %all-gather.35.cloned.1.call-start = ((), (), s32[]{:S(2)}) async-start(), calls=%async_computation.36 | async-start | bytes 3932160 | tf_op jit(solution)/shard_map/all_gather | solution.py:101
  179.4 776.9 %copy-start.137 = (f32[768]{0:T(1024)}, f32[768]{0:T(1024)S(1)}, u32[]{:S(2)}) copy-start(f32[768]{0:T(1024)S(1)} %get-tuple-element.349) | copy-start | bytes 9220
  219.4 152.5 %all-gather.39.cloned.1.call-start = ((), (), s32[]{:S(2)}) async-start(), calls=%async_computation.38 | async-start | bytes 2359296 | tf_op jit(solution)/shard_map/all_gather | solution.py:126
  308.8 86.1 %all-gather.37.cloned.1.call-start = ((), (), s32[]{:S(2)}) async-start(), calls=%async_computation.37 | async-start | bytes 2359296 | tf_op jit(solution)/shard_map/all_gather | solution.py:127
  368.4 78.8 %reduce-scatter.45.cloned.1.call-start = ((), (), s32[]{:S(2)}) async-start(), calls=%async_computation.39 | async-start | bytes 3932160 | tf_op jit(solution)/shard_map/reduce_scatter | solution.py:105
  410.0 423.8 %all-gather.29.cloned.1.call-start = ((), (), s32[]{:S(2)}) async-start(), calls=%async_computation.30 | async-start | bytes 22560768 | tf_op jit(solution)/shard_map/all_gather | solution.py:305
  414.3 501.5 %all-gather.43.cloned.1.call-start = ((), (), s32[]{:S(2)}) async-start(), calls=%async_computation.41 | async-start | bytes 5308416 | tf_op jit(solution)/shard_map/all_gather | solution.py:303
  415.3 529.4 %all-gather.41.cloned.1.call-start = ((), (), s32[]{:S(2)}) async-start(), calls=%async_computation.40 | async-start | bytes 3932160 | tf_op jit(solution)/shard_map/all_gather | solution.py:101
  448.6 578.9 %copy-start.5 = (f32[4,128,768]{2,1,0:T(8,128)}, f32[4,128,768]{2,1,0:T(8,128)S(1)}, u32[]{:S(2)}) copy-start(f32[4,128,768]{2,1,0:T(8,128)S(1)} %get-tuple-element.455) | copy-start | bytes 4718596
  450.2 503.7 %reduce-scatter.39.cloned.1.call-start = ((), (), s32[]{:S(2)}) async-start(), calls=%async_computation.31 | async-start | bytes 1966080 | tf_op jit(solution)/shard_map/reduce_scatter | solution.py:105
  866.2 125.2 %all-gather.31.cloned.1.call-start = ((), (), s32[]{:S(2)}) async-start(), calls=%async_computation.32 | async-start | bytes 1966080 | tf_op jit(solution)/shard_map/all_gather | solution.py:101
  958.3 69.2 %reduce-scatter.47.cloned.1.call-start = ((), (), s32[]{:S(2)}) async-start(), calls=%async_computation.42 | async-start | bytes 3932160 | tf_op jit(solution)/shard_map/reduce_scatter | solution.py:105
  981.9 73.9 %reduce-scatter.41.cloned.1.call-start = ((), (), s32[]{:S(2)}) async-start(), calls=%async_computation.34 | async-start | bytes 1966080 | tf_op jit(solution)/shard_map/reduce_scatter | solution.py:105
  1027.4 59.2 %all-gather.45.cloned.1.call-start = ((), (), s32[]{:S(2)}) async-start(), calls=%async_computation.43 | async-start | bytes 3932160 | tf_op jit(solution)/shard_map/all_gather | solution.py:101
  1031.3 77.3 %all-gather.49.cloned.1.call-start = ((), (), s32[]{:S(2)}) async-start(), calls=%async_computation.45 | async-start | bytes 1966080 | tf_op jit(solution)/shard_map/all_gather | solution.py:101
  1060.4 77.4 %all-gather.51.cloned.1.call-start = ((), (), s32[]{:S(2)}) async-start(), calls=%async_computation.46 | async-start | bytes 2359296 | tf_op jit(solution)/shard_map/all_gather | solution.py:126
  1090.6 76.7 %all-gather.47.cloned.1.call-start = ((), (), s32[]{:S(2)}) async-start(), calls=%async_computation.44 | async-start | bytes 2359296 | tf_op jit(solution)/shard_map/all_gather | solution.py:127
  1097.9 106.3 %reduce-scatter.49.cloned.1.call-start = ((), (), s32[]{:S(2)}) async-start(), calls=%async_computation.47 | async-start | bytes 1966080 | tf_op jit(solution)/shard_map/reduce_scatter | solution.py:105
  1175.8 50.7 %all-gather.53.cloned.1.call-start = ((), (), s32[]{:S(2)}) async-start(), calls=%async_computation.48 | async-start | bytes 1966080 | tf_op jit(solution)/shard_map/all_gather | solution.py:101
  1206.8 65.2 %reduce-scatter.51.cloned.1.call-start = ((), (), s32[]{:S(2)}) async-start(), calls=%async_computation.49 | async-start | bytes 1966080 | tf_op jit(solution)/shard_map/reduce_scatter | solution.py:105
  1243.7 51.2 %all-gather.55.cloned.1.call-start = ((), (), s32[]{:S(2)}) async-start(), calls=%async_computation.50 | async-start | bytes 1966080 | tf_op jit(solution)/shard_map/all_gather | solution.py:101
  1275.1 1152.2 %reduce-scatter.53.cloned.1.call-start = ((), (), s32[]{:S(2)}) async-start(), calls=%async_computation.51 | async-start | bytes 1966080 | tf_op jit(solution)/shard_map/reduce_scatter | solution.py:105
  1399.8 577.2 %copy-start.117 = (f32[4,64,64]{2,1,0:T(8,128)S(1)}, f32[4,64,64]{2,1,0:T(8,128)}, u32[]{:S(2)}) copy-start(f32[4,64,64]{2,1,0:T(8,128)} %param.32) | copy-start | bytes 196612
  2398.4 55.3 %all-gather.57.cloned.1.call-start = ((), (), s32[]{:S(2)}) async-start(), calls=%async_computation.52 | async-start | bytes 1966080 | tf_op jit(solution)/shard_map/all_gather | solution.py:101
  2433.9 59.7 %reduce-scatter.55.cloned.1.call-start = ((), (), s32[]{:S(2)}) async-start(), calls=%async_computation.53 | async-start | bytes 1966080 | tf_op jit(solution)/shard_map/reduce_scatter | solution.py:105
  2465.3 55.3 %all-gather.59.cloned.1.call-start = ((), (), s32[]{:S(2)}) async-start(), calls=%async_computation.54 | async-start | bytes 1966080 | tf_op jit(solution)/shard_map/all_gather | solution.py:101
  2500.8 69.2 %reduce-scatter.57.cloned.1.call-start = ((), (), s32[]{:S(2)}) async-start(), calls=%async_computation.55 | async-start | bytes 2359296 | tf_op jit(solution)/shard_map/reduce_scatter | solution.py:167
  2543.8 55.1 %reduce-scatter.59.cloned.1.call-start = ((), (), s32[]{:S(2)}) async-start(), calls=%async_computation.56 | async-start | bytes 2359296 | tf_op jit(solution)/shard_map/reduce_scatter | solution.py:173
  2551.4 91.5 %reduce-scatter.61.cloned.1.call-start = ((), (), s32[]{:S(2)}) async-start(), calls=%async_computation.57 | async-start | bytes 3932160 | tf_op jit(solution)/shard_map/reduce_scatter | solution.py:105
  2604.8 73.8 %all-gather.61.cloned.1.call-start = ((), (), s32[]{:S(2)}) async-start(), calls=%async_computation.58 | async-start | bytes 3932160 | tf_op jit(solution)/shard_map/all_gather | solution.py:101
  2650.0 59.6 %reduce-scatter.69.cloned.1.call-start = ((), (), s32[]{:S(2)}) async-start(), calls=%async_computation.63 | async-start | bytes 1966080 | tf_op jit(solution)/shard_map/reduce_scatter | solution.py:105
  2658.1 96.0 %reduce-scatter.63.cloned.1.call-start = ((), (), s32[]{:S(2)}) async-start(), calls=%async_computation.59 | async-start | bytes 3932160 | tf_op jit(solution)/shard_map/reduce_scatter | solution.py:105
  2696.6 67.0 %all-gather.65.cloned.1.call-start = ((), (), s32[]{:S(2)}) async-start(), calls=%async_computation.64 | async-start | bytes 1966080 | tf_op jit(solution)/shard_map/all_gather | solution.py:101
  2717.8 73.6 %all-gather.63.cloned.1.call-start = ((), (), s32[]{:S(2)}) async-start(), calls=%async_computation.60 | async-start | bytes 3932160 | tf_op jit(solution)/shard_map/all_gather | solution.py:101
  2762.7 90.0 %reduce-scatter.71.cloned.1.call-start = ((), (), s32[]{:S(2)}) async-start(), calls=%async_computation.65 | async-start | bytes 1179648 | tf_op jit(solution)/shard_map/reduce_scatter | solution.py:167
  2774.8 81.3 %reduce-scatter.73.cloned.1.call-start = ((), (), s32[]{:S(2)}) async-start(), calls=%async_computation.66 | async-start | bytes 1179648 | tf_op jit(solution)/shard_map/reduce_scatter | solution.py:173
  2781.6 92.8 %reduce-scatter.65.cloned.1.call-start = ((), (), s32[]{:S(2)}) async-start(), calls=%async_computation.61 | async-start | bytes 2359296 | tf_op jit(solution)/shard_map/reduce_scatter | solution.py:167
  2835.4 54.7 %reduce-scatter.67.cloned.1.call-start = ((), (), s32[]{:S(2)}) async-start(), calls=%async_computation.62 | async-start | bytes 2359296 | tf_op jit(solution)/shard_map/reduce_scatter | solution.py:173
  2848.1 72.7 %reduce-scatter.85.cloned.1.call-start = ((), (), s32[]{:S(2)}) async-start(), calls=%async_computation.73 | async-start | bytes 1966080 | tf_op jit(solution)/shard_map/reduce_scatter | solution.py:105
  2860.1 104.4 %reduce-scatter.79.cloned.1.call-start = ((), (), s32[]{:S(2)}) async-start(), calls=%async_computation.69 | async-start | bytes 3932160 | tf_op jit(solution)/shard_map/reduce_scatter | solution.py:105
  2897.8 131.1 %all-gather.69.cloned.1.call-start = ((), (), s32[]{:S(2)}) async-start(), calls=%async_computation.74 | async-start | bytes 1966080 | tf_op jit(solution)/shard_map/all_gather | solution.py:101
  2928.2 130.3 %all-gather.67.cloned.1.call-start = ((), (), s32[]{:S(2)}) async-start(), calls=%async_computation.70 | async-start | bytes 3932160 | tf_op jit(solution)/shard_map/all_gather | solution.py:101
  2971.8 128.6 %reduce-scatter.75.cloned.1.call-start = ((), (), s32[]{:S(2)}) async-start(), calls=%async_computation.67 | async-start | bytes 5898240 | tf_op jit(solution)/shard_map/reduce_scatter | solution.py:594
  2987.2 130.6 %reduce-scatter.95.cloned.1.call-start = ((), (), s32[]{:S(2)}) async-start(), calls=%async_computation.80 | async-start | bytes 1228800
  2995.2 178.3 %reduce-scatter.91.cloned.1.call-start = ((), (), s32[]{:S(2)}) async-start(), calls=%async_computation.78 | async-start | bytes 3440640
  3028.6 176.9 %reduce-scatter.81.cloned.1.call-start = ((), (), s32[]{:S(2)}) async-start(), calls=%async_computation.71 | async-start | bytes 1474560 | tf_op jit(solution)/shard_map/reduce_scatter | solution.py:597
  3064.6 474.6 %reduce-scatter.87.cloned.1.call-start = ((), (), s32[]{:S(2)}) async-start(), calls=%async_computation.75 | async-start | bytes 25067520 | tf_op jit(solution)/shard_map/reduce_scatter | solution.py:600
  3100.3 506.1 %reduce-scatter.77.cloned.1.call-start = ((), (), s32[]{:S(2)}) async-start(), calls=%async_computation.68 | async-start | bytes 1769472 | tf_op jit(solution)/shard_map/reduce_scatter | solution.py:611
  3101.1 438.5 %copy-start.212 = (f32[768]{0:T(1024)S(1)}, f32[768]{0:T(1024)}, u32[]{:S(2)}) copy-start(f32[768]{0:T(1024)} %get-tuple-element.420) | copy-start | bytes 9220
  3101.1 438.5 %copy-start.211 = (f32[768]{0:T(1024)S(1)}, f32[768]{0:T(1024)}, u32[]{:S(2)}) copy-start(f32[768]{0:T(1024)} %get-tuple-element.358) | copy-start | bytes 9220
  3101.1 438.5 %copy-start.210 = (f32[768]{0:T(1024)S(1)}, f32[768]{0:T(1024)}, u32[]{:S(2)}) copy-start(f32[768]{0:T(1024)} %get-tuple-element.370) | copy-start | bytes 9220
  3101.1 507.3 %reduce-scatter.97.cloned.1.call-start = ((), (), s32[]{:S(2)}) async-start(), calls=%async_computation.81 | async-start | bytes 368640
  3117.9 424.2 %copy-start.260 = (f32[3,64]{1,0:T(4,128)S(1)}, f32[3,64]{1,0:T(4,128)}, u32[]{:S(2)}) copy-start(f32[3,64]{1,0:T(4,128)} %get-tuple-element.516) | copy-start | bytes 2308
  3117.9 424.4 %copy-start.223 = (f32[768]{0:T(1024)S(1)}, f32[768]{0:T(1024)}, u32[]{:S(2)}) copy-start(f32[768]{0:T(1024)} %get-tuple-element.425) | copy-start | bytes 9220
  3117.9 424.9 %copy-start.222 = (f32[768]{0:T(1024)S(1)}, f32[768]{0:T(1024)}, u32[]{:S(2)}) copy-start(f32[768]{0:T(1024)} %get-tuple-element.356) | copy-start | bytes 9220
  3117.9 425.5 %copy-start.221 = (f32[768]{0:T(1024)S(1)}, f32[768]{0:T(1024)}, u32[]{:S(2)}) copy-start(f32[768]{0:T(1024)} %get-tuple-element.374) | copy-start | bytes 9220
  3117.9 492.4 %reduce-scatter.93.cloned.1.call-start = ((), (), s32[]{:S(2)}) async-start(), calls=%async_computation.79 | async-start | bytes 1032192
  3173.6 441.6 %reduce-scatter.83.cloned.1.call-start = ((), (), s32[]{:S(2)}) async-start(), calls=%async_computation.72 | async-start | bytes 442368 | tf_op jit(solution)/shard_map/reduce_scatter | solution.py:614
  3205.5 472.4 %reduce-scatter.89.cloned.1.call-start = ((), (), s32[]{:S(2)}) async-start(), calls=%async_computation.76 | async-start | bytes 7520256 | tf_op jit(solution)/shard_map/reduce_scatter | solution.py:617
  3539.3 233.8 %all-reduce.6.cloned.1.call-start = ((), (), s32[]{:S(2)}) async-start(), calls=%async_computation.77 | async-start | bytes 4866048 | tf_op jit(solution)/shard_map/psum | solution.py:586
  (285 other events, 9010.9 us)
Sparse Core Ops, SparseCore 0:
  174.2 37.7 reduce-scatter.42
  308.9 52.3 all-gather.38
  368.5 25.5 all-gather.36
  866.3 28.1 reduce-scatter.38
  958.4 19.6 all-gather.30
  982.0 37.9 reduce-scatter.46
  1027.5 28.2 reduce-scatter.40
  1058.0 28.5 all-gather.44
  1088.8 19.7 all-gather.48
  1110.6 27.1 all-gather.50
  1140.1 27.2 all-gather.46
  1176.0 28.1 reduce-scatter.48
  1206.9 19.6 all-gather.52
  1243.8 28.1 reduce-scatter.50
  1275.2 19.6 all-gather.54
  2398.5 28.7 reduce-scatter.52
  2434.0 19.6 all-gather.56
  2465.4 28.1 reduce-scatter.54
  2500.9 19.6 all-gather.58
  2543.9 26.0 reduce-scatter.56
  2572.9 26.0 reduce-scatter.58
  2604.9 37.9 reduce-scatter.60
  2717.9 19.8 all-gather.64
  2762.8 28.5 all-gather.62
  2794.2 17.4 reduce-scatter.70
  2813.8 17.4 reduce-scatter.72
  2835.5 26.0 reduce-scatter.64
  2863.9 26.1 reduce-scatter.66
  2892.6 28.1 reduce-scatter.84
  2923.9 40.4 reduce-scatter.78
  3598.6 174.4 all-reduce.5
Sparse Core Ops, SparseCore 1:
  177.6 98.5 all-gather.32
  278.2 26.5 all-gather.34
  410.1 37.0 reduce-scatter.44
  449.3 384.5 all-gather.28
  836.3 79.5 all-gather.42
  918.1 26.6 all-gather.40
  2650.1 28.4 all-gather.60
  2681.5 28.1 reduce-scatter.68
  2712.8 41.3 reduce-scatter.62
  2928.3 19.8 all-gather.68
  2971.9 28.4 all-gather.66
  3003.2 85.1 reduce-scatter.74
  3091.2 26.6 reduce-scatter.94
  3120.9 52.6 reduce-scatter.90
  3176.6 28.8 reduce-scatter.80
  3208.0 331.2 reduce-scatter.86
  3541.5 22.8 reduce-scatter.76
  3566.6 11.4 reduce-scatter.96
  3580.2 16.2 reduce-scatter.92
  3598.7 13.0 reduce-scatter.82
  3614.0 63.8 reduce-scatter.88
where the time goes:
time: 3880 us; the launch traced here: 3860 us
  waiting for transfers between devices  1710 us (44%)
  local copies, waits for them, and re-layouts  1060 us (27%)
  matrix products  461 us (12%)
  other arithmetic  417 us (11%)
  blocking collectives  174 us (4%)
    gather x3, local copies, waits for them, and re-layouts, local(): jnp.take_along_axis(teach_rows_logits, teach_clipped, axis=2)  577 us
    dot_general x76, matrix products, product(): return jnp.einsum(pattern, left, right, preferred_element_type=jnp.float32)  461 us
    all_gather x1, waiting for transfers between devices, local(): lax.all_gather(to_low(embed_table), ('fsdp', 'ctx'), axis=1, tiled=True)  384 us
    reduce_scatter x14, waiting for transfers between devices, sum_rows(): lax.psum_scatter(values.astype(jnp.bfloat16), 'tp', scatter_dimension=1,...  349 us
    reduce_scatter x1, waiting for transfers between devices, local(): lax.psum_scatter(grad_table.astype(jnp.bfloat16), 'fsdp', scatter_dimensi...  334 us
    all_gather x14, waiting for transfers between devices, gather_rows(): return lax.all_gather(values, 'tp', axis=1, tiled=True)  181 us
    unnamed x630, local copies, waits for them, and re-layouts  165 us
    unnamed x9, other arithmetic  122 us
  transfers between devices with their start and end apart: 54, of which 36 were waited for; matrix products, arithmetic and copies ran while one was open for 15% of the time, Pallas kernels for 0%

commit v1 on v0

v1 whole, which is shorter than its diff:
```python
import functools
import math

import jax
import jax.numpy as jnp
from jax import lax
from jax.experimental import pallas as pl
from jax.experimental.pallas import tpu as pltpu
from jax.sharding import PartitionSpec as P

D = 768
H = 12
HD = 64
FF = 3072
MEL = 80
KW = 3
NVEC = 35
EPSILON = 1e-05
CLIP_NORM = 1.0
MOMENTUM = 0.9
LEARN_RATE = 20.0
AVERAGE_RATE = 0.1
NEG_FILL = -1e30
CHUNK = 512
LANES = 128
VMEM_LIMIT = 56 * 1024 * 1024
PLANE = ("ctx", "tp")
ALL = ("fsdp", "ctx", "tp")


def to_low(values):
    return values.astype(jnp.bfloat16)


def product(pattern, left, right):
    return jnp.einsum(pattern, left, right, preferred_element_type=jnp.float32)


def layer_norm(values, scale_row, shift_row):
    center = values - jnp.mean(values, axis=-1, keepdims=True)
    spread = jnp.mean(center * center, axis=-1, keepdims=True)
    return center * lax.rsqrt(spread + EPSILON) * scale_row + shift_row


def norm_back(values, scale_row, shift_row, upstream):
    unused_out, pullback = jax.vjp(layer_norm, values, scale_row, shift_row)
    return pullback(upstream)


def gelu_exact(values):
    return jax.nn.gelu(values, approximate=False)


def gelu_back(values, upstream):
    unused_out, pullback = jax.vjp(gelu_exact, values)
    return pullback(upstream)[0]


def sinusoid(start, count, width):
    half_width = width // 2
    increment = math.log(10000.0) / (half_width - 1)
    inverse = jnp.exp(-increment * jnp.arange(half_width, dtype=jnp.int32).astype(jnp.float32))
    moments = (start + jnp.arange(count, dtype=jnp.int32)).astype(jnp.float32)
    angles = moments[:, None] * inverse[None, :]
    return jnp.concatenate([jnp.sin(angles), jnp.cos(angles)], axis=1)


def pick(values, index):
    return lax.dynamic_index_in_dim(values, index, 0, keepdims=False)


def place(values, part, index):
    return lax.dynamic_update_index_in_dim(values, part, index, 0)


def shifted(axis, step):
    count = lax.axis_size(axis)
    return [(i, (i + step) % count) for i in range(count)]


def in_order(arrived, axis):
    count = len(arrived)
    index = lax.axis_index(axis)
    if count == 2:
        return jnp.where(index == 0, jnp.stack(arrived), jnp.stack(arrived[::-1]))
    out = jnp.zeros((count,) + arrived[0].shape, arrived[0].dtype)
    for step, piece in enumerate(arrived):
        out = place(out, piece, lax.rem(index - step + count, count))
    return out


def sent_to_all(values, axis):
    count = lax.axis_size(axis)
    return [values] + [
        lax.ppermute(values, axis, shifted(axis, step)) for step in range(1, count)
    ]


def spread(values, axis):
    return in_order(sent_to_all(values, axis), axis)


def sent_to_owners(pieces_for, axis):
    count = lax.axis_size(axis)
    return [pieces_for(0)] + [
        lax.ppermute(pieces_for(step), axis, shifted(axis, step)) for step in range(1, count)
    ]


def wide_sum(pieces):
    total = pieces[0].astype(jnp.float32)
    for piece in pieces[1:]:
        total = total + piece.astype(jnp.float32)
    return total


def sum_to_owner(values, axis):
    count = lax.axis_size(axis)
    index = lax.axis_index(axis)
    return wide_sum(
        sent_to_owners(lambda step: pick(values, lax.rem(index + step, count)), axis)
    )


def together(*values):
    return lax.optimization_barrier(values)


def exchanged_sum(values, axes):
    for axis in axes:
        count = lax.axis_size(axis)
        bit = 1
        while bit < count:
            values = values + lax.ppermute(values, axis, [(i, i ^ bit) for i in range(count)])
            bit *= 2
    return values


def head_scores(queries, keys, key_place, query_place):
    scores = product("qhd,khd->hqk", queries, keys) * HD ** (-0.5)
    if key_place is not None:
        allowed = key_place[None, :] <= query_place[:, None]
        scores = jnp.where(allowed[None], scores, NEG_FILL)
    return scores


def split_heads(values):
    return values.reshape(values.shape[0], H, HD)


def attention_forward(rows_q, rows_k, weights, biases, key_place, query_place):
    queries = split_heads(to_low(product("qd,dh->qh", rows_q, weights[0]) + biases[0]))
    keys = split_heads(to_low(product("qd,dh->qh", rows_k, weights[1])))
    values = split_heads(to_low(product("qd,dh->qh", rows_k, weights[2]) + biases[1]))
    scores = head_scores(queries, keys, key_place, query_place)
    top = jnp.max(scores, axis=-1, keepdims=True)
    raised = jnp.exp(scores - top)
    total = jnp.sum(raised, axis=-1, keepdims=True)
    mixed = product("hqk,khd->qhd", to_low(raised / total), values)
    mixed = to_low(mixed.reshape(rows_q.shape))
    out = product("qh,oh->qo", mixed, weights[3]) + biases[2]
    return out, (queries, keys, values, mixed, top + jnp.log(total))


def attention_backward(rows_q, rows_k, weights, saved, grad_out, key_place, query_place):
    queries, keys, values, mixed, log_total = saved
    grad_out_weight = product("qo,qh->oh", grad_out, mixed)
    grad_mixed = split_heads(to_low(product("qo,oh->qh", grad_out, weights[3])))
    scores = head_scores(queries, keys, key_place, query_place)
    probs = jnp.exp(scores - log_total)
    grad_probs = product("qhd,khd->hqk", grad_mixed, values)
    inner = jnp.sum(probs * grad_probs, axis=-1, keepdims=True)
    grad_scores = to_low(probs * (grad_probs - inner))
    factor = HD ** (-0.5)
    grad_q = to_low(product("hqk,khd->qhd", grad_scores, keys) * factor).reshape(rows_q.shape)
    grad_k = to_low(product("hqk,qhd->khd", grad_scores, queries) * factor).reshape(rows_k.shape)
    grad_v = to_low(product("hqk,qhd->khd", to_low(probs), grad_mixed)).reshape(rows_k.shape)
    grad_weights = (
        product("qd,qh->dh", rows_q, grad_q),
        product("qd,qh->dh", rows_k, grad_k),
        product("qd,qh->dh", rows_k, grad_v),
        grad_out_weight,
    )
    bias_q = jnp.sum(grad_q, axis=0, dtype=jnp.float32)
    bias_v = jnp.sum(grad_v, axis=0, dtype=jnp.float32)
    back_q = product("qh,dh->qd", grad_q, weights[0])
    back_k = product("qh,dh->qd", grad_k, weights[1]) + product("qh,dh->qd", grad_v, weights[2])
    return grad_weights, bias_q, bias_v, back_q, back_k


def feed_forward_pass(rows, weight_in, bias_in, weight_out, bias_out):
    hidden = product("qd,df->qf", rows, weight_in) + bias_in
    active = to_low(gelu_exact(hidden))
    return product("qf,of->qo", active, weight_out) + bias_out, (hidden, active)


def feed_backward(rows, weight_in, weight_out, saved, grad_out):
    hidden, active = saved
    grad_weight_out = product("qo,qf->of", grad_out, active)
    grad_active = product("qo,of->qf", grad_out, weight_out)
    grad_hidden = to_low(gelu_back(hidden, grad_active))
    grad_weight_in = product("qd,qf->df", rows, grad_hidden)
    grad_bias_in = jnp.sum(grad_hidden, axis=0, dtype=jnp.float32)
    back = product("qf,df->qd", grad_hidden, weight_in)
    return grad_weight_in, grad_weight_out, grad_bias_in, back


def nesterov(weight, grad, moment, average, factor):
    clipped = grad * factor
    moment_new = MOMENTUM * moment + clipped
    change = -LEARN_RATE * (clipped + MOMENTUM * moment_new)
    average_new = average + AVERAGE_RATE * (weight + change - average)
    return (change, moment_new, average_new)


def stats_kernel(
    blocks, rows, teach, final_ref, bias_ref, target_ref, weight_ref, table_ref,
    top_ref, total_ref, pick_ref, dot_ref,
):
    chunk = table_ref.shape[1]
    tiles = chunk // LANES

    @pl.when(pl.program_id(0) == 0)
    def _():
        top_ref[...] = jnp.full(top_ref.shape, 2.0 * NEG_FILL, jnp.float32)
        total_ref[...] = jnp.zeros(total_ref.shape, jnp.float32)
        pick_ref[...] = jnp.zeros(pick_ref.shape, jnp.float32)
        dot_ref[...] = jnp.zeros(dot_ref.shape, jnp.float32)

    start = pl.program_id(0) * chunk
    for block in range(blocks):
        span = pl.ds(block * rows, rows)
        logits = jnp.dot(final_ref[span, :], table_ref[...], preferred_element_type=jnp.float32)
        target = target_ref[span, :] - start
        top_old = top_ref[span, :]
        masked = []
        picked = pick_ref[span, :]
        top_new = top_old
        dots = dot_ref[...]
        for tile in range(tiles):
            lanes = slice(tile * LANES, (tile + 1) * LANES)
            piece = logits[:, lanes]
            column = lax.broadcasted_iota(jnp.int32, (rows, LANES), 1) + tile * LANES
            picked = picked + jnp.where(column == target, piece, 0.0)
            dots = dots + piece[:teach] * weight_ref[
                tile, pl.ds(block * teach, teach), :
            ].astype(jnp.float32)
            piece = piece + bias_ref[:, lanes]
            masked.append(piece)
            top_new = jnp.maximum(top_new, piece)
        total = total_ref[span, :] * jnp.exp(top_old - top_new)
        for piece in masked:
            total = total + jnp.exp(piece - top_new)
        top_ref[span, :] = top_new
        total_ref[span, :] = total
        pick_ref[span, :] = picked
        dot_ref[...] = dots


def loss_stats(final_all, table, bias_row, targets, weights, blocks):
    count = final_all.shape[0]
    width = table.shape[1]
    rows = count // blocks
    teach = weights.shape[1] // blocks
    whole = lambda j: (0, 0)
    by_chunk = lambda j: (0, j)
    row_stat = jax.ShapeDtypeStruct((count, LANES), jnp.float32)
    return pl.pallas_call(
        functools.partial(stats_kernel, blocks, rows, teach),
        grid=(width // CHUNK,),
        in_specs=[
            pl.BlockSpec((count, D), whole),
            pl.BlockSpec((1, CHUNK), by_chunk),
            pl.BlockSpec((count, 1), whole),
            pl.BlockSpec((CHUNK // LANES, weights.shape[1], LANES), lambda j: (j, 0, 0)),
            pl.BlockSpec((D, CHUNK), by_chunk),
        ],
        out_specs=[
            pl.BlockSpec((count, LANES), whole),
            pl.BlockSpec((count, LANES), whole),
            pl.BlockSpec((count, LANES), whole),
            pl.BlockSpec((teach, LANES), whole),
        ],
        out_shape=[
            row_stat,
            row_stat,
            row_stat,
            jax.ShapeDtypeStruct((teach, LANES), jnp.float32),
        ],
        compiler_params=pltpu.CompilerParams(
            vmem_limit_bytes=VMEM_LIMIT, dimension_semantics=("arbitrary",)
        ),
        cost_estimate=pl.CostEstimate(
            flops=2 * count * D * width,
            bytes_accessed=2 * (D + weights.shape[1]) * width,
            transcendentals=count * width,
        ),
        name="loss_stats",
    )(final_all, bias_row, targets, weights, table)


def grads_kernel(
    blocks, rows, teach, token_share, final_ref, flipped_ref, bias_ref, target_ref, level_ref,
    weight_ref, table_ref, final_grad_ref, table_grad_ref, low_ref,
):
    chunk = table_ref.shape[1]
    start = pl.program_id(0) * chunk

    @pl.when(pl.program_id(0) == 0)
    def _():
        final_grad_ref[...] = jnp.zeros(final_grad_ref.shape, jnp.float32)

    for block in range(blocks):
        span = pl.ds(block * rows, rows)
        logits = jnp.dot(final_ref[span, :], table_ref[...], preferred_element_type=jnp.float32)
        column = lax.broadcasted_iota(jnp.int32, (rows, chunk), 1)
        target = target_ref[span, :] - start
        grad = jnp.exp(logits + bias_ref[...] - level_ref[span, :])
        grad = grad - jnp.where(column == target, token_share, 0.0)
        for tile in range(chunk // LANES):
            lanes = slice(tile * LANES, (tile + 1) * LANES)
            weight = weight_ref[tile, pl.ds(block * teach, teach), :].astype(jnp.float32)
            low_ref[pl.ds(block * rows, teach), lanes] = to_low(grad[:teach, lanes] - weight)
        low_ref[pl.ds(block * rows + teach, rows - teach), :] = to_low(grad[teach:])
        final_grad_ref[span, :] += lax.dot_general(
            low_ref[span, :],
            table_ref[...],
            (((1,), (1,)), ((), ())),
            preferred_element_type=jnp.float32,
        )
    table_grad_ref[...] = to_low(
        jnp.dot(flipped_ref[...], low_ref[...], preferred_element_type=jnp.float32)
    )


def loss_grads(final_all, table, bias_row, targets, levels, weights, blocks, token_share):
    count = final_all.shape[0]
    width = table.shape[1]
    rows = count // blocks
    teach = weights.shape[1] // blocks
    whole = lambda j: (0, 0)
    by_chunk = lambda j: (0, j)
    return pl.pallas_call(
        functools.partial(grads_kernel, blocks, rows, teach, token_share),
        grid=(width // CHUNK,),
        in_specs=[
            pl.BlockSpec((count, D), whole),
            pl.BlockSpec((D, count), whole),
            pl.BlockSpec((1, CHUNK), by_chunk),
            pl.BlockSpec((count, 1), whole),
            pl.BlockSpec((count, 1), whole),
            pl.BlockSpec((CHUNK // LANES, weights.shape[1], LANES), lambda j: (j, 0, 0)),
            pl.BlockSpec((D, CHUNK), by_chunk),
        ],
        out_specs=[pl.BlockSpec((count, D), whole), pl.BlockSpec((D, CHUNK), by_chunk)],
        out_shape=[
            jax.ShapeDtypeStruct((count, D), jnp.float32),
            jax.ShapeDtypeStruct((D, width), jnp.bfloat16),
        ],
        scratch_shapes=[pltpu.VMEM((count, CHUNK), jnp.bfloat16)],
        compiler_params=pltpu.CompilerParams(
            vmem_limit_bytes=VMEM_LIMIT, dimension_semantics=("arbitrary",)
        ),
        cost_estimate=pl.CostEstimate(
            flops=6 * count * D * width,
            bytes_accessed=2 * (2 * D + weights.shape[1]) * width + 4 * count * D,
            transcendentals=count * width,
        ),
        name="loss_grads",
    )(final_all, final_all.T, bias_row, targets, levels, weights, table)


def lookup_kernel(place_ref, table_ref, out_ref):
    def some(group, carry):
        for at in range(16):
            row = group * 16 + at
            out_ref[pl.ds(row, 1), :] = table_ref[pl.ds(place_ref[row], 1), :]
        return carry

    lax.fori_loop(0, out_ref.shape[0] // 16, some, 0)


def lookup(places, table):
    count, width = places.shape[0], table.shape[1]
    return pl.pallas_call(
        lookup_kernel,
        out_shape=jax.ShapeDtypeStruct((count, width), jnp.float32),
        in_specs=[
            pl.BlockSpec(memory_space=pltpu.SMEM),
            pl.BlockSpec(memory_space=pltpu.VMEM),
        ],
        out_specs=pl.BlockSpec(memory_space=pltpu.VMEM),
        compiler_params=pltpu.CompilerParams(vmem_limit_bytes=VMEM_LIMIT),
        cost_estimate=pl.CostEstimate(
            flops=count * width, bytes_accessed=70_000_000, transcendentals=0
        ),
        name="lookup",
    )(places, table)


def scatter_kernel(place_ref, grad_ref, out_ref, *sum_refs):
    streams = len(sum_refs)
    for sum_ref in sum_refs:
        sum_ref[...] = jnp.zeros(sum_ref.shape, jnp.float32)
    run = grad_ref.shape[0] // streams

    def some(group, carry):
        for at in range(4):
            for stream, sum_ref in enumerate(sum_refs):
                row = stream * run + group * 4 + at
                sum_ref[pl.ds(place_ref[row], 1), :] += grad_ref[pl.ds(row, 1), :]
        return carry

    lax.fori_loop(0, run // 4, some, 0)
    total = sum_refs[0][: out_ref.shape[0], :]
    for sum_ref in sum_refs[1:]:
        total = total + sum_ref[: out_ref.shape[0], :]
    out_ref[...] = total


def scatter_add(places, grads, height):
    count, width = grads.shape
    return pl.pallas_call(
        scatter_kernel,
        out_shape=jax.ShapeDtypeStruct((height, width), jnp.float32),
        in_specs=[
            pl.BlockSpec(memory_space=pltpu.SMEM),
            pl.BlockSpec(memory_space=pltpu.VMEM),
        ],
        out_specs=pl.BlockSpec(memory_space=pltpu.VMEM),
        scratch_shapes=[pltpu.VMEM((height + 8, width), jnp.float32)] * 4,
        compiler_params=pltpu.CompilerParams(vmem_limit_bytes=VMEM_LIMIT),
        cost_estimate=pl.CostEstimate(
            flops=count * width, bytes_accessed=90_000_000, transcendentals=0
        ),
        name="scatter_add",
    )(places, grads)


def local(
    mel_frames,
    dec_ids,
    targets,
    teach_rows,
    teach_ids,
    teach_probs,
    vocab_mask,
    projections,
    out_proj,
    feed_forward,
    conv_kernels,
    embed_table,
    small_params,
    moment_projections,
    moment_out_proj,
    moment_feed_forward,
    moment_conv_kernels,
    moment_embed_table,
    moment_small_params,
    average_projections,
    average_out_proj,
    average_feed_forward,
    average_conv_kernels,
    average_embed_table,
    average_small_params,
):
    fsdp_count, ctx_count, tp_count = (lax.axis_size(axis) for axis in ALL)
    fsdp_index, ctx_index, tp_index = (lax.axis_index(axis) for axis in ALL)
    clip_count = mel_frames.shape[0]
    blocks = ctx_count * tp_count
    part_count = ctx_count
    paired = ctx_count == 2 and tp_count % 2 == 0
    block_index = ctx_index * tp_count + tp_index
    if paired:
        clip_index, part_index = block_index // 2, block_index % 2
        part_of_block = jnp.arange(blocks, dtype=jnp.int32) % 2
    else:
        clip_index, part_index = tp_index, ctx_index
        part_of_block = jnp.arange(blocks, dtype=jnp.int32) // tp_count

    def in_blocks(values):
        if paired:
            values = jnp.swapaxes(values, 0, 1)
        return values.reshape((blocks,) + values.shape[2:])

    pairs = [(i, i ^ 1) for i in range(tp_count)]

    def spread_rows(rows):
        if paired:
            return jnp.concatenate([rows, lax.ppermute(rows, "tp", pairs)], axis=0)
        return lax.all_gather(rows, "ctx", axis=0, tiled=True)

    def collect_rows(rows):
        if paired:
            half = rows.shape[0] // 2
            other = lax.ppermute(to_low(rows[half:]), "tp", pairs)
            return rows[:half] + other.astype(jnp.float32)
        return lax.psum_scatter(to_low(rows), "ctx", scatter_dimension=0, tiled=True).astype(
            jnp.float32
        )

    enc_rows = mel_frames.shape[1] // 2
    dec_rows = dec_ids.shape[1]
    teach_count = teach_rows.shape[1]
    vocab_local = embed_table.shape[0]

    piece = D // (fsdp_count * ctx_count * tp_count)
    thick = D // (fsdp_count * ctx_count)

    def by_owner(values):
        count, height, width = values.shape
        return values.reshape(count, tp_count, height // tp_count, width).swapaxes(0, 1)

    def swapped_rows(values):
        arrived = lax.all_to_all(values, "tp", 0, 0, tiled=True)
        return arrived.transpose(1, 2, 0, 3).reshape(arrived.shape[1], arrived.shape[2], D)

    narrow_attn = by_owner(jnp.concatenate([to_low(projections), to_low(out_proj)], axis=0))
    narrow_conv = by_owner(to_low(conv_kernels)[None])
    narrow_conv = narrow_conv.reshape(tp_count, KW, piece, D // tp_count)
    own_rows = swapped_rows(jnp.concatenate([narrow_attn, narrow_conv], axis=1))
    feed_low = to_low(feed_forward)

    groups = (
        ((0, 1, 2, 9), (), True),
        ((), (0, 1), False),
        ((3, 4, 5, 10, 6, 7, 8, 11), (), False),
        ((), (2, 3), False),
    )
    narrow_full, feed_full = {}, {}
    stacks = []
    for narrow_members, feed_members, with_conv in groups:
        parts = []
        if with_conv:
            parts.append(own_rows[12:].reshape(KW * piece, D))
        parts += [own_rows[member] for member in narrow_members]
        parts += [feed_low[member] for member in feed_members]
        stacks.append(jnp.concatenate(parts, axis=0))
    held_of = [spread(stack, "fsdp") for stack in stacks]

    def plane_full(held):
        return lax.all_gather(held, PLANE, axis=0).reshape(
            (ctx_count, tp_count) + held.shape
        )

    def unpack(group, full):
        narrow_members, feed_members, with_conv = group
        offset = KW * piece if with_conv else 0
        for member in narrow_members:
            narrow_full[member] = (
                full[:, :, :, offset : offset + piece].transpose(2, 0, 1, 3, 4).reshape(D, D)
            )
            offset += piece
        for member in feed_members:
            feed_full[member] = (
                full[:, :, :, offset : offset + thick].transpose(2, 0, 3, 1, 4).reshape(D, FF)
            )
            offset += thick

    vocab_part = -(-vocab_local // (ctx_count * CHUNK)) * CHUNK
    table_low = to_low(embed_table)
    table_wide = jnp.pad(table_low.T, ((0, 0), (0, ctx_count * vocab_part - vocab_local)))

    def vocab_slice(step):
        start = lax.rem(ctx_index + step, ctx_count) * vocab_part
        return lax.dynamic_slice_in_dim(table_wide, start, vocab_part, 1)

    table_held = in_order(sent_to_owners(vocab_slice, "ctx"), "ctx")
    table_held = table_held.reshape(ctx_count * thick, vocab_part)

    held_of[0], dec_ids = together(held_of[0], dec_ids)
    full = plane_full(held_of[0])
    conv_full = full[:, :, :, : KW * piece].transpose(2, 0, 1, 3, 4).reshape(KW, D, D)
    unpack(groups[0], full)
    ids_plane = spread(jnp.stack([dec_ids, targets]), "ctx")
    ids_all = spread(in_blocks(ids_plane[:, 0]), "fsdp").reshape(
        fsdp_count, ctx_count, tp_count, dec_rows
    )
    target_blocks = in_blocks(ids_plane[:, 1])

    ids_local = ids_all.transpose(2, 0, 1, 3).reshape(-1) - tp_index * vocab_local
    ids_inside = jnp.logical_and(ids_local >= 0, ids_local < vocab_local)
    looked = lookup(jnp.where(ids_inside, ids_local, 0), embed_table)
    looked = to_low(jnp.where(ids_inside[:, None], looked, 0.0))
    looked = looked.reshape(tp_count, fsdp_count * ctx_count * dec_rows, thick)
    looked = lax.psum_scatter(looked, "tp", scatter_dimension=0, tiled=False)
    looked = looked.reshape(fsdp_count * ctx_count, dec_rows, thick)
    looked = lax.all_to_all(looked, ("fsdp", "ctx"), 0, 0, tiled=True)
    embedded = looked.transpose(1, 0, 2).reshape(dec_rows, D).astype(jnp.float32)

    packed = jnp.concatenate(
        [
            teach_probs,
            teach_ids.astype(jnp.float32),
            teach_rows[..., None].astype(jnp.float32),
        ],
        axis=2,
    )
    packed, held_of[2] = together(packed, held_of[2])
    unpack(groups[2], plane_full(held_of[2]))
    packed = in_blocks(spread(packed, "ctx"))
    top_count = teach_probs.shape[2]
    taught = (
        packed[:, :, -1].astype(jnp.int32),
        packed[:, :, top_count : 2 * top_count].astype(jnp.int32),
        packed[:, :, :top_count],
    )
    token_total = clip_count * fsdp_count * dec_rows * ctx_count
    teach_total = clip_count * fsdp_count * teach_count * ctx_count
    token_share = 1.0 / token_total
    row_place = jnp.arange(dec_rows, dtype=jnp.int32)
    taught_rows = taught[0] - part_of_block[:, None] * dec_rows
    hits = taught_rows[:, :, None] == row_place[None, None, :]
    rank_taught = jnp.sum(
        jnp.where(hits, jnp.arange(teach_count, dtype=jnp.int32)[None, :, None], 0), axis=1
    )
    is_taught = jnp.any(hits, axis=1)
    earlier = row_place[None, :, None] < row_place[None, None, :]
    rank_other = teach_count + jnp.sum(
        jnp.where(jnp.logical_and(earlier, ~is_taught[:, :, None]), 1, 0), axis=1
    )
    new_place = jnp.where(is_taught, rank_taught, rank_other)
    moved = new_place[:, None, :] == row_place[None, :, None]
    vocab_start = tp_index * vocab_local + ctx_index * vocab_part
    vocab_valid = jnp.minimum(vocab_part, vocab_local - ctx_index * vocab_part)
    target_local = (
        jnp.sum(jnp.where(moved, target_blocks[:, None, :], 0), axis=2) - vocab_start
    )
    target_local = jnp.where(
        jnp.logical_and(target_local >= 0, target_local < vocab_valid), target_local, -1
    ).reshape(-1, 1)
    share_taught = taught[2] / teach_total
    row_weight = jnp.concatenate(
        [
            token_share + jnp.sum(share_taught, axis=2),
            jnp.full((blocks, dec_rows - teach_count), token_share, jnp.float32),
        ],
        axis=1,
    ).reshape(-1)
    taught_local = (taught[1] - vocab_start).reshape(blocks * teach_count, -1)
    inside = jnp.logical_and(taught_local >= 0, taught_local < vocab_valid)
    high = jnp.where(inside, taught_local // LANES, -1)
    low_part = taught_local - taught_local // LANES * LANES
    high_hot = jnp.where(
        high[:, None, :] == jnp.arange(vocab_part // LANES, dtype=jnp.int32)[None, :, None],
        share_taught.reshape(blocks * teach_count, 1, -1),
        0.0,
    ).astype(jnp.bfloat16)
    low_hot = (
        low_part[:, None, :] == jnp.arange(LANES, dtype=jnp.int32)[None, :, None]
    ).astype(jnp.bfloat16)
    teach_weight = to_low(product("rhk,rlk->hrl", high_hot, low_hot))
    mask_wide = jnp.pad(vocab_mask, (0, ctx_count * vocab_part - vocab_local))
    mask_part = lax.dynamic_slice_in_dim(mask_wide, ctx_index * vocab_part, vocab_part, 0)
    bias_row = jnp.where(mask_part > 0, 0.0, NEG_FILL).astype(jnp.float32)[None, :]

    if paired:
        partner_block = (1 - ctx_index) * tp_count + tp_index
        mine = pick(mel_frames, clip_index)
        arrived = lax.ppermute(pick(mel_frames, partner_block // 2), "ctx", [(0, 1), (1, 0)])
        clip_mel = jnp.where(
            ctx_index == 0,
            jnp.concatenate([mine, arrived], axis=0),
            jnp.concatenate([arrived, mine], axis=0),
        )
    else:
        clip_mel = lax.all_gather(pick(mel_frames, clip_index), "ctx", axis=0, tiled=True)
    frame_pairs = jnp.pad(clip_mel.reshape(-1, 2 * MEL), ((1, 1), (0, 0)))
    near = lax.dynamic_slice_in_dim(frame_pairs, part_index * enc_rows, enc_rows + 2, 0)
    evens, odds = near[:, :MEL], near[:, MEL:]
    evens, odds, held_of[1] = together(evens, odds, held_of[1])
    unpack(groups[1], plane_full(held_of[1]))
    taps_even = jnp.concatenate([odds[:-2], evens[1:-1], odds[1:-1]], axis=1)
    taps_odd = jnp.concatenate([evens[:-1], odds[:-1], evens[1:]], axis=1)

    hidden_bias = small_params[27:NVEC].reshape(2, FF)
    kernel_one = to_low(small_params[NVEC : NVEC + KW * MEL])
    pre_even = product("fm,mo->fo", taps_even, kernel_one) + small_params[14]
    pre_odd = product("fm,mo->fo", taps_odd, kernel_one) + small_params[14]
    odd_open = jnp.logical_or(
        part_index > 0, jnp.arange(enc_rows + 1, dtype=jnp.int32) > 0
    )[:, None]
    first_even = to_low(gelu_exact(pre_even))
    first_odd = to_low(jnp.where(odd_open, gelu_exact(pre_odd), 0.0))
    first_even, first_odd, held_of[3], teach_weight = together(
        first_even, first_odd, held_of[3], teach_weight
    )
    unpack(groups[3], plane_full(held_of[3]))
    taps_two = (first_odd[:-1], first_even, first_odd[1:])
    second_pre = small_params[15]
    for tap in range(KW):
        second_pre = second_pre + product("ji,oi->jo", taps_two[tap], conv_full[tap])
    stream_zero = gelu_exact(second_pre) + sinusoid(part_index * enc_rows, enc_rows, D)
    enc_one = to_low(layer_norm(stream_zero, small_params[0], small_params[1]))
    enc_one, table_held = together(enc_one, table_held)
    table_block = lax.all_gather(table_held, "fsdp", axis=0, tiled=True)
    enc_one_clip = spread_rows(enc_one)
    enc_weights = (narrow_full[0], narrow_full[1], narrow_full[2], narrow_full[9])
    attn_out, enc_saved = attention_forward(
        enc_one,
        enc_one_clip,
        enc_weights,
        (small_params[16], small_params[17], small_params[18]),
        None,
        None,
    )
    stream_one = stream_zero + attn_out
    enc_two = to_low(layer_norm(stream_one, small_params[2], small_params[3]))
    feed_out, enc_feed_saved = feed_forward_pass(
        enc_two, feed_full[0], hidden_bias[0], feed_full[1], small_params[19]
    )
    stream_two = stream_one + feed_out
    encoded = to_low(layer_norm(stream_two, small_params[4], small_params[5]))
    encoded_clip = spread_rows(encoded)

    dec_start = part_index * dec_rows
    query_place = dec_start + row_place
    if paired:
        key_place = jnp.concatenate([query_place, (1 - part_index) * dec_rows + row_place])
    else:
        key_place = jnp.arange(dec_rows * part_count, dtype=jnp.int32)
    position_start = NVEC + KW * MEL
    tokens_zero = embedded + lax.dynamic_slice_in_dim(
        small_params, position_start + dec_start, dec_rows, 0
    )
    dec_one = to_low(layer_norm(tokens_zero, small_params[6], small_params[7]))
    dec_one_clip = spread_rows(dec_one)
    self_weights = (narrow_full[3], narrow_full[4], narrow_full[5], narrow_full[10])
    self_out, self_saved = attention_forward(
        dec_one,
        dec_one_clip,
        self_weights,
        (small_params[20], small_params[21], small_params[22]),
        key_place,
        query_place,
    )
    tokens_one = tokens_zero + self_out
    dec_two = to_low(layer_norm(tokens_one, small_params[8], small_params[9]))
    cross_weights = (narrow_full[6], narrow_full[7], narrow_full[8], narrow_full[11])
    cross_out, cross_saved = attention_forward(
        dec_two,
        encoded_clip,
        cross_weights,
        (small_params[23], small_params[24], small_params[25]),
        None,
        None,
    )
    tokens_two = tokens_one + cross_out
    dec_three = to_low(layer_norm(tokens_two, small_params[10], small_params[11]))
    dec_feed_out, dec_feed_saved = feed_forward_pass(
        dec_three, feed_full[2], hidden_bias[1], feed_full[3], small_params[26]
    )
    tokens_three = tokens_two + dec_feed_out
    tokens_three, table_block = together(tokens_three, table_block)
    final = to_low(layer_norm(tokens_three, small_params[12], small_params[13]))

    moved_own = pick(moved, block_index).astype(jnp.bfloat16)
    final_moved = to_low(product("np,pd->nd", moved_own, final))
    final_all = lax.all_gather(final_moved, PLANE, axis=0, tiled=True)
    top_lanes, total_lanes, picked, dots = loss_stats(
        final_all, table_block, bias_row, target_local, teach_weight, blocks
    )
    top_own = jnp.max(top_lanes, axis=1)
    total_own = jnp.sum(total_lanes * jnp.exp(top_lanes - top_own[:, None]), axis=1)
    stats = lax.all_gather(jnp.stack([top_own, total_own]), PLANE, axis=0)
    joint_top = jnp.max(stats[:, 0], axis=0)
    joint_total = jnp.sum(stats[:, 1] * jnp.exp(stats[:, 0] - joint_top), axis=0)
    log_total = joint_top + jnp.log(joint_total)
    loss_term = (
        jnp.sum(row_weight * log_total) / blocks
        + jnp.sum(teach_probs * jnp.log(teach_probs)) / (teach_total * tp_count)
        - jnp.sum(picked) * token_share
        - jnp.sum(dots)
    )
    levels = (log_total - jnp.log(row_weight))[:, None]
    final_grad, table_grad = loss_grads(
        final_all, table_block, bias_row, target_local, levels, teach_weight, blocks, token_share
    )
    grad_final_moved = lax.psum_scatter(
        to_low(final_grad), PLANE, scatter_dimension=0, tiled=True
    )
    grad_final = product("np,nd->pd", moved_own, grad_final_moved)

    table_sum = lax.psum_scatter(table_grad, "fsdp", scatter_dimension=0, tiled=True)

    def cut_narrow(grad, height):
        return (
            to_low(grad)
            .reshape(fsdp_count, ctx_count, tp_count, height, D)
            .transpose(1, 2, 0, 3, 4)
        )

    def cut_feed(grad):
        return (
            to_low(grad)
            .reshape(fsdp_count, ctx_count, thick, tp_count, D)
            .transpose(1, 3, 0, 2, 4)
        )

    def packed_grads(pieces):
        held = jnp.concatenate(pieces, axis=3)
        return held.reshape((blocks,) + held.shape[2:])

    def plane_sum(held):
        return lax.psum_scatter(held, PLANE, scatter_dimension=0, tiled=False)

    def own_columns(grad, heights):
        cut = to_low(grad).reshape(grad.shape[0], tp_count, D // tp_count).swapaxes(0, 1)
        arrived = lax.all_to_all(cut, "tp", 0, 0, tiled=True).astype(jnp.float32)
        out, offset = [], 0
        for height in heights:
            out.append(
                arrived[:, offset : offset + height].reshape(
                    tp_count * height, D // tp_count
                )
            )
            offset += height
        return out

    row_grads = {}
    grad_three, row_grads[12], row_grads[13] = norm_back(
        tokens_three, small_params[12], small_params[13], grad_final
    )
    grad_feed = to_low(grad_three)
    row_grads[26] = jnp.sum(grad_feed, axis=0, dtype=jnp.float32)
    feed_grad_2, feed_grad_3, dec_bias_in, back = feed_backward(
        dec_three, feed_full[2], feed_full[3], dec_feed_saved, grad_feed
    )
    held_dec_feed = packed_grads([cut_feed(feed_grad_2), cut_feed(feed_grad_3)])
    back, held_dec_feed = together(back, held_dec_feed)
    part_dec_feed = plane_sum(held_dec_feed)
    back, row_grads[10], row_grads[11] = norm_back(
        tokens_two, small_params[10], small_params[11], back
    )
    grad_two = grad_three + back
    grad_cross = to_low(grad_two)
    row_grads[25] = jnp.sum(grad_cross, axis=0, dtype=jnp.float32)
    cross_grads, row_grads[23], row_grads[24], back_q, back_encoded = attention_backward(
        dec_two, encoded_clip, cross_weights, cross_saved, grad_cross, None, None
    )
    back, row_grads[8], row_grads[9] = norm_back(
        tokens_one, small_params[8], small_params[9], back_q
    )
    grad_one = grad_two + back
    grad_self = to_low(grad_one)
    row_grads[22] = jnp.sum(grad_self, axis=0, dtype=jnp.float32)
    self_grads, row_grads[20], row_grads[21], back_q, back_k = attention_backward(
        dec_one, dec_one_clip, self_weights, self_saved, grad_self, key_place, query_place
    )
    held_dec_attn = packed_grads([cut_narrow(grad, piece) for grad in self_grads + cross_grads])
    back, row_grads[6], row_grads[7] = norm_back(
        tokens_zero, small_params[6], small_params[7], back_q + collect_rows(back_k)
    )
    grad_zero = grad_one + back
    position_rows = lax.dynamic_update_slice_in_dim(
        jnp.zeros((dec_rows * part_count, D), jnp.float32), grad_zero, dec_start, 0
    )
    sent = to_low(grad_zero).reshape(dec_rows, fsdp_count * ctx_count, thick).swapaxes(0, 1)
    sent = lax.all_to_all(sent, ("fsdp", "ctx"), 0, 0, tiled=True)
    sent = sent.reshape(fsdp_count, ctx_count, dec_rows, thick)
    sent = lax.all_gather(sent, "tp", axis=0).reshape(-1, thick).astype(jnp.float32)
    embed_grad = scatter_add(jnp.where(ids_inside, ids_local, vocab_local), sent, vocab_local)

    def small_plane_sum(rows):
        rows = jnp.pad(rows, ((0, -rows.shape[0] % (8 * blocks)), (0, 0)))
        return lax.psum_scatter(rows, PLANE, scatter_dimension=0, tiled=True)

    position_part = small_plane_sum(position_rows)

    back_encoded, held_dec_attn, table_sum = together(back_encoded, held_dec_attn, table_sum)
    part_dec_attn = plane_sum(held_dec_attn)
    back_encoded_own = collect_rows(back_encoded)
    grad_stream_two, row_grads[4], row_grads[5] = norm_back(
        stream_two, small_params[4], small_params[5], back_encoded_own
    )
    grad_feed = to_low(grad_stream_two)
    row_grads[19] = jnp.sum(grad_feed, axis=0, dtype=jnp.float32)
    feed_grad_0, feed_grad_1, enc_bias_in, back = feed_backward(
        enc_two, feed_full[0], feed_full[1], enc_feed_saved, grad_feed
    )
    held_enc_feed = packed_grads([cut_feed(feed_grad_0), cut_feed(feed_grad_1)])
    back, row_grads[2], row_grads[3] = norm_back(
        stream_one, small_params[2], small_params[3], back
    )
    grad_stream_one = grad_stream_two + back
    grad_stream_one, part_dec_feed, held_enc_feed = together(
        grad_stream_one, part_dec_feed, held_enc_feed
    )
    part_enc_feed = plane_sum(held_enc_feed)
    sum_dec_feed = sum_to_owner(part_dec_feed, "fsdp")
    grad_attn = to_low(grad_stream_one)
    row_grads[18] = jnp.sum(grad_attn, axis=0, dtype=jnp.float32)
    enc_grads, row_grads[16], row_grads[17], back_q, back_k = attention_backward(
        enc_one, enc_one_clip, enc_weights, enc_saved, grad_attn, None, None
    )
    back, row_grads[0], row_grads[1] = norm_back(
        stream_zero, small_params[0], small_params[1], back_q + collect_rows(back_k)
    )
    grad_stream_zero = grad_stream_one + back
    grad_stream_zero, part_dec_attn, position_part, sum_dec_feed = together(
        grad_stream_zero, part_dec_attn, position_part, sum_dec_feed
    )
    sum_dec_attn = sum_to_owner(part_dec_attn, "fsdp")
    position_part = exchanged_sum(position_part, ("fsdp",))
    table_sum = table_sum.reshape(ctx_count, thick, vocab_part)
    table_sum = in_order(
        sent_to_owners(lambda step: pick(table_sum, lax.rem(ctx_index + step, ctx_count)), "ctx"),
        "ctx",
    )
    table_sum = table_sum.swapaxes(0, 1).reshape(thick, ctx_count * vocab_part)[:, :vocab_local]
    grad_second = to_low(gelu_back(second_pre, grad_stream_zero))
    row_grads[15] = jnp.sum(grad_second, axis=0, dtype=jnp.float32)
    conv_grads = [product("jo,ji->oi", grad_second, taps_two[tap]) for tap in range(KW)]
    held_enc_attn = packed_grads(
        [cut_narrow(jnp.concatenate(conv_grads, axis=0), KW * piece)]
        + [cut_narrow(grad, piece) for grad in enc_grads]
    )
    sum_enc_attn = sum_to_owner(plane_sum(held_enc_attn), "fsdp")
    sum_enc_feed = sum_to_owner(part_enc_feed, "fsdp")
    grad_taps = [product("jo,oi->ji", grad_second, conv_full[tap]) for tap in range(KW)]
    grad_odd = jnp.pad(grad_taps[0], ((0, 1), (0, 0))) + jnp.pad(grad_taps[2], ((1, 0), (0, 0)))
    grad_pre_even = to_low(gelu_back(pre_even, grad_taps[1]))
    grad_pre_odd = to_low(jnp.where(odd_open, gelu_back(pre_odd, grad_odd), 0.0))
    row_grads[14] = jnp.sum(grad_pre_even, axis=0, dtype=jnp.float32) + jnp.sum(
        grad_pre_odd, axis=0, dtype=jnp.float32
    )
    kernel_rows = product("fm,fo->mo", taps_even, grad_pre_even) + product(
        "fm,fo->mo", taps_odd, grad_pre_odd
    )

    vector_rows = jnp.concatenate(
        [
            jnp.stack([row_grads[row] for row in range(27)]),
            enc_bias_in.reshape(4, D),
            dec_bias_in.reshape(4, D),
            kernel_rows,
        ]
    )
    vector_part = exchanged_sum(small_plane_sum(vector_rows), ("fsdp",))
    all_small = lax.all_gather(jnp.concatenate([vector_part, position_part]), PLANE, axis=0)
    split = vector_part.shape[0]
    small_grad = jnp.concatenate(
        [
            all_small[:, :split].reshape(-1, D)[: vector_rows.shape[0]],
            all_small[:, split:].reshape(-1, D)[: position_rows.shape[0]],
        ]
    )

    (embed_flat,) = together(embed_grad.T)
    shard_table = table_sum.astype(jnp.float32) + embed_flat
    dec_list = own_columns(sum_dec_attn, (piece,) * 8)
    enc_list = own_columns(sum_enc_attn, (KW * piece,) + (piece,) * 4)
    shard_conv = enc_list[0]
    shard_proj = jnp.stack(enc_list[1:4] + dec_list[0:3] + dec_list[4:7])
    shard_out = jnp.stack([enc_list[4], dec_list[3], dec_list[7]])
    shard_feed = jnp.concatenate([sum_enc_feed, sum_dec_feed]).reshape(4, thick, D)
    local_squares = (
        jnp.sum(shard_proj * shard_proj)
        + jnp.sum(shard_out * shard_out)
        + jnp.sum(shard_feed * shard_feed)
        + jnp.sum(shard_conv * shard_conv)
        + jnp.sum(shard_table * shard_table)
    )
    loss_value, big_squares = exchanged_sum(jnp.stack([loss_term, local_squares]), ALL)
    grad_norm = jnp.sqrt(big_squares + jnp.sum(small_grad * small_grad))
    factor = jnp.minimum(1.0, CLIP_NORM / (grad_norm + 1e-06))
    results = [
        nesterov(projections, shard_proj, moment_projections, average_projections, factor),
        nesterov(out_proj, shard_out, moment_out_proj, average_out_proj, factor),
        nesterov(feed_forward, shard_feed, moment_feed_forward, average_feed_forward, factor),
        nesterov(conv_kernels, shard_conv, moment_conv_kernels, average_conv_kernels, factor),
        tuple(
            part.T
            for part in nesterov(
                embed_table.T, shard_table, moment_embed_table.T, average_embed_table.T, factor
            )
        ),
        nesterov(small_params, small_grad, moment_small_params, average_small_params, factor),
    ]
    return (loss_value, grad_norm) + tuple(
        result[kind] for kind in range(3) for result in results
    )


def solution(mesh):
    by_rows = P(None, ("fsdp", "ctx"), "tp")
    weights = (
        by_rows,
        by_rows,
        by_rows,
        P(("fsdp", "ctx"), "tp"),
        P("tp", ("fsdp", "ctx")),
        P(),
    )
    pair = P("fsdp", "ctx")
    wide = P("fsdp", "ctx", None)
    in_specs = (wide, pair, pair, pair, wide, wide, P("tp")) + 3 * weights
    out_specs = (P(), P()) + 3 * weights
    return jax.shard_map(local, mesh=mesh, in_specs=in_specs, out_specs=out_specs, check_vma=False)
```

time: 3880 us -> 1510 us (0.39)
  waiting for transfers between devices: 1710 us -> 390 us
  local copies, waits for them, and re-layouts: 1060 us -> 314 us
  other arithmetic: 417 us -> 179 us
  matrix products: 461 us -> 297 us
  Pallas kernels: 0 us -> 155 us
  blocking collectives: 174 us -> 41.9 us
  starting transfers between devices: 11.8 us -> 94 us
    reduce_scatter x26 -> x9, waiting for transfers between devices: 829 us -> 140 us  [the longest x4 66.2 us: plane_sum(): return lax.psum_scatter(held, PLANE, scatter_dimension=0, tiled=False)]
    gather x8 -> x0, local copies, waits for them, and re-layouts: 636 us -> none  [the longest x3 577 us: local(): jnp.take_along_axis(teach_rows_logits, teach_clipped, axis=2)]
    all_gather x21 -> x8, waiting for transfers between devices: 715 us -> 89.5 us  [the longest x1 61.8 us: local(): table_block = lax.all_gather(table_held, 'fsdp', axis=0, tiled=True)]
    dot_general x76 -> x82, matrix products: 461 us -> 297 us  [product(): return jnp.einsum(pattern, left, right, preferred_element_type=jnp.float32)]
    ppermute x2 -> x47, waiting for transfers between devices: 0.01 us -> 158 us  [the longest x17 67.6 us: sent_to_all(): lax.ppermute(values, axis, shifted(axis, step))]
    pallas_call x0 -> x4, Pallas kernels: none -> 155 us  [the longest x1 82.5 us: loss_grads(): pl.pallas_call(functools.partial(grads_kernel, blocks, rows, teach, token...]
    all_gather x8 -> x1, blocking collectives: 134 us -> 9.18 us  [local(): stats = lax.all_gather(jnp.stack([top_own, total_own]), PLANE, axis=0)]
    unnamed x9 -> x8, other arithmetic: 122 us -> 0.03 us
  transfers between devices with their start and end apart: 54 -> 67, of which waited for: 36 -> 29; matrix products, arithmetic and copies ran while one was open for 15% -> 43% of each run, Pallas kernels for 0% -> 1%
where the time goes in v1:
time: 1510 us; the launch traced here: 1500 us
  waiting for transfers between devices  390 us (26%)
  local copies, waits for them, and re-layouts  314 us (21%)
  matrix products  297 us (20%)
  other arithmetic  179 us (12%)
  Pallas kernels  155 us (10%)
  starting transfers between devices  94 us (6%)
  blocking collectives  41.9 us (3%)
  between operations  29.3 us (2%)
    dot_general x82, matrix products, product(): return jnp.einsum(pattern, left, right, preferred_element_type=jnp.float32)  297 us
    unnamed x696, local copies, waits for them, and re-layouts  97.7 us
    pallas_call x1, Pallas kernels, loss_grads(): pl.pallas_call(functools.partial(grads_kernel, blocks, rows, teach, token...  82.5 us
    ppermute x17, waiting for transfers between devices, sent_to_all(): lax.ppermute(values, axis, shifted(axis, step))  67.6 us
    ppermute x14, waiting for transfers between devices, sent_to_owners(): lax.ppermute(pieces_for(step), axis, shifted(axis, step))  66.6 us
    reduce_scatter x4, waiting for transfers between devices, plane_sum(): return lax.psum_scatter(held, PLANE, scatter_dimension=0, tiled=False)  66.2 us
    all_gather x1, waiting for transfers between devices, local(): table_block = lax.all_gather(table_held, 'fsdp', axis=0, tiled=True)  61.8 us
    reshape x8, local copies, waits for them, and re-layouts, cut_feed(): return to_low(grad).reshape(fsdp_count, ctx_count, thick, tp_count, D).tr...  56.9 us
  transfers between devices with their start and end apart: 67, of which 29 were waited for; matrix products, arithmetic and copies ran while one was open for 43% of the time, Pallas kernels for 1%

profile of v1, /device:TPU:0, one launch (start us, length us, event | category | flops | bytes accessed | tf_op | source)
XLA Modules:
  0.0 1499.5 jit_solution(15521165452870199606)
XLA Ops:
  10.7 15.2 %all_to_all.25 = bf16[4,15,24,192]{3,2,1,0:T(8,128)(2,1)S(1)} all-to-all(bf16[4,15,24,192]{3,2,1,0:T(8,128)(2,1)S(1)} %copy.520), channel_id=1, replica_groups=mesh['fsdp'=4,'ctx'=2,'tp'=4] {'tp'}, dimensions={0} | all-to-all | bytes 1105920 | tf_op jit(solution)/shard_map/all_to_all | solution.py:515
  38.5 9.8 collective-permute-done.5
  52.7 6.0 collective-permute-start.8
  61.2 6.4 copy.541.table_ref
  68.7 13.8 lookup.1
  82.5 6.0 select_convert_fusion.2
  109.6 15.0 collective-permute-done.17
  126.6 13.2 collective-permute-done.14
  153.4 6.2 collective-permute-done
  159.7 9.3 collective-permute-done.1
  172.4 6.6 select_convert_fusion.4
  180.6 6.2 multiply_convert_fusion.9
  186.7 6.5 collective-permute-done.3
  193.7 10.6 fusion.1
  226.5 10.4 all-to-all-start.1
  237.5 20.1 %collective-permute-done.19 = bf16[96,6656]{1,0:T(8,128)(2,1)} collective-permute-done((bf16[96,6656]{1,0:T(8,128)(2,1)S(1)}, bf16[96,6656]{1,0:T(8,128)(2,1)}, u32[]{:S(2)}, u32[]{:S(2)}) %collective-permute-start.19) | collective-permute-done | bytes 1277984 | tf_op jit(solution)/shard_map/ppermute | solution.py:106
  271.3 11.4 fusion.178
  305.1 10.4 multiply_reduce_fusion.1
  315.6 12.0 fusion
  327.6 11.1 fusion.72
  351.1 18.7 %multiply_convert_fusion.3 = (bf16[512,3072]{1,0:T(8,128)(2,1)S(1)}, f32[512,3072]{1,0:T(8,128)}, f32[512,3072]{1,0:T(8,128)}) fusion(f32[3072]{0:T(1024)S(1)} %copy-done.261, bf16[768,3072]{1,0:T(8,128)(2,1)S(1)} %bitcast.669, f32[512,768]{1,0:T(8,128)S(1)} %copy-done.31, f32[768]{0:T(1024)S(1)} %get-tuple-element.265, f32[768]{0:T(1024)S(1)} %get-tuple-element.266, ...), kind=kOutput, calls=%fused_computation.51 | convolution fusion | flops 2521694208 | bytes 22042624 | tf_op jit(solution)/shard_map/qd,df->qf/dot_general | solution.py:36
  379.9 6.3 slice_bitcast_fusion.6
  418.1 6.8 slice_bitcast_fusion
  424.9 6.0 copy.567
  455.7 11.0 multiply_convert_fusion.6
  469.5 61.8 %all-gather.16.cloned.1.call-done.table_ref = bf16[768,6656]{1,0:T(8,128)(2,1)} async-done(((bf16[192,6656]{1,0:T(8,128)(2,1)}), bf16[768,6656]{1,0:T(8,128)(2,1)}) %all-gather.16.cloned.1.call-update) | async-done | bytes 10223632 | tf_op jit(solution)/shard_map/all_gather | solution.py:696
  537.1 27.6 %all-gather.18.cloned.1.call-done = bf16[2048,768]{0,1:T(8,128)(2,1)} async-done(((bf16[256,768]{0,1:T(8,128)(2,1)}), bf16[2048,768]{0,1:T(8,128)(2,1)}) %all-gather.18.cloned.1.call-update) | async-done | bytes 3145744 | tf_op jit(solution)/shard_map/all_gather | solution.py:759
  569.4 36.5 %loss_stats.1 = (f32[2048,128]{1,0:T(8,128)}, f32[2048,128]{1,0:T(8,128)}, f32[2048,128]{1,0:T(8,128)}, f32[64,128]{1,0:T(8,128)}) custom-call(bf16[2048,768]{1,0:T(8,128)(2,1)} %copy.574.final_ref, f32[1,6656]{1,0:T(1,128)} %broadcast_in_dim.320.bias_ref, s32[2048,1]{1,0:T(8,128)} %bitcast_select_fusion.target_ref, bf16[52,512,128]{2,1,0:T(8,128)(2,1)} %bitcast.654, ...), custom_call_target="tpu_custom_call" | custom-call | flops 20937965568 | bytes 17039360 | tf_op jit(solution)/shard_map/loss_stats/pallas_call | solution.py:268
  609.5 9.2 all-gather.6
  620.9 82.5 %loss_grads.1 = (f32[2048,768]{1,0:T(8,128)}, bf16[768,6656]{1,0:T(8,128)(2,1)}) custom-call(bf16[2048,768]{1,0:T(8,128)(2,1)} %copy.574.final_ref, bf16[768,2048]{1,0:T(8,128)(2,1)} %bitcast.707, f32[1,6656]{1,0:T(1,128)} %broadcast_in_dim.320.bias_ref, s32[2048,1]{1,0:T(8,128)} %bitcast_select_fusion.target_ref, f32[2048,1]{1,0:T(8,128)} %copy.577.level_ref, ...), custom_call_target="tpu_custom_call" | custom-call | flops 62813896704 | bytes 33554432 | tf_op jit(solution)/shard_map/loss_grads/pallas_call | solution.py:343
  709.0 45.4 %reduce-scatter.12.cloned.1.call-done = bf16[256,768]{1,0:T(8,128)(2,1)} async-done(((bf16[2048,768]{1,0:T(8,128)(2,1)}), bf16[256,768]{1,0:T(8,128)(2,1)}) %reduce-scatter.12.cloned.1.call-update) | async-done | bytes 393232 | tf_op jit(solution)/shard_map/reduce_scatter | solution.py:779
  761.5 9.8 reshape.914
  787.2 9.8 reshape.913
  800.4 6.8 pad_maximum_fusion
  813.6 11.4 multiply_reduce_fusion.2
  825.0 6.6 multiply_convert_fusion.1
  890.2 8.5 copy.582
  902.2 28.2 %reduce-scatter.14.cloned.1.call-done = bf16[192,6656]{1,0:T(8,128)(2,1)} async-done(((bf16[768,6656]{1,0:T(8,128)(2,1)}), bf16[192,6656]{1,0:T(8,128)(2,1)}) %reduce-scatter.14.cloned.1.call-update) | async-done | bytes 2555920 | tf_op jit(solution)/shard_map/reduce_scatter | solution.py:784
  955.0 9.8 reshape.934
  970.3 10.1 convert_reduce_fusion
  986.8 9.8 reshape.933
  1000.0 6.1 multiply_reduce_fusion.8
  1014.1 22.4 %multiply_reduce_fusion = (f32[12,512]{1,0:T(8,128)S(1)}, f32[12,512,1024]{2,1,0:T(8,128)}) fusion(f32[12,512,1024]{2,1,0:T(8,128)} %get-tuple-element.452, f32[12,512]{1,0:T(8,128)} %log_add_fusion, bf16[512,12,64]{0,2,1:T(8,128)(2,1)S(1)} %bitcast.650, bf16[1024,12,64]{0,2,1:T(8,128)(2,1)S(1)} %bitcast.724), kind=kOutput, calls=%fused_computation.1 | convolution fusion | flops 830466048 | bytes 52740096 | tf_op jit(solution)/shard_map/qhd,khd->hqk/dot_general | solution.py:36
  1036.5 17.0 %multiply_convert_fusion = bf16[12,512,1024]{2,1,0:T(8,128)(2,1)S(1)} fusion(f32[12,512,1024]{2,1,0:T(8,128)} %get-tuple-element.475, f32[12,512,1024]{2,1,0:T(8,128)} %get-tuple-element.452, f32[12,512]{1,0:T(8,128)S(1)} %get-tuple-element.474, f32[12,512]{1,0:T(8,128)S(1)} %copy-done.145), kind=kLoop, calls=%fused_computation | loop fusion | flops 31457280 | bytes 62963712 | tf_op jit(solution)/shard_map/convert_element_type | solution.py:32
  1059.1 14.6 convert_reduce_fusion.3
  1087.8 6.3 convert_reduce_fusion.8
  1094.3 18.2 %collective-permute-done.26 = bf16[192,768]{1,0:T(8,128)(2,1)} collective-permute-done((bf16[192,768]{1,0:T(8,128)(2,1)}, bf16[192,768]{1,0:T(8,128)(2,1)}, u32[]{:S(2)}, u32[]{:S(2)}) %collective-permute-start.26) | collective-permute-done | bytes 294944 | tf_op jit(solution)/shard_map/ppermute | solution.py:106
  1121.1 11.3 reduce-scatter.18.cloned.1.call-done
  1148.2 17.5 %all_to_all.26 = bf16[8,256,96]{1,2,0:T(8,128)(2,1)} all-to-all(bf16[8,256,96]{1,2,0:T(8,128)(2,1)} %bitcast.733), channel_id=1, replica_groups=mesh['fsdp'=4,'ctx'=2,'tp'=4] {'fsdp','ctx'}, dimensions={0} | all-to-all | bytes 786432 | tf_op jit(solution)/shard_map/all_to_all | solution.py:859
  1183.6 7.3 copy.586
  1204.7 6.5 collective-permute-done.46
  1217.5 6.5 copy.594
  1224.0 6.6 copy.592
  1241.0 21.8 %scatter_add.1 = f32[12968,96]{1,0:T(8,128)} custom-call(s32[8192]{0:T(1024)} %get-tuple-element.436.place_ref, f32[8192,96]{1,0:T(8,128)} %bitcast.633), custom_call_target="tpu_custom_call" | custom-call | flops 786432 | bytes 90000000 | tf_op jit(solution)/shard_map/scatter_add/pallas_call | solution.py:423
  1266.8 6.1 collective-permute-done.37
  1279.9 9.9 collective-permute-done.32
  1302.1 5.8 multiply_reduce_fusion.4
  1313.2 54.8 %reduce-scatter.24.cloned.1.call-done = bf16[1,4,192,768]{3,2,1,0:T(8,128)(2,1)} async-done(((bf16[8,4,192,768]{3,2,1,0:T(8,128)(2,1)}), bf16[1,4,192,768]{3,2,1,0:T(8,128)(2,1)}) %reduce-scatter.24.cloned.1.call-update) | async-done | bytes 1179664 | tf_op jit(solution)/shard_map/reduce_scatter | solution.py:805
  1386.6 12.3 collective-permute-done.35
  1440.3 17.2 %fusion.18 = (f32[12968,96]{1,0:T(8,128)}, f32[12968,96]{1,0:T(8,128)}, f32[12968,96]{1,0:T(8,128)}) fusion(f32[12968,96]{1,0:T(8,128)} %copy.541.table_ref, f32[12968,96]{1,0:T(8,128)} %copy.594, f32[12968,96]{1,0:T(8,128)} %copy.592, f32[]{:T(128)S(6)} %min.7, f32[96,12968]{0,1:T(8,128)} %bitcast.616, bf16[96,13312]{0,1:T(8,128)(2,1)S(1)} %bitcast.622), kind=kLoop, calls=%fused_computation.37 | loop fusion | flops 14939136 | bytes 37347844 | tf_op jit(solution)/shard_map/transpose | solution.py:973
  1457.5 6.4 copy.596
  1463.9 6.4 copy.597
  1470.3 6.5 copy.598
  1482.1 5.6 multiply_add_fusion
  (1226 shorter events, 548.6 us)
Async XLA Ops:
  8.0 216.6 %reduce-scatter.10.cloned.1.call-start = ((), (), s32[]{:S(2)}) async-start(), calls=%async_computation.14 | async-start | bytes 1966080 | tf_op jit(solution)/shard_map/reduce_scatter | solution.py:586
  27.4 11.1 collective-permute-start.4
  29.0 19.3 %collective-permute-start.5 = (bf16[168,768]{1,0:T(8,128)(2,1)S(1)}, bf16[168,768]{1,0:T(8,128)(2,1)S(1)}, u32[]{:S(2)}, u32[]{:S(2)}) collective-permute-start(bf16[168,768]{1,0:T(8,128)(2,1)S(1)} %constant_dynamic-update-slice_fusion.8), channel_id=1, source_target_pairs={{0,16},{8,24},{16,0},{24,8},{1,17},{9,25},{17,1},{25,9},{2,18},{10... | collective-permute-start | bytes 774152 | tf_op jit(solution)/shard_map/ppermute | solution.py:95
  31.6 16.7 %collective-permute-start.6 = (bf16[168,768]{1,0:T(8,128)(2,1)S(1)}, bf16[168,768]{1,0:T(8,128)(2,1)S(1)}, u32[]{:S(2)}, u32[]{:S(2)}) collective-permute-start(bf16[168,768]{1,0:T(8,128)(2,1)S(1)} %constant_dynamic-update-slice_fusion.8), channel_id=1, source_target_pairs={{0,24},{8,0},{16,8},{24,16},{1,25},{9,1},{17,9},{25,17},{2,26},{10... | collective-permute-start | bytes 774152 | tf_op jit(solution)/shard_map/ppermute | solution.py:95
  48.4 3.7 collective-permute-start.7
  52.7 15.0 collective-permute-start.8
  58.8 9.0 collective-permute-start.9
  60.4 7.4 collective-permute-start.10
  91.0 173.9 %all-gather.24.cloned.1.call-start = ((), (), s32[]{:S(2)}) async-start(), calls=%async_computation.27 | async-start | bytes 9289728 | tf_op jit(solution)/shard_map/all_gather | solution.py:542
  91.6 249.7 %all-gather.26.cloned.1.call-start = ((), (), s32[]{:S(2)}) async-start(), calls=%async_computation.28 | async-start | bytes 10616832 | tf_op jit(solution)/shard_map/all_gather | solution.py:542
  92.4 15.1 %collective-permute-start.16 = (bf16[192,768]{1,0:T(8,128)(2,1)S(1)}, bf16[192,768]{1,0:T(8,128)(2,1)}, u32[]{:S(2)}, u32[]{:S(2)}) collective-permute-start(bf16[192,768]{1,0:T(8,128)(2,1)S(1)} %pad_maximum_fusion.11), channel_id=1, source_target_pairs={{0,8},{8,16},{16,24},{24,0},{1,9},{9,17},{17,25},{25,1},{2,10},{10... | collective-permute-start | bytes 884744 | tf_op jit(solution)/shard_map/ppermute | solution.py:95
  93.6 30.9 %collective-permute-start.17 = (bf16[192,768]{1,0:T(8,128)(2,1)S(1)}, bf16[192,768]{1,0:T(8,128)(2,1)}, u32[]{:S(2)}, u32[]{:S(2)}) collective-permute-start(bf16[192,768]{1,0:T(8,128)(2,1)S(1)} %pad_maximum_fusion.11), channel_id=1, source_target_pairs={{0,16},{8,24},{16,0},{24,8},{1,17},{9,25},{17,1},{25,9},{2,18},{10... | collective-permute-start | bytes 884744 | tf_op jit(solution)/shard_map/ppermute | solution.py:95
  94.9 45.8 %collective-permute-start.18 = (bf16[192,768]{1,0:T(8,128)(2,1)S(1)}, bf16[192,768]{1,0:T(8,128)(2,1)}, u32[]{:S(2)}, u32[]{:S(2)}) collective-permute-start(bf16[192,768]{1,0:T(8,128)(2,1)S(1)} %pad_maximum_fusion.11), channel_id=1, source_target_pairs={{0,24},{8,0},{16,8},{24,16},{1,25},{9,1},{17,9},{25,17},{2,26},{10... | collective-permute-start | bytes 884744 | tf_op jit(solution)/shard_map/ppermute | solution.py:95
  96.3 5.5 collective-permute-start.12
  98.6 27.0 %collective-permute-start.13 = (bf16[192,768]{1,0:T(8,128)(2,1)}, bf16[192,768]{1,0:T(8,128)(2,1)}, u32[]{:S(2)}, u32[]{:S(2)}) collective-permute-start(bf16[192,768]{1,0:T(8,128)(2,1)} %pad_maximum_fusion.10), channel_id=1, source_target_pairs={{0,8},{8,16},{16,24},{24,0},{1,9},{9,17},{17,25},{25,1},{2,10},{10... | collective-permute-start | bytes 884744 | tf_op jit(solution)/shard_map/ppermute | solution.py:95
  101.8 37.9 %collective-permute-start.14 = (bf16[192,768]{1,0:T(8,128)(2,1)}, bf16[192,768]{1,0:T(8,128)(2,1)}, u32[]{:S(2)}, u32[]{:S(2)}) collective-permute-start(bf16[192,768]{1,0:T(8,128)(2,1)} %pad_maximum_fusion.10), channel_id=1, source_target_pairs={{0,16},{8,24},{16,0},{24,8},{1,17},{9,25},{17,1},{25,9},{2,18},{10... | collective-permute-start | bytes 884744 | tf_op jit(solution)/shard_map/ppermute | solution.py:95
  107.5 33.3 %collective-permute-start.15 = (bf16[192,768]{1,0:T(8,128)(2,1)}, bf16[192,768]{1,0:T(8,128)(2,1)S(1)}, u32[]{:S(2)}, u32[]{:S(2)}) collective-permute-start(bf16[192,768]{1,0:T(8,128)(2,1)} %pad_maximum_fusion.10), channel_id=1, source_target_pairs={{0,24},{8,0},{16,8},{24,16},{1,25},{9,1},{17,9},{25,17},{2,26},{10... | collective-permute-start | bytes 884744 | tf_op jit(solution)/shard_map/ppermute | solution.py:95
  142.9 237.0 %all-gather.22.cloned.1.call-start = ((), (), s32[]{:S(2)}) async-start(), calls=%async_computation.26 | async-start | bytes 10616832 | tf_op jit(solution)/shard_map/all_gather | solution.py:542
  146.0 13.7 collective-permute-start
  150.9 18.1 %collective-permute-start.1 = (bf16[192,768]{1,0:T(8,128)(2,1)S(1)}, bf16[192,768]{1,0:T(8,128)(2,1)S(1)}, u32[]{:S(2)}, u32[]{:S(2)}) collective-permute-start(bf16[192,768]{1,0:T(8,128)(2,1)S(1)} %constant_dynamic-update-slice_fusion), channel_id=1, source_target_pairs={{0,16},{8,24},{16,0},{24,8},{1,17},{9,25},{17,1},{25,9},{2,18},{10... | collective-permute-start | bytes 884744 | tf_op jit(solution)/shard_map/ppermute | solution.py:95
  152.5 16.6 %collective-permute-start.2 = (bf16[192,768]{1,0:T(8,128)(2,1)S(1)}, bf16[192,768]{1,0:T(8,128)(2,1)S(1)}, u32[]{:S(2)}, u32[]{:S(2)}) collective-permute-start(bf16[192,768]{1,0:T(8,128)(2,1)S(1)} %constant_dynamic-update-slice_fusion), channel_id=1, source_target_pairs={{0,24},{8,0},{16,8},{24,16},{1,25},{9,1},{17,9},{25,17},{2,26},{10... | collective-permute-start | bytes 884744 | tf_op jit(solution)/shard_map/ppermute | solution.py:95
  170.2 247.8 %all-gather.28.cloned.1.call-start = ((), (), s32[]{:S(2)}) async-start(), calls=%async_computation.29 | async-start | bytes 10616832 | tf_op jit(solution)/shard_map/all_gather | solution.py:542
  179.0 14.3 collective-permute-start.3
  212.1 45.5 %collective-permute-start.19 = (bf16[96,6656]{1,0:T(8,128)(2,1)S(1)}, bf16[96,6656]{1,0:T(8,128)(2,1)}, u32[]{:S(2)}, u32[]{:S(2)}) collective-permute-start(bf16[96,6656]{1,0:T(8,128)(2,1)S(1)} %get-tuple-element.378), channel_id=1, source_target_pairs={{0,4},{4,0},{1,5},{5,1},{2,6},{6,2},{3,7},{7,3},{8,12},{12,8},{9,1... | collective-permute-start | bytes 3833864 | tf_op jit(solution)/shard_map/ppermute | solution.py:106
  226.5 34.8 %all-to-all-start.1 = ((bf16[8,256,96]{1,2,0:T(8,128)(2,1)}), bf16[8,256,96]{1,2,0:T(8,128)(2,1)S(1)}, u32[]{:S(2)}, u32[]{:S(2)}) async-start(bf16[8,256,96]{1,2,0:T(8,128)(2,1)} %copy.543), calls=%async_computation.2 | async-start | bytes 786432 | tf_op jit(solution)/shard_map/all_to_all | solution.py:588
  236.9 294.4 %all-gather.16.cloned.1.call-start = ((), (), s32[]{:S(2)}) async-start(), calls=%async_computation.15 | async-start | bytes 12779520 | tf_op jit(solution)/shard_map/all_gather | solution.py:696
  264.9 122.5 %collective-permute-start.11 = (bf16[256,768]{1,0:T(8,128)(2,1)}, bf16[256,768]{1,0:T(8,128)(2,1)}, u32[]{:S(2)}, u32[]{:S(2)}) collective-permute-start(bf16[256,768]{1,0:T(8,128)(2,1)} %add_convert_fusion.15), channel_id=1, source_target_pairs={{0,1},{1,0},{2,3},{3,2},{4,5},{5,4},{6,7},{7,6},{8,9},{9,8},{10,11... | collective-permute-start | bytes 1179656 | tf_op jit(solution)/shard_map/ppermute | solution.py:490
  284.3 16.1 %collective-permute-start.20 = (bf16[512,768]{1,0:T(8,128)(2,1)}, bf16[512,768]{1,0:T(8,128)(2,1)}, u32[]{:S(2)}, u32[]{:S(2)}) collective-permute-start(bf16[512,768]{1,0:T(8,128)(2,1)} %add_convert_fusion.9), channel_id=1, source_target_pairs={{0,1},{1,0},{2,3},{3,2},{4,5},{5,4},{6,7},{7,6},{8,9},{9,8},{10,11... | collective-permute-start | bytes 2359304 | tf_op jit(solution)/shard_map/ppermute | solution.py:490
  299.0 265.8 %all-gather.18.cloned.1.call-start = ((), (), s32[]{:S(2)}) async-start(), calls=%async_computation.16 | async-start | bytes 3538944 | tf_op jit(solution)/shard_map/all_gather | solution.py:759
  379.8 56.8 %collective-permute-start.21 = (bf16[512,768]{1,0:T(8,128)(2,1)}, bf16[512,768]{1,0:T(8,128)(2,1)}, u32[]{:S(2)}, u32[]{:S(2)}) collective-permute-start(bf16[512,768]{1,0:T(8,128)(2,1)} %add_convert_fusion.6), channel_id=1, source_target_pairs={{0,1},{1,0},{2,3},{3,2},{4,5},{5,4},{6,7},{7,6},{8,9},{9,8},{10,11... | collective-permute-start | bytes 2359304 | tf_op jit(solution)/shard_map/ppermute | solution.py:490
  533.8 220.6 %reduce-scatter.12.cloned.1.call-start = ((), (), s32[]{:S(2)}) async-start(), calls=%async_computation.17 | async-start | bytes 3538944 | tf_op jit(solution)/shard_map/reduce_scatter | solution.py:779
  708.2 222.2 %reduce-scatter.14.cloned.1.call-start = ((), (), s32[]{:S(2)}) async-start(), calls=%async_computation.18 | async-start | bytes 12779520 | tf_op jit(solution)/shard_map/reduce_scatter | solution.py:784
  708.8 302.9 %reduce-scatter.16.cloned.1.call-start = ((), (), s32[]{:S(2)}) async-start(), calls=%async_computation.19 | async-start | bytes 10616832 | tf_op jit(solution)/shard_map/reduce_scatter | solution.py:805
  808.8 312.3 %reduce-scatter.20.cloned.1.call-start = ((), (), s32[]{:S(2)}) async-start(), calls=%async_computation.21 | async-start | bytes 1769472 | tf_op jit(solution)/shard_map/reduce_scatter | solution.py:866
  850.6 28.4 %collective-permute-start.24 = (bf16[256,768]{1,0:T(8,128)(2,1)}, bf16[256,768]{1,0:T(8,128)(2,1)}, u32[]{:S(2)}, u32[]{:S(2)}) collective-permute-start(bf16[256,768]{1,0:T(8,128)(2,1)} %slice.646), channel_id=1, source_target_pairs={{0,1},{1,0},{2,3},{3,2},{4,5},{5,4},{6,7},{7,6},{8,9},{9,8},{10,11... | collective-permute-start | bytes 1179656 | tf_op jit(solution)/shard_map/ppermute | solution.py:496
  884.4 248.0 %reduce-scatter.18.cloned.1.call-start = ((), (), s32[]{:S(2)}) async-start(), calls=%async_computation.20 | async-start | bytes 10616832 | tf_op jit(solution)/shard_map/reduce_scatter | solution.py:805
  931.3 10.0 collective-permute-start.22
  941.2 252.1 %reduce-scatter.26.cloned.1.call-start = ((), (), s32[]{:S(2)}) async-start(), calls=%async_computation.25 | async-start | bytes 1105920 | tf_op jit(solution)/shard_map/reduce_scatter | solution.py:866
  1079.0 35.8 %collective-permute-start.23 = (bf16[512,768]{1,0:T(8,128)(2,1)}, bf16[512,768]{1,0:T(8,128)(2,1)}, u32[]{:S(2)}, u32[]{:S(2)}) collective-permute-start(bf16[512,768]{1,0:T(8,128)(2,1)} %slice.644), channel_id=1, source_target_pairs={{0,1},{1,0},{2,3},{3,2},{4,5},{5,4},{6,7},{7,6},{8,9},{9,8},{10,11... | collective-permute-start | bytes 2359304 | tf_op jit(solution)/shard_map/ppermute | solution.py:496
  1081.1 13.2 collective-permute-start.27
  1083.4 29.2 %collective-permute-start.26 = (bf16[192,768]{1,0:T(8,128)(2,1)}, bf16[192,768]{1,0:T(8,128)(2,1)}, u32[]{:S(2)}, u32[]{:S(2)}) collective-permute-start(bf16[192,768]{1,0:T(8,128)(2,1)} %get-tuple-element.391), channel_id=1, source_target_pairs={{0,16},{8,24},{16,0},{24,8},{1,17},{9,25},{17,1},{25,9},{2,18},{10... | collective-permute-start | bytes 884744 | tf_op jit(solution)/shard_map/ppermute | solution.py:106
  1085.5 27.0 %collective-permute-start.25 = (bf16[192,768]{1,0:T(8,128)(2,1)S(1)}, bf16[192,768]{1,0:T(8,128)(2,1)}, u32[]{:S(2)}, u32[]{:S(2)}) collective-permute-start(bf16[192,768]{1,0:T(8,128)(2,1)S(1)} %get-tuple-element.389), channel_id=1, source_target_pairs={{0,8},{8,16},{16,24},{24,0},{1,9},{9,17},{17,25},{25,1},{2,10},{10... | collective-permute-start | bytes 884744 | tf_op jit(solution)/shard_map/ppermute | solution.py:106
  1147.2 89.4 %all-gather.20.cloned.1.call-start = ((), (), s32[]{:S(2)}) async-start(), calls=%async_computation.24 | async-start | bytes 1966080 | tf_op jit(solution)/shard_map/all_gather | solution.py:861
  1165.7 134.1 %reduce-scatter.22.cloned.1.call-start = ((), (), s32[]{:S(2)}) async-start(), calls=%async_computation.22 | async-start | bytes 9289728 | tf_op jit(solution)/shard_map/reduce_scatter | solution.py:805
  1190.9 177.1 %reduce-scatter.24.cloned.1.call-start = ((), (), s32[]{:S(2)}) async-start(), calls=%async_computation.23 | async-start | bytes 10616832 | tf_op jit(solution)/shard_map/reduce_scatter | solution.py:805
  1191.7 210.4 %all-gather.30.cloned.1.call-start = ((), (), s32[]{:S(2)}) async-start(), calls=%async_computation.30 | async-start | bytes 2875392 | tf_op jit(solution)/shard_map/all_gather | solution.py:940
  1192.2 6.1 collective-permute-start.45
  1193.4 8.1 collective-permute-start.43
  1198.2 12.9 collective-permute-start.46
  1202.4 10.1 collective-permute-start.44
  1215.7 57.2 %collective-permute-start.37 = (bf16[96,6656]{1,0:T(8,128)(2,1)S(1)}, bf16[96,6656]{1,0:T(8,128)(2,1)}, u32[]{:S(2)}, u32[]{:S(2)}) collective-permute-start(bf16[96,6656]{1,0:T(8,128)(2,1)S(1)} %get-tuple-element.376), channel_id=1, source_target_pairs={{0,4},{4,0},{1,5},{5,1},{2,6},{6,2},{3,7},{7,3},{8,12},{12,8},{9,1... | collective-permute-start | bytes 3833864 | tf_op jit(solution)/shard_map/ppermute | solution.py:106
  1263.7 16.1 %collective-permute-start.33 = (bf16[192,768]{1,0:T(8,128)(2,1)}, bf16[192,768]{1,0:T(8,128)(2,1)}, u32[]{:S(2)}, u32[]{:S(2)}) collective-permute-start(bf16[192,768]{1,0:T(8,128)(2,1)} %get-tuple-element.387), channel_id=1, source_target_pairs={{0,24},{8,0},{16,8},{24,16},{1,25},{9,1},{17,9},{25,17},{2,26},{10... | collective-permute-start | bytes 884744 | tf_op jit(solution)/shard_map/ppermute | solution.py:106
  1266.2 23.5 %collective-permute-start.32 = (bf16[192,768]{1,0:T(8,128)(2,1)}, bf16[192,768]{1,0:T(8,128)(2,1)}, u32[]{:S(2)}, u32[]{:S(2)}) collective-permute-start(bf16[192,768]{1,0:T(8,128)(2,1)} %get-tuple-element.388), channel_id=1, source_target_pairs={{0,16},{8,24},{16,0},{24,8},{1,17},{9,25},{17,1},{25,9},{2,18},{10... | collective-permute-start | bytes 884744 | tf_op jit(solution)/shard_map/ppermute | solution.py:106
  1266.2 23.5 %collective-permute-start.31 = (bf16[192,768]{1,0:T(8,128)(2,1)}, bf16[192,768]{1,0:T(8,128)(2,1)}, u32[]{:S(2)}, u32[]{:S(2)}) collective-permute-start(bf16[192,768]{1,0:T(8,128)(2,1)} %get-tuple-element.386), channel_id=1, source_target_pairs={{0,8},{8,16},{16,24},{24,0},{1,9},{9,17},{17,25},{25,1},{2,10},{10... | collective-permute-start | bytes 884744 | tf_op jit(solution)/shard_map/ppermute | solution.py:106
  1295.7 78.9 %all-to-all-start.3 = ((bf16[4,192,192]{2,1,0:T(8,128)(2,1)}), bf16[4,192,192]{2,1,0:T(8,128)(2,1)}, u32[]{:S(2)}, u32[]{:S(2)}) async-start(bf16[4,192,192]{2,1,0:T(8,128)(2,1)} %copy.588), calls=%async_computation.10 | async-start | bytes 786432 | tf_op jit(solution)/shard_map/all_to_all | solution.py:809
  1302.1 71.4 %collective-permute-start.30 = (bf16[168,768]{1,0:T(8,128)(2,1)}, bf16[168,768]{1,0:T(8,128)(2,1)}, u32[]{:S(2)}, u32[]{:S(2)}) collective-permute-start(bf16[168,768]{1,0:T(8,128)(2,1)} %get-tuple-element.393), channel_id=1, source_target_pairs={{0,24},{8,0},{16,8},{24,16},{1,25},{9,1},{17,9},{25,17},{2,26},{10... | collective-permute-start | bytes 774152 | tf_op jit(solution)/shard_map/ppermute | solution.py:106
  1307.9 68.5 %collective-permute-start.29 = (bf16[168,768]{1,0:T(8,128)(2,1)}, bf16[168,768]{1,0:T(8,128)(2,1)}, u32[]{:S(2)}, u32[]{:S(2)}) collective-permute-start(bf16[168,768]{1,0:T(8,128)(2,1)} %get-tuple-element.394), channel_id=1, source_target_pairs={{0,16},{8,24},{16,0},{24,8},{1,17},{9,25},{17,1},{25,9},{2,18},{10... | collective-permute-start | bytes 774152 | tf_op jit(solution)/shard_map/ppermute | solution.py:106
  1311.1 65.3 %collective-permute-start.28 = (bf16[168,768]{1,0:T(8,128)(2,1)}, bf16[168,768]{1,0:T(8,128)(2,1)}, u32[]{:S(2)}, u32[]{:S(2)}) collective-permute-start(bf16[168,768]{1,0:T(8,128)(2,1)} %get-tuple-element.392), channel_id=1, source_target_pairs={{0,8},{8,16},{16,24},{24,0},{1,9},{9,17},{17,25},{25,1},{2,10},{10... | collective-permute-start | bytes 774152 | tf_op jit(solution)/shard_map/ppermute | solution.py:106
  1370.1 16.5 %collective-permute-start.36 = (bf16[192,768]{1,0:T(8,128)(2,1)}, bf16[192,768]{1,0:T(8,128)(2,1)}, u32[]{:S(2)}, u32[]{:S(2)}) collective-permute-start(bf16[192,768]{1,0:T(8,128)(2,1)} %get-tuple-element.384), channel_id=1, source_target_pairs={{0,24},{8,0},{16,8},{24,16},{1,25},{9,1},{17,9},{25,17},{2,26},{10... | collective-permute-start | bytes 884744 | tf_op jit(solution)/shard_map/ppermute | solution.py:106
  1373.5 25.5 %collective-permute-start.35 = (bf16[192,768]{1,0:T(8,128)(2,1)}, bf16[192,768]{1,0:T(8,128)(2,1)}, u32[]{:S(2)}, u32[]{:S(2)}) collective-permute-start(bf16[192,768]{1,0:T(8,128)(2,1)} %get-tuple-element.385), channel_id=1, source_target_pairs={{0,16},{8,24},{16,0},{24,8},{1,17},{9,25},{17,1},{25,9},{2,18},{10... | collective-permute-start | bytes 884744 | tf_op jit(solution)/shard_map/ppermute | solution.py:106
  1373.5 25.5 %collective-permute-start.34 = (bf16[192,768]{1,0:T(8,128)(2,1)}, bf16[192,768]{1,0:T(8,128)(2,1)}, u32[]{:S(2)}, u32[]{:S(2)}) collective-permute-start(bf16[192,768]{1,0:T(8,128)(2,1)} %get-tuple-element.383), channel_id=1, source_target_pairs={{0,8},{8,16},{16,24},{24,0},{1,9},{9,17},{17,25},{25,1},{2,10},{10... | collective-permute-start | bytes 884744 | tf_op jit(solution)/shard_map/ppermute | solution.py:106
  1382.3 25.3 %all-to-all-start.2 = ((bf16[4,168,192]{2,1,0:T(8,128)(2,1)}), bf16[4,168,192]{2,1,0:T(8,128)(2,1)}, u32[]{:S(2)}, u32[]{:S(2)}) async-start(bf16[4,168,192]{2,1,0:T(8,128)(2,1)} %copy.587), calls=%async_computation.9 | async-start | bytes 688128 | tf_op jit(solution)/shard_map/all_to_all | solution.py:809
  1418.0 3.5 collective-permute-start.38
  1421.6 4.4 collective-permute-start.39
  (328 other events, 3195.3 us)
Sparse Core Ops, SparseCore 0:
  91.1 33.2 reduce-scatter.9
  1165.8 17.6 all-gather.19
  1213.4 63.7 all-gather.29
Sparse Core Ops, SparseCore 1:
  93.9 53.1 all-gather.23
  149.4 63.9 all-gather.25
  215.1 74.1 all-gather.21
  291.2 59.0 all-gather.27
  351.8 179.5 all-gather.15
  533.9 30.8 all-gather.17
  708.2 46.1 reduce-scatter.11
  756.6 173.7 reduce-scatter.13
  933.7 77.2 reduce-scatter.15
  1014.3 38.3 reduce-scatter.19
  1056.1 76.2 reduce-scatter.17
  1147.3 36.9 reduce-scatter.25
  1191.0 97.1 reduce-scatter.21
  1291.7 76.3 reduce-scatter.23

commit v2 on v1

--- a/solution.py
+++ b/solution.py
@@ -129,6 +129,10 @@
 def exchanged_sum(values, axes):
     for axis in axes:
         count = lax.axis_size(axis)
+        if count == 4:
+            at = sent_to_all(values, axis)
+            values = (at[0] + at[2]) + (at[1] + at[3])
+            continue
         bit = 1
         while bit < count:
             values = values + lax.ppermute(values, axis, [(i, i ^ bit) for i in range(count)])
@@ -301,7 +305,7 @@
 
 def grads_kernel(
     blocks, rows, teach, token_share, final_ref, flipped_ref, bias_ref, target_ref, level_ref,
-    weight_ref, table_ref, final_grad_ref, table_grad_ref, low_ref,
+    weight_ref, table_ref, final_low_ref, table_grad_ref, low_ref, final_grad_ref,
 ):
     chunk = table_ref.shape[1]
     start = pl.program_id(0) * chunk
@@ -331,6 +335,10 @@
     table_grad_ref[...] = to_low(
         jnp.dot(flipped_ref[...], low_ref[...], preferred_element_type=jnp.float32)
     )
+
+    @pl.when(pl.program_id(0) == pl.num_programs(0) - 1)
+    def _():
+        final_low_ref[...] = to_low(final_grad_ref[...])
 
 
 def loss_grads(final_all, table, bias_row, targets, levels, weights, blocks, token_share):
@@ -354,10 +362,13 @@
         ],
         out_specs=[pl.BlockSpec((count, D), whole), pl.BlockSpec((D, CHUNK), by_chunk)],
         out_shape=[
-            jax.ShapeDtypeStruct((count, D), jnp.float32),
+            jax.ShapeDtypeStruct((count, D), jnp.bfloat16),
             jax.ShapeDtypeStruct((D, width), jnp.bfloat16),
         ],
-        scratch_shapes=[pltpu.VMEM((count, CHUNK), jnp.bfloat16)],
+        scratch_shapes=[
+            pltpu.VMEM((count, CHUNK), jnp.bfloat16),
+            pltpu.VMEM((count, D), jnp.float32),
+        ],
         compiler_params=pltpu.CompilerParams(
             vmem_limit_bytes=VMEM_LIMIT, dimension_semantics=("arbitrary",)
         ),
@@ -400,6 +411,7 @@
 
 def scatter_kernel(place_ref, grad_ref, out_ref, *sum_refs):
     streams = len(sum_refs)
+    width = grad_ref.shape[1]
     for sum_ref in sum_refs:
         sum_ref[...] = jnp.zeros(sum_ref.shape, jnp.float32)
     run = grad_ref.shape[0] // streams
@@ -408,33 +420,41 @@
         for at in range(4):
             for stream, sum_ref in enumerate(sum_refs):
                 row = stream * run + group * 4 + at
-                sum_ref[pl.ds(place_ref[row], 1), :] += grad_ref[pl.ds(row, 1), :]
+                sum_ref[pl.ds(place_ref[row], 1), :width] += grad_ref[pl.ds(row, 1), :]
         return carry
 
     lax.fori_loop(0, run // 4, some, 0)
-    total = sum_refs[0][: out_ref.shape[0], :]
-    for sum_ref in sum_refs[1:]:
-        total = total + sum_ref[: out_ref.shape[0], :]
-    out_ref[...] = total
+
+    def turn(block, carry):
+        span = pl.ds(pl.multiple_of(block * LANES, LANES), LANES)
+        total = sum_refs[0][span, :]
+        for sum_ref in sum_refs[1:]:
+            total = total + sum_ref[span, :]
+        out_ref[:, span] = total.T[:width]
+        return carry
+
+    lax.fori_loop(0, out_ref.shape[1] // LANES, turn, 0)
 
 
 def scatter_add(places, grads, height):
     count, width = grads.shape
-    return pl.pallas_call(
+    padded = (height // LANES + 1) * LANES
+    out = pl.pallas_call(
         scatter_kernel,
-        out_shape=jax.ShapeDtypeStruct((height, width), jnp.float32),
+        out_shape=jax.ShapeDtypeStruct((width, padded), jnp.float32),
         in_specs=[
             pl.BlockSpec(memory_space=pltpu.SMEM),
             pl.BlockSpec(memory_space=pltpu.VMEM),
         ],
         out_specs=pl.BlockSpec(memory_space=pltpu.VMEM),
-        scratch_shapes=[pltpu.VMEM((height + 8, width), jnp.float32)] * 4,
+        scratch_shapes=[pltpu.VMEM((padded, LANES), jnp.float32)] * 4,
         compiler_params=pltpu.CompilerParams(vmem_limit_bytes=VMEM_LIMIT),
         cost_estimate=pl.CostEstimate(
             flops=count * width, bytes_accessed=90_000_000, transcendentals=0
         ),
         name="scatter_add",
     )(places, grads)
+    return out[:, :height]
 
 
 def local(
@@ -569,9 +589,7 @@
     table_held = table_held.reshape(ctx_count * thick, vocab_part)
 
     held_of[0], dec_ids = together(held_of[0], dec_ids)
-    full = plane_full(held_of[0])
-    conv_full = full[:, :, :, : KW * piece].transpose(2, 0, 1, 3, 4).reshape(KW, D, D)
-    unpack(groups[0], full)
+    first_full = plane_full(held_of[0])
     ids_plane = spread(jnp.stack([dec_ids, targets]), "ctx")
     ids_all = spread(in_blocks(ids_plane[:, 0]), "fsdp").reshape(
         fsdp_count, ctx_count, tp_count, dec_rows
@@ -596,8 +614,8 @@
         ],
         axis=2,
     )
-    packed, held_of[2] = together(packed, held_of[2])
-    unpack(groups[2], plane_full(held_of[2]))
+    packed, held_of[1] = together(packed, held_of[1])
+    unpack(groups[1], plane_full(held_of[1]))
     packed = in_blocks(spread(packed, "ctx"))
     top_count = teach_probs.shape[2]
     taught = (
@@ -668,8 +686,17 @@
     frame_pairs = jnp.pad(clip_mel.reshape(-1, 2 * MEL), ((1, 1), (0, 0)))
     near = lax.dynamic_slice_in_dim(frame_pairs, part_index * enc_rows, enc_rows + 2, 0)
     evens, odds = near[:, :MEL], near[:, MEL:]
-    evens, odds, held_of[1] = together(evens, odds, held_of[1])
-    unpack(groups[1], plane_full(held_of[1]))
+    evens, odds, held_of[2], held_of[3], table_held, first_full = together(
+        evens, odds, held_of[2], held_of[3], table_held, first_full
+    )
+    rest_full = plane_full(jnp.concatenate(held_of[2:], axis=1))
+    offset = 0
+    for group, held in zip(groups[2:], held_of[2:]):
+        unpack(group, rest_full[:, :, :, offset : offset + held.shape[1]])
+        offset += held.shape[1]
+    table_block = lax.all_gather(table_held, "fsdp", axis=0, tiled=True)
+    conv_full = first_full[:, :, :, : KW * piece].transpose(2, 0, 1, 3, 4).reshape(KW, D, D)
+    unpack(groups[0], first_full)
     taps_even = jnp.concatenate([odds[:-2], evens[1:-1], odds[1:-1]], axis=1)
     taps_odd = jnp.concatenate([evens[:-1], odds[:-1], evens[1:]], axis=1)
 
@@ -682,18 +709,13 @@
     )[:, None]
     first_even = to_low(gelu_exact(pre_even))
     first_odd = to_low(jnp.where(odd_open, gelu_exact(pre_odd), 0.0))
-    first_even, first_odd, held_of[3], teach_weight = together(
-        first_even, first_odd, held_of[3], teach_weight
-    )
-    unpack(groups[3], plane_full(held_of[3]))
+    first_even, first_odd, teach_weight = together(first_even, first_odd, teach_weight)
     taps_two = (first_odd[:-1], first_even, first_odd[1:])
     second_pre = small_params[15]
     for tap in range(KW):
         second_pre = second_pre + product("ji,oi->jo", taps_two[tap], conv_full[tap])
     stream_zero = gelu_exact(second_pre) + sinusoid(part_index * enc_rows, enc_rows, D)
     enc_one = to_low(layer_norm(stream_zero, small_params[0], small_params[1]))
-    enc_one, table_held = together(enc_one, table_held)
-    table_block = lax.all_gather(table_held, "fsdp", axis=0, tiled=True)
     enc_one_clip = spread_rows(enc_one)
     enc_weights = (narrow_full[0], narrow_full[1], narrow_full[2], narrow_full[9])
     attn_out, enc_saved = attention_forward(
@@ -776,9 +798,7 @@
     final_grad, table_grad = loss_grads(
         final_all, table_block, bias_row, target_local, levels, teach_weight, blocks, token_share
     )
-    grad_final_moved = lax.psum_scatter(
-        to_low(final_grad), PLANE, scatter_dimension=0, tiled=True
-    )
+    grad_final_moved = lax.psum_scatter(final_grad, PLANE, scatter_dimension=0, tiled=True)
     grad_final = product("np,nd->pd", moved_own, grad_final_moved)
 
     table_sum = lax.psum_scatter(table_grad, "fsdp", scatter_dimension=0, tiled=True)
@@ -826,9 +846,7 @@
     feed_grad_2, feed_grad_3, dec_bias_in, back = feed_backward(
         dec_three, feed_full[2], feed_full[3], dec_feed_saved, grad_feed
     )
-    held_dec_feed = packed_grads([cut_feed(feed_grad_2), cut_feed(feed_grad_3)])
-    back, held_dec_feed = together(back, held_dec_feed)
-    part_dec_feed = plane_sum(held_dec_feed)
+    back, feed_grad_2, feed_grad_3 = together(back, to_low(feed_grad_2), to_low(feed_grad_3))
     back, row_grads[10], row_grads[11] = norm_back(
         tokens_two, small_params[10], small_params[11], back
     )
@@ -847,7 +865,10 @@
     self_grads, row_grads[20], row_grads[21], back_q, back_k = attention_backward(
         dec_one, dec_one_clip, self_weights, self_saved, grad_self, key_place, query_place
     )
-    held_dec_attn = packed_grads([cut_narrow(grad, piece) for grad in self_grads + cross_grads])
+    held_dec = packed_grads(
+        [cut_narrow(grad, piece) for grad in self_grads + cross_grads]
+        + [cut_feed(feed_grad_2), cut_feed(feed_grad_3)]
+    )
     back, row_grads[6], row_grads[7] = norm_back(
         tokens_zero, small_params[6], small_params[7], back_q + collect_rows(back_k)
     )
@@ -861,14 +882,8 @@
     sent = lax.all_gather(sent, "tp", axis=0).reshape(-1, thick).astype(jnp.float32)
     embed_grad = scatter_add(jnp.where(ids_inside, ids_local, vocab_local), sent, vocab_local)
 
-    def small_plane_sum(rows):
-        rows = jnp.pad(rows, ((0, -rows.shape[0] % (8 * blocks)), (0, 0)))
-        return lax.psum_scatter(rows, PLANE, scatter_dimension=0, tiled=True)
-
-    position_part = small_plane_sum(position_rows)
-
-    back_encoded, held_dec_attn, table_sum = together(back_encoded, held_dec_attn, table_sum)
-    part_dec_attn = plane_sum(held_dec_attn)
+    back_encoded, held_dec = together(back_encoded, held_dec)
+    part_dec = plane_sum(held_dec)
     back_encoded_own = collect_rows(back_encoded)
     grad_stream_two, row_grads[4], row_grads[5] = norm_back(
         stream_two, small_params[4], small_params[5], back_encoded_own
@@ -878,16 +893,13 @@
     feed_grad_0, feed_grad_1, enc_bias_in, back = feed_backward(
         enc_two, feed_full[0], feed_full[1], enc_feed_saved, grad_feed
     )
-    held_enc_feed = packed_grads([cut_feed(feed_grad_0), cut_feed(feed_grad_1)])
     back, row_grads[2], row_grads[3] = norm_back(
         stream_one, small_params[2], small_params[3], back
     )
     grad_stream_one = grad_stream_two + back
-    grad_stream_one, part_dec_feed, held_enc_feed = together(
-        grad_stream_one, part_dec_feed, held_enc_feed
-    )
-    part_enc_feed = plane_sum(held_enc_feed)
-    sum_dec_feed = sum_to_owner(part_dec_feed, "fsdp")
+    grad_stream_one, feed_grad_0, feed_grad_1, table_sum = together(
+        grad_stream_one, to_low(feed_grad_0), to_low(feed_grad_1), table_sum
+    )
     grad_attn = to_low(grad_stream_one)
     row_grads[18] = jnp.sum(grad_attn, axis=0, dtype=jnp.float32)
     enc_grads, row_grads[16], row_grads[17], back_q, back_k = attention_backward(
@@ -897,11 +909,13 @@
         stream_zero, small_params[0], small_params[1], back_q + collect_rows(back_k)
     )
     grad_stream_zero = grad_stream_one + back
-    grad_stream_zero, part_dec_attn, position_part, sum_dec_feed = together(
-        grad_stream_zero, part_dec_attn, position_part, sum_dec_feed
-    )
-    sum_dec_attn = sum_to_owner(part_dec_attn, "fsdp")
-    position_part = exchanged_sum(position_part, ("fsdp",))
+    enc_cuts = [cut_narrow(grad, piece) for grad in enc_grads] + [
+        cut_feed(feed_grad_0),
+        cut_feed(feed_grad_1),
+    ]
+    grad_stream_zero, enc_cuts = together(grad_stream_zero, enc_cuts)
+    sum_dec = sum_to_owner(part_dec, "fsdp")
+    dec_list = own_columns(sum_dec[: 8 * piece], (piece,) * 8)
     table_sum = table_sum.reshape(ctx_count, thick, vocab_part)
     table_sum = in_order(
         sent_to_owners(lambda step: pick(table_sum, lax.rem(ctx_index + step, ctx_count)), "ctx"),
@@ -911,12 +925,11 @@
     grad_second = to_low(gelu_back(second_pre, grad_stream_zero))
     row_grads[15] = jnp.sum(grad_second, axis=0, dtype=jnp.float32)
     conv_grads = [product("jo,ji->oi", grad_second, taps_two[tap]) for tap in range(KW)]
-    held_enc_attn = packed_grads(
-        [cut_narrow(jnp.concatenate(conv_grads, axis=0), KW * piece)]
-        + [cut_narrow(grad, piece) for grad in enc_grads]
-    )
-    sum_enc_attn = sum_to_owner(plane_sum(held_enc_attn), "fsdp")
-    sum_enc_feed = sum_to_owner(part_enc_feed, "fsdp")
+    part_enc = plane_sum(
+        packed_grads(
+            enc_cuts + [cut_narrow(jnp.concatenate(conv_grads, axis=0), KW * piece)]
+        )
+    )
     grad_taps = [product("jo,oi->ji", grad_second, conv_full[tap]) for tap in range(KW)]
     grad_odd = jnp.pad(grad_taps[0], ((0, 1), (0, 0))) + jnp.pad(grad_taps[2], ((1, 0), (0, 0)))
     grad_pre_even = to_low(gelu_back(pre_even, grad_taps[1]))
@@ -936,33 +949,38 @@
             kernel_rows,
         ]
     )
-    vector_part = exchanged_sum(small_plane_sum(vector_rows), ("fsdp",))
-    all_small = lax.all_gather(jnp.concatenate([vector_part, position_part]), PLANE, axis=0)
-    split = vector_part.shape[0]
-    small_grad = jnp.concatenate(
-        [
-            all_small[:, :split].reshape(-1, D)[: vector_rows.shape[0]],
-            all_small[:, split:].reshape(-1, D)[: position_rows.shape[0]],
-        ]
-    )
-
-    (embed_flat,) = together(embed_grad.T)
-    shard_table = table_sum.astype(jnp.float32) + embed_flat
-    dec_list = own_columns(sum_dec_attn, (piece,) * 8)
-    enc_list = own_columns(sum_enc_attn, (KW * piece,) + (piece,) * 4)
-    shard_conv = enc_list[0]
-    shard_proj = jnp.stack(enc_list[1:4] + dec_list[0:3] + dec_list[4:7])
-    shard_out = jnp.stack([enc_list[4], dec_list[3], dec_list[7]])
-    shard_feed = jnp.concatenate([sum_enc_feed, sum_dec_feed]).reshape(4, thick, D)
+    small_rows = jnp.concatenate([vector_rows, position_rows])
+    small_count = small_rows.shape[0]
+    small_rows = jnp.pad(small_rows, ((0, -small_count % (8 * blocks)), (0, 0)))
+    small_rows, part_enc, sum_dec, dec_list, table_sum, embed_grad = together(
+        small_rows, part_enc, sum_dec, dec_list, table_sum, embed_grad
+    )
+    small_part = lax.psum_scatter(small_rows, PLANE, scatter_dimension=0, tiled=True)
+    small_part = exchanged_sum(small_part, ("fsdp",))
+    small_grad = lax.all_gather(small_part, PLANE, axis=0, tiled=True)[:small_count]
+    sum_enc = sum_to_owner(part_enc, "fsdp")
+    enc_feed_end = 4 * piece + 2 * thick
+    enc_list = own_columns(
+        jnp.concatenate([sum_enc[: 4 * piece], sum_enc[enc_feed_end:]]),
+        (piece,) * 4 + (KW * piece,),
+    )
+    shard_conv = enc_list[4]
+
+    shard_table = table_sum.astype(jnp.float32) + embed_grad
+    shard_proj = jnp.stack(enc_list[0:3] + dec_list[0:3] + dec_list[4:7])
+    shard_out = jnp.stack([enc_list[3], dec_list[3], dec_list[7]])
+    shard_feed = jnp.concatenate([sum_enc[4 * piece : enc_feed_end], sum_dec[8 * piece :]])
+    shard_feed = shard_feed.reshape(4, thick, D)
     local_squares = (
         jnp.sum(shard_proj * shard_proj)
         + jnp.sum(shard_out * shard_out)
         + jnp.sum(shard_feed * shard_feed)
         + jnp.sum(shard_conv * shard_conv)
         + jnp.sum(shard_table * shard_table)
-    )
-    loss_value, big_squares = exchanged_sum(jnp.stack([loss_term, local_squares]), ALL)
-    grad_norm = jnp.sqrt(big_squares + jnp.sum(small_grad * small_grad))
+        + jnp.sum(small_part * small_part) / fsdp_count
+    )
+    loss_value, squares = exchanged_sum(jnp.stack([loss_term, local_squares]), ALL)
+    grad_norm = jnp.sqrt(squares)
     factor = jnp.minimum(1.0, CLIP_NORM / (grad_norm + 1e-06))
     results = [
         nesterov(projections, shard_proj, moment_projections, average_projections, factor),

time: 1510 us -> 1360 us (0.901)
  waiting for transfers between devices: 390 us -> 283 us
  local copies, waits for them, and re-layouts: 314 us -> 285 us
  other arithmetic: 179 us -> 151 us
  blocking collectives: 41.9 us -> 24.3 us
  starting transfers between devices: 94 us -> 111 us
    reduce_scatter x4 -> x2, waiting for transfers between devices: 66.2 us -> 19 us  [plane_sum(): return lax.psum_scatter(held, PLANE, scatter_dimension=0, tiled=False)]
    ppermute x17 -> x26, starting transfers between devices: 32 us -> 74 us  [sent_to_all(): lax.ppermute(values, axis, shifted(axis, step))]
    reduce_scatter x1, waiting for transfers between devices: 28.2 us -> 0.01 us  [local(): lax.psum_scatter(table_grad, 'fsdp', scatter_dimension=0, tiled=True)]
    all_gather x1, waiting for transfers between devices: 61.8 us -> 35.3 us  [local(): table_block = lax.all_gather(table_held, 'fsdp', axis=0, tiled=True)]
    ppermute x9 -> x1, waiting for transfers between devices: 21.9 us -> 2.01 us  [exchanged_sum(): lax.ppermute(values, axis, [(i, i ^ bit) for i in range(count)])]
    reshape x8 -> x4, local copies, waits for them, and re-layouts: 56.9 us -> 39.3 us  [cut_feed(): return to_low(grad).reshape(fsdp_count, ctx_count, thick, tp_count, D).tr...]
    all_to_all x1 -> x0, blocking collectives: 17.5 us -> none  [local(): sent = lax.all_to_all(sent, ('fsdp', 'ctx'), 0, 0, tiled=True)]
    unnamed x696 -> x688, local copies, waits for them, and re-layouts: 97.7 us -> 83.8 us
  transfers between devices with their start and end apart: 67 -> 59, of which waited for: 29 -> 29; matrix products, arithmetic and copies ran while one was open for 43% -> 50% of each run, Pallas kernels for 1% -> 3%
where the time goes in v2:
time: 1360 us; the launch traced here: 1350 us
  matrix products  303 us (22%)
  local copies, waits for them, and re-layouts  285 us (21%)
  waiting for transfers between devices  283 us (21%)
  Pallas kernels  166 us (12%)
  other arithmetic  151 us (11%)
  starting transfers between devices  111 us (8%)
  between operations  28.9 us (2%)
  blocking collectives  24.3 us (2%)
    dot_general x82, matrix products, product(): return jnp.einsum(pattern, left, right, preferred_element_type=jnp.float32)  303 us
    unnamed x688, local copies, waits for them, and re-layouts  83.8 us
    pallas_call x1, Pallas kernels, loss_grads(): pl.pallas_call(functools.partial(grads_kernel, blocks, rows, teach, token...  83.5 us
    ppermute x26, starting transfers between devices, sent_to_all(): lax.ppermute(values, axis, shifted(axis, step))  74 us
    ppermute x26, waiting for transfers between devices, sent_to_all(): lax.ppermute(values, axis, shifted(axis, step))  63.8 us
    ppermute x8, waiting for transfers between devices, sent_to_owners(): lax.ppermute(pieces_for(step), axis, shifted(axis, step))  63.6 us
    reduce_scatter x1, waiting for transfers between devices, local(): lax.psum_scatter(final_grad, PLANE, scatter_dimension=0, tiled=True)  44.6 us
    reshape x4, local copies, waits for them, and re-layouts, cut_feed(): return to_low(grad).reshape(fsdp_count, ctx_count, thick, tp_count, D).tr...  39.3 us
  transfers between devices with their start and end apart: 59, of which 29 were waited for; matrix products, arithmetic and copies ran while one was open for 50% of the time, Pallas kernels for 3%

profile of v2, /device:TPU:0, one launch (start us, length us, event | category | flops | bytes accessed | tf_op | source)
XLA Modules:
  0.0 1351.7 jit_solution(3036506465836899646)
XLA Ops:
  10.7 15.2 %all_to_all.25 = bf16[4,15,24,192]{3,2,1,0:T(8,128)(2,1)S(1)} all-to-all(bf16[4,15,24,192]{3,2,1,0:T(8,128)(2,1)S(1)} %copy.568), channel_id=1, replica_groups=mesh['fsdp'=4,'ctx'=2,'tp'=4] {'tp'}, dimensions={0} | all-to-all | bytes 1105920 | tf_op jit(solution)/shard_map/all_to_all | solution.py:535
  33.1 5.4 collective-permute-done.4
  38.5 9.8 collective-permute-done.5
  53.8 6.0 collective-permute-start.8
  62.2 6.6 copy.581.table_ref
  69.9 13.8 %lookup.1 = f32[8192,96]{1,0:T(8,128)} custom-call(s32[8192]{0:T(1024)} %get-tuple-element.309.place_ref, f32[12968,96]{1,0:T(8,128)} %copy.581.table_ref), custom_call_target="tpu_custom_call" | custom-call | flops 786432 | bytes 70000000 | tf_op jit(solution)/shard_map/lookup/pallas_call | solution.py:396
  83.7 6.0 select_convert_fusion.2
  99.1 6.3 collective-permute-done
  105.5 10.8 collective-permute-done.1
  118.2 5.9 collective-permute-start.16
  145.1 7.9 collective-permute-start.13
  164.6 9.7 collective-permute-done.14
  175.7 8.0 collective-permute-done.19
  206.3 8.8 fusion.1
  221.4 7.6 copy.693
  235.4 4.9 multiply_convert_fusion.9
  240.5 5.3 select_convert_fusion.4
  248.9 11.6 fusion.174
  278.1 10.4 multiply_reduce_fusion.1
  288.5 11.2 fusion
  302.6 11.9 fusion.72
  317.1 8.0 slice_bitcast_fusion.2
  325.1 6.0 copy.608
  332.5 21.2 %multiply_convert_fusion.3 = (bf16[512,3072]{1,0:T(8,128)(2,1)}, f32[512,3072]{1,0:T(8,128)}, f32[512,3072]{1,0:T(8,128)}) fusion(f32[3072]{0:T(1024)S(1)} %copy-done.228, bf16[768,3072]{1,0:T(8,128)(2,1)S(1)} %bitcast.641, f32[512,768]{1,0:T(8,128)S(1)} %copy-done.22, f32[768]{0:T(1024)S(1)} %get-tuple-element.139, f32[768]{0:T(1024)S(1)} %get-tuple-element.140, ...), kind=kOutput, calls=%fused_computation.40 | convolution fusion | flops 2521694208 | bytes 22042624 | tf_op jit(solution)/shard_map/qd,df->qf/dot_general | solution.py:36
  363.9 6.2 slice_bitcast_fusion.6
  403.1 6.8 slice_bitcast_fusion
  409.9 6.0 copy.615
  440.7 11.1 multiply_convert_fusion.6
  454.4 35.3 %all-gather.13.cloned.1.call-done.table_ref = bf16[768,6656]{1,0:T(8,128)(2,1)} async-done(((bf16[192,6656]{1,0:T(8,128)(2,1)}), bf16[768,6656]{1,0:T(8,128)(2,1)}) %all-gather.13.cloned.1.call-update) | async-done | bytes 10223632 | tf_op jit(solution)/shard_map/all_gather | solution.py:697
  497.3 26.0 %all-gather.15.cloned.1.call-done = bf16[2048,768]{0,1:T(8,128)(2,1)} async-done(((bf16[256,768]{0,1:T(8,128)(2,1)}), bf16[2048,768]{0,1:T(8,128)(2,1)}) %all-gather.15.cloned.1.call-update) | async-done | bytes 3145744 | tf_op jit(solution)/shard_map/all_gather | solution.py:781
  523.3 4.8 copy.622.final_ref
  528.1 36.5 %loss_stats.1 = (f32[2048,128]{1,0:T(8,128)}, f32[2048,128]{1,0:T(8,128)}, f32[2048,128]{1,0:T(8,128)}, f32[64,128]{1,0:T(8,128)}) custom-call(bf16[2048,768]{1,0:T(8,128)(2,1)} %copy.622.final_ref, f32[1,6656]{1,0:T(1,128)} %broadcast_in_dim.320.bias_ref, s32[2048,1]{1,0:T(8,128)} %bitcast_select_fusion.target_ref, bf16[52,512,128]{2,1,0:T(8,128)(2,1)} %bitcast.627, ...), custom_call_target="tpu_custom_call" | custom-call | flops 20937965568 | bytes 17039360 | tf_op jit(solution)/shard_map/loss_stats/pallas_call | solution.py:272
  568.4 9.2 all-gather.4
  579.8 83.5 %loss_grads.1 = (bf16[2048,768]{1,0:T(8,128)(2,1)}, bf16[768,6656]{1,0:T(8,128)(2,1)}) custom-call(bf16[2048,768]{1,0:T(8,128)(2,1)} %copy.622.final_ref, bf16[768,2048]{1,0:T(8,128)(2,1)} %bitcast.681, f32[1,6656]{1,0:T(1,128)} %broadcast_in_dim.320.bias_ref, s32[2048,1]{1,0:T(8,128)} %bitcast_select_fusion.target_ref, f32[2048,1]{1,0:T(8,128)} %copy.625.level_ref, ...), custom_call_target="tpu_custom_call" | custom-call | flops 62813896704 | bytes 33554432 | tf_op jit(solution)/shard_map/loss_grads/pallas_call | solution.py:351
  665.1 44.6 %reduce-scatter.9.cloned.1.call-done = bf16[256,768]{1,0:T(8,128)(2,1)} async-done(((bf16[2048,768]{1,0:T(8,128)(2,1)}), bf16[256,768]{1,0:T(8,128)(2,1)}) %reduce-scatter.9.cloned.1.call-update) | async-done | bytes 393232 | tf_op jit(solution)/shard_map/reduce_scatter | solution.py:801
  717.3 6.1 convert_reduce_fusion.1
  731.3 11.8 multiply_reduce_fusion.2
  744.6 6.5 multiply_convert_fusion.1
  794.9 5.6 all-to-all-start.3
  809.3 14.6 %all-to-all-done.3 = bf16[8,256,96]{1,2,0:T(8,128)(2,1)S(1)} async-done(((bf16[8,256,96]{1,2,0:T(8,128)(2,1)}), bf16[8,256,96]{1,2,0:T(8,128)(2,1)S(1)}, u32[]{:S(2)}, u32[]{:S(2)}) %all-to-all-start.3) | async-done | bytes 393248 | tf_op jit(solution)/shard_map/all_to_all | solution.py:880
  827.3 9.8 reshape.928
  837.0 9.8 reshape.929
  871.3 9.9 convert_reduce_fusion
  891.6 4.7 convolution_convert_fusion.1
  898.8 24.8 %multiply_reduce_fusion = (f32[12,512]{1,0:T(8,128)S(1)}, f32[12,512,1024]{2,1,0:T(8,128)}) fusion(f32[12,512,1024]{2,1,0:T(8,128)} %get-tuple-element.324, f32[12,512]{1,0:T(8,128)} %log_add_fusion, bf16[512,12,64]{0,2,1:T(8,128)(2,1)S(1)} %bitcast.623, bf16[1024,12,64]{0,2,1:T(8,128)(2,1)S(1)} %bitcast.698), kind=kOutput, calls=%fused_computation.1 | convolution fusion | flops 830466048 | bytes 52740096 | tf_op jit(solution)/shard_map/qhd,khd->hqk/dot_general | solution.py:36
  923.6 18.1 %multiply_convert_fusion = bf16[12,512,1024]{2,1,0:T(8,128)(2,1)S(1)} fusion(f32[12,512,1024]{2,1,0:T(8,128)} %get-tuple-element.347, f32[12,512,1024]{2,1,0:T(8,128)} %get-tuple-element.324, f32[12,512]{1,0:T(8,128)S(1)} %get-tuple-element.346, f32[12,512]{1,0:T(8,128)S(1)} %copy-done.127), kind=kLoop, calls=%fused_computation | loop fusion | flops 31457280 | bytes 62963712 | tf_op jit(solution)/shard_map/convert_element_type | solution.py:32
  947.4 12.7 convert_reduce_fusion.3
  967.0 6.8 convert_reduce_fusion.8
  987.0 9.8 reshape.953
  996.7 10.0 reshape.954
  1006.8 7.6 copy_bitcast_fusion
  1054.6 4.6 copy.649
  1059.2 31.7 %scatter_add.1 = f32[96,13056]{1,0:T(8,128)} custom-call(s32[8192]{0:T(1024)} %get-tuple-element.308.place_ref, f32[8192,96]{1,0:T(8,128)} %bitcast.607), custom_call_target="tpu_custom_call" | custom-call | flops 786432 | bytes 90000000 | tf_op jit(solution)/shard_map/scatter_add/pallas_call | solution.py:442
  1116.5 5.3 concatenate.98
  1125.6 24.4 %collective-permute-done.26 = bf16[384,768]{1,0:T(8,128)(2,1)} collective-permute-done((bf16[384,768]{1,0:T(8,128)(2,1)}, bf16[384,768]{1,0:T(8,128)(2,1)}, u32[]{:S(2)}, u32[]{:S(2)}) %collective-permute-start.26) | collective-permute-done | bytes 589856 | tf_op jit(solution)/shard_map/ppermute | solution.py:106
  1161.2 8.6 all-to-all-done.2
  1171.6 19.0 %reduce-scatter.13.cloned.1.call-done = bf16[1,4,360,768]{3,2,1,0:T(8,128)(2,1)} async-done(((bf16[8,4,360,768]{3,2,1,0:T(8,128)(2,1)}), bf16[1,4,360,768]{3,2,1,0:T(8,128)(2,1)}) %reduce-scatter.13.cloned.1.call-update) | async-done | bytes 2211856 | tf_op jit(solution)/shard_map/reduce_scatter | solution.py:825
  1204.5 6.3 collective-permute-done.29
  1210.8 22.8 %collective-permute-done.30 = bf16[360,768]{1,0:T(8,128)(2,1)} collective-permute-done((bf16[360,768]{1,0:T(8,128)(2,1)}, bf16[360,768]{1,0:T(8,128)(2,1)}, u32[]{:S(2)}, u32[]{:S(2)}) %collective-permute-start.30) | collective-permute-done | bytes 552992 | tf_op jit(solution)/shard_map/ppermute | solution.py:106
  1255.2 11.3 collective-permute-start.32
  1281.2 7.7 collective-permute-done.32
  1292.3 9.2 collective-permute-start.35
  1327.3 8.4 fusion.30
  1335.7 7.5 multiply_add_fusion
  (1192 shorter events, 499.0 us)
Async XLA Ops:
  8.0 178.9 %all-gather.21.cloned.1.call-start = ((), (), s32[]{:S(2)}) async-start(), calls=%async_computation.21 | async-start | bytes 9289728 | tf_op jit(solution)/shard_map/all_gather | solution.py:562
  27.4 11.1 collective-permute-start.4
  29.0 19.3 %collective-permute-start.5 = (bf16[168,768]{1,0:T(8,128)(2,1)S(1)}, bf16[168,768]{1,0:T(8,128)(2,1)S(1)}, u32[]{:S(2)}, u32[]{:S(2)}) collective-permute-start(bf16[168,768]{1,0:T(8,128)(2,1)S(1)} %constant_dynamic-update-slice_fusion), channel_id=1, source_target_pairs={{0,16},{8,24},{16,0},{24,8},{1,17},{9,25},{17,1},{25,9},{2,18},{10... | collective-permute-start | bytes 774152 | tf_op jit(solution)/shard_map/ppermute | solution.py:95
  31.6 16.7 %collective-permute-start.6 = (bf16[168,768]{1,0:T(8,128)(2,1)S(1)}, bf16[168,768]{1,0:T(8,128)(2,1)S(1)}, u32[]{:S(2)}, u32[]{:S(2)}) collective-permute-start(bf16[168,768]{1,0:T(8,128)(2,1)S(1)} %constant_dynamic-update-slice_fusion), channel_id=1, source_target_pairs={{0,24},{8,0},{16,8},{24,16},{1,25},{9,1},{17,9},{25,17},{2,26},{10... | collective-permute-start | bytes 774152 | tf_op jit(solution)/shard_map/ppermute | solution.py:95
  49.3 165.8 %reduce-scatter.7.cloned.1.call-start = ((), (), s32[]{:S(2)}) async-start(), calls=%async_computation.11 | async-start | bytes 1966080 | tf_op jit(solution)/shard_map/reduce_scatter | solution.py:604
  49.4 3.7 collective-permute-start.7
  53.8 15.1 %collective-permute-start.8 = (s32[8,256]{1,0:T(8,128)S(1)}, s32[8,256]{1,0:T(8,128)S(1)}, u32[]{:S(2)}, u32[]{:S(2)}) collective-permute-start(s32[8,256]{1,0:T(8,128)S(1)} %reshape.880), channel_id=1, source_target_pairs={{0,8},{8,16},{16,24},{24,0},{1,9},{9,17},{17,25},{25,1},{2,10},{10... | collective-permute-start | bytes 24584 | tf_op jit(solution)/shard_map/ppermute | solution.py:95
  59.8 9.2 collective-permute-start.9
  61.4 7.6 collective-permute-start.10
  92.2 224.9 %all-gather.25.cloned.1.call-start = ((), (), s32[]{:S(2)}) async-start(), calls=%async_computation.23 | async-start | bytes 10616832 | tf_op jit(solution)/shard_map/all_gather | solution.py:562
  93.6 11.9 collective-permute-start
  94.9 21.4 %collective-permute-start.1 = (bf16[192,768]{1,0:T(8,128)(2,1)S(1)}, bf16[192,768]{1,0:T(8,128)(2,1)S(1)}, u32[]{:S(2)}, u32[]{:S(2)}) collective-permute-start(bf16[192,768]{1,0:T(8,128)(2,1)S(1)} %pad_maximum_fusion.8), channel_id=1, source_target_pairs={{0,16},{8,24},{16,0},{24,8},{1,17},{9,25},{17,1},{25,9},{2,18},{10... | collective-permute-start | bytes 884744 | tf_op jit(solution)/shard_map/ppermute | solution.py:95
  96.9 19.4 %collective-permute-start.2 = (bf16[192,768]{1,0:T(8,128)(2,1)S(1)}, bf16[192,768]{1,0:T(8,128)(2,1)S(1)}, u32[]{:S(2)}, u32[]{:S(2)}) collective-permute-start(bf16[192,768]{1,0:T(8,128)(2,1)S(1)} %pad_maximum_fusion.8), channel_id=1, source_target_pairs={{0,24},{8,0},{16,8},{24,16},{1,25},{9,1},{17,9},{25,17},{2,26},{10... | collective-permute-start | bytes 884744 | tf_op jit(solution)/shard_map/ppermute | solution.py:95
  117.4 246.5 %all-gather.23.cloned.1.call-start = ((), (), s32[]{:S(2)}) async-start(), calls=%async_computation.22 | async-start | bytes 21233664 | tf_op jit(solution)/shard_map/all_gather | solution.py:562
  118.2 21.3 %collective-permute-start.16 = (bf16[192,768]{1,0:T(8,128)(2,1)}, bf16[192,768]{1,0:T(8,128)(2,1)}, u32[]{:S(2)}, u32[]{:S(2)}) collective-permute-start(bf16[192,768]{1,0:T(8,128)(2,1)} %pad_maximum_fusion.9), channel_id=1, source_target_pairs={{0,8},{8,16},{16,24},{24,0},{1,9},{9,17},{17,25},{25,1},{2,10},{10... | collective-permute-start | bytes 884744 | tf_op jit(solution)/shard_map/ppermute | solution.py:95
  124.0 17.3 %collective-permute-start.17 = (bf16[192,768]{1,0:T(8,128)(2,1)}, bf16[192,768]{1,0:T(8,128)(2,1)}, u32[]{:S(2)}, u32[]{:S(2)}) collective-permute-start(bf16[192,768]{1,0:T(8,128)(2,1)} %pad_maximum_fusion.9), channel_id=1, source_target_pairs={{0,16},{8,24},{16,0},{24,8},{1,17},{9,25},{17,1},{25,9},{2,18},{10... | collective-permute-start | bytes 884744 | tf_op jit(solution)/shard_map/ppermute | solution.py:95
  124.1 28.9 %collective-permute-start.18 = (bf16[192,768]{1,0:T(8,128)(2,1)}, bf16[192,768]{1,0:T(8,128)(2,1)}, u32[]{:S(2)}, u32[]{:S(2)}) collective-permute-start(bf16[192,768]{1,0:T(8,128)(2,1)} %pad_maximum_fusion.9), channel_id=1, source_target_pairs={{0,24},{8,0},{16,8},{24,16},{1,25},{9,1},{17,9},{25,17},{2,26},{10... | collective-permute-start | bytes 884744 | tf_op jit(solution)/shard_map/ppermute | solution.py:95
  126.4 12.1 collective-permute-start.12
  135.6 48.1 %collective-permute-start.19 = (bf16[96,6656]{1,0:T(8,128)(2,1)}, bf16[96,6656]{1,0:T(8,128)(2,1)}, u32[]{:S(2)}, u32[]{:S(2)}) collective-permute-start(bf16[96,6656]{1,0:T(8,128)(2,1)} %get-tuple-element.256), channel_id=1, source_target_pairs={{0,4},{4,0},{1,5},{5,1},{2,6},{6,2},{3,7},{7,3},{8,12},{12,8},{9,1... | collective-permute-start | bytes 3833864 | tf_op jit(solution)/shard_map/ppermute | solution.py:106
  139.5 100.9 %copy-start.74 = (bf16[514,80]{1,0:T(8,128)(2,1)}, bf16[514,80]{1,0:T(8,128)(2,1)S(1)}, u32[]{:S(2)}) copy-start(bf16[514,80]{1,0:T(8,128)(2,1)S(1)} %get-tuple-element.75) | copy-start | bytes 246724
  145.1 18.8 %collective-permute-start.13 = (bf16[192,768]{1,0:T(8,128)(2,1)S(1)}, bf16[192,768]{1,0:T(8,128)(2,1)S(1)}, u32[]{:S(2)}, u32[]{:S(2)}) collective-permute-start(bf16[192,768]{1,0:T(8,128)(2,1)S(1)} %constant_dynamic-update-slice_fusion.5), channel_id=1, source_target_pairs={{0,8},{8,16},{16,24},{24,0},{1,9},{9,17},{17,25},{25,1},{2,10},{10... | collective-permute-start | bytes 884744 | tf_op jit(solution)/shard_map/ppermute | solution.py:95
  154.0 20.2 %collective-permute-start.14 = (bf16[192,768]{1,0:T(8,128)(2,1)S(1)}, bf16[192,768]{1,0:T(8,128)(2,1)S(1)}, u32[]{:S(2)}, u32[]{:S(2)}) collective-permute-start(bf16[192,768]{1,0:T(8,128)(2,1)S(1)} %constant_dynamic-update-slice_fusion.5), channel_id=1, source_target_pairs={{0,16},{8,24},{16,0},{24,8},{1,17},{9,25},{17,1},{25,9},{2,18},{10... | collective-permute-start | bytes 884744 | tf_op jit(solution)/shard_map/ppermute | solution.py:95
  157.4 17.5 %collective-permute-start.15 = (bf16[192,768]{1,0:T(8,128)(2,1)S(1)}, bf16[192,768]{1,0:T(8,128)(2,1)S(1)}, u32[]{:S(2)}, u32[]{:S(2)}) collective-permute-start(bf16[192,768]{1,0:T(8,128)(2,1)S(1)} %constant_dynamic-update-slice_fusion.5), channel_id=1, source_target_pairs={{0,24},{8,0},{16,8},{24,16},{1,25},{9,1},{17,9},{25,17},{2,26},{10... | collective-permute-start | bytes 884744 | tf_op jit(solution)/shard_map/ppermute | solution.py:95
  196.8 8.4 collective-permute-start.3
  201.2 131.0 %copy-start.226 = (f32[768]{0:T(1024)}, f32[768]{0:T(1024)S(1)}, u32[]{:S(2)}) copy-start(f32[768]{0:T(1024)S(1)} %get-tuple-element.140) | copy-start | bytes 9220
  201.2 131.0 %copy-start.267 = (f32[768]{0:T(1024)}, f32[768]{0:T(1024)S(1)}, u32[]{:S(2)}) copy-start(f32[768]{0:T(1024)S(1)} %get-tuple-element.139) | copy-start | bytes 9220
  217.1 14.3 %all-to-all-start.1 = ((bf16[8,256,96]{1,2,0:T(8,128)(2,1)}), bf16[8,256,96]{1,2,0:T(8,128)(2,1)}, u32[]{:S(2)}, u32[]{:S(2)}) async-start(bf16[8,256,96]{1,2,0:T(8,128)(2,1)} %copy.583), calls=%async_computation.2 | async-start | bytes 786432 | tf_op jit(solution)/shard_map/all_to_all | solution.py:606
  221.2 268.5 %all-gather.13.cloned.1.call-start = ((), (), s32[]{:S(2)}) async-start(), calls=%async_computation.12 | async-start | bytes 12779520 | tf_op jit(solution)/shard_map/all_gather | solution.py:697
  234.9 164.3 %copy-start.3 = (f32[256,768]{1,0:T(8,128)}, f32[256,768]{1,0:T(8,128)S(1)}, u32[]{:S(2)}) copy-start(f32[256,768]{1,0:T(8,128)S(1)} %get-tuple-element.224) | copy-start | bytes 2359300
  262.1 12.7 collective-permute-start.20
  262.3 121.9 %copy-start.93 = (bf16[256,768]{1,0:T(8,128)(2,1)}, bf16[256,768]{1,0:T(8,128)(2,1)S(1)}, u32[]{:S(2)}) copy-start(bf16[256,768]{1,0:T(8,128)(2,1)S(1)} %add_convert_fusion.15) | copy-start | bytes 1179652
  262.3 110.1 %collective-permute-start.11 = (bf16[256,768]{1,0:T(8,128)(2,1)S(1)}, bf16[256,768]{1,0:T(8,128)(2,1)}, u32[]{:S(2)}, u32[]{:S(2)}) collective-permute-start(bf16[256,768]{1,0:T(8,128)(2,1)S(1)} %add_convert_fusion.15), channel_id=1, source_target_pairs={{0,1},{1,0},{2,3},{3,2},{4,5},{5,4},{6,7},{7,6},{8,9},{9,8},{10,11... | collective-permute-start | bytes 1179656 | tf_op jit(solution)/shard_map/ppermute | solution.py:510
  274.7 248.6 %all-gather.15.cloned.1.call-start = ((), (), s32[]{:S(2)}) async-start(), calls=%async_computation.13 | async-start | bytes 3538944 | tf_op jit(solution)/shard_map/all_gather | solution.py:781
  363.7 58.0 %collective-permute-start.21 = (bf16[512,768]{1,0:T(8,128)(2,1)}, bf16[512,768]{1,0:T(8,128)(2,1)}, u32[]{:S(2)}, u32[]{:S(2)}) collective-permute-start(bf16[512,768]{1,0:T(8,128)(2,1)} %add_convert_fusion.6), channel_id=1, source_target_pairs={{0,1},{1,0},{2,3},{3,2},{4,5},{5,4},{6,7},{7,6},{8,9},{9,8},{10,11... | collective-permute-start | bytes 2359304 | tf_op jit(solution)/shard_map/ppermute | solution.py:510
  492.1 217.6 %reduce-scatter.9.cloned.1.call-start = ((), (), s32[]{:S(2)}) async-start(), calls=%async_computation.14 | async-start | bytes 3538944 | tf_op jit(solution)/shard_map/reduce_scatter | solution.py:801
  663.3 233.0 %reduce-scatter.11.cloned.1.call-start = ((), (), s32[]{:S(2)}) async-start(), calls=%async_computation.15 | async-start | bytes 12779520 | tf_op jit(solution)/shard_map/reduce_scatter | solution.py:804
  769.0 21.8 %collective-permute-start.24 = (bf16[256,768]{1,0:T(8,128)(2,1)S(1)}, bf16[256,768]{1,0:T(8,128)(2,1)S(1)}, u32[]{:S(2)}, u32[]{:S(2)}) collective-permute-start(bf16[256,768]{1,0:T(8,128)(2,1)S(1)} %slice.670), channel_id=1, source_target_pairs={{0,1},{1,0},{2,3},{3,2},{4,5},{5,4},{6,7},{7,6},{8,9},{9,8},{10,11... | collective-permute-start | bytes 1179656 | tf_op jit(solution)/shard_map/ppermute | solution.py:516
  794.9 29.0 %all-to-all-start.3 = ((bf16[8,256,96]{1,2,0:T(8,128)(2,1)}), bf16[8,256,96]{1,2,0:T(8,128)(2,1)S(1)}, u32[]{:S(2)}, u32[]{:S(2)}) async-start(bf16[8,256,96]{1,2,0:T(8,128)(2,1)} %bitcast.199), calls=%async_computation.8 | async-start | bytes 786432 | tf_op jit(solution)/shard_map/all_to_all | solution.py:880
  800.5 254.1 %all-gather.17.cloned.1.call-start = ((), (), s32[]{:S(2)}) async-start(), calls=%async_computation.18 | async-start | bytes 1966080 | tf_op jit(solution)/shard_map/all_gather | solution.py:882
  824.7 279.6 %reduce-scatter.15.cloned.1.call-start = ((), (), s32[]{:S(2)}) async-start(), calls=%async_computation.17 | async-start | bytes 21233664 | tf_op jit(solution)/shard_map/reduce_scatter | solution.py:825
  862.8 327.8 %reduce-scatter.13.cloned.1.call-start = ((), (), s32[]{:S(2)}) async-start(), calls=%async_computation.16 | async-start | bytes 19906560 | tf_op jit(solution)/shard_map/reduce_scatter | solution.py:825
  864.4 2.4 collective-permute-start.22
  967.0 47.4 %collective-permute-start.23 = (bf16[512,768]{1,0:T(8,128)(2,1)}, bf16[512,768]{1,0:T(8,128)(2,1)}, u32[]{:S(2)}, u32[]{:S(2)}) collective-permute-start(bf16[512,768]{1,0:T(8,128)(2,1)} %slice.668), channel_id=1, source_target_pairs={{0,1},{1,0},{2,3},{3,2},{4,5},{5,4},{6,7},{7,6},{8,9},{9,8},{10,11... | collective-permute-start | bytes 2359304 | tf_op jit(solution)/shard_map/ppermute | solution.py:516
  1092.5 65.7 %collective-permute-start.28 = (bf16[96,6656]{1,0:T(8,128)(2,1)}, bf16[96,6656]{1,0:T(8,128)(2,1)}, u32[]{:S(2)}, u32[]{:S(2)}) collective-permute-start(bf16[96,6656]{1,0:T(8,128)(2,1)} %get-tuple-element.254), channel_id=1, source_target_pairs={{0,4},{4,0},{1,5},{5,1},{2,6},{6,2},{3,7},{7,3},{8,12},{12,8},{9,1... | collective-permute-start | bytes 3833864 | tf_op jit(solution)/shard_map/ppermute | solution.py:106
  1107.1 18.4 %collective-permute-start.25 = (bf16[384,768]{1,0:T(8,128)(2,1)}, bf16[384,768]{1,0:T(8,128)(2,1)}, u32[]{:S(2)}, u32[]{:S(2)}) collective-permute-start(bf16[384,768]{1,0:T(8,128)(2,1)} %get-tuple-element.259), channel_id=1, source_target_pairs={{0,8},{8,16},{16,24},{24,0},{1,9},{9,17},{17,25},{25,1},{2,10},{10... | collective-permute-start | bytes 1769480 | tf_op jit(solution)/shard_map/ppermute | solution.py:106
  1107.9 42.1 %collective-permute-start.26 = (bf16[384,768]{1,0:T(8,128)(2,1)}, bf16[384,768]{1,0:T(8,128)(2,1)}, u32[]{:S(2)}, u32[]{:S(2)}) collective-permute-start(bf16[384,768]{1,0:T(8,128)(2,1)} %get-tuple-element.261), channel_id=1, source_target_pairs={{0,16},{8,24},{16,0},{24,8},{1,17},{9,25},{17,1},{25,9},{2,18},{10... | collective-permute-start | bytes 1769480 | tf_op jit(solution)/shard_map/ppermute | solution.py:106
  1110.6 39.5 %collective-permute-start.27 = (bf16[384,768]{1,0:T(8,128)(2,1)}, bf16[384,768]{1,0:T(8,128)(2,1)}, u32[]{:S(2)}, u32[]{:S(2)}) collective-permute-start(bf16[384,768]{1,0:T(8,128)(2,1)} %get-tuple-element.260), channel_id=1, source_target_pairs={{0,24},{8,0},{16,8},{24,16},{1,25},{9,1},{17,9},{25,17},{2,26},{10... | collective-permute-start | bytes 1769480 | tf_op jit(solution)/shard_map/ppermute | solution.py:106
  1154.1 15.7 %all-to-all-start.2 = ((bf16[4,192,192]{2,1,0:T(8,128)(2,1)}), bf16[4,192,192]{2,1,0:T(8,128)(2,1)}, u32[]{:S(2)}, u32[]{:S(2)}) async-start(bf16[4,192,192]{2,1,0:T(8,128)(2,1)} %bitcast.573), calls=%async_computation.7 | async-start | bytes 786432 | tf_op jit(solution)/shard_map/all_to_all | solution.py:829
  1158.2 97.0 %reduce-scatter.17.cloned.1.call-start = ((), (), s32[]{:S(2)}) async-start(), calls=%async_computation.19 | async-start | bytes 2875392 | tf_op jit(solution)/shard_map/reduce_scatter | solution.py:958
  1193.3 17.6 %collective-permute-start.29 = (bf16[360,768]{1,0:T(8,128)(2,1)}, bf16[360,768]{1,0:T(8,128)(2,1)S(1)}, u32[]{:S(2)}, u32[]{:S(2)}) collective-permute-start(bf16[360,768]{1,0:T(8,128)(2,1)} %get-tuple-element.262), channel_id=1, source_target_pairs={{0,8},{8,16},{16,24},{24,0},{1,9},{9,17},{17,25},{25,1},{2,10},{10... | collective-permute-start | bytes 1658888 | tf_op jit(solution)/shard_map/ppermute | solution.py:106
  1194.8 38.9 %collective-permute-start.30 = (bf16[360,768]{1,0:T(8,128)(2,1)}, bf16[360,768]{1,0:T(8,128)(2,1)}, u32[]{:S(2)}, u32[]{:S(2)}) collective-permute-start(bf16[360,768]{1,0:T(8,128)(2,1)} %get-tuple-element.264), channel_id=1, source_target_pairs={{0,16},{8,24},{16,0},{24,8},{1,17},{9,25},{17,1},{25,9},{2,18},{10... | collective-permute-start | bytes 1658888 | tf_op jit(solution)/shard_map/ppermute | solution.py:106
  1197.1 36.5 %collective-permute-start.31 = (bf16[360,768]{1,0:T(8,128)(2,1)}, bf16[360,768]{1,0:T(8,128)(2,1)}, u32[]{:S(2)}, u32[]{:S(2)}) collective-permute-start(bf16[360,768]{1,0:T(8,128)(2,1)} %get-tuple-element.263), channel_id=1, source_target_pairs={{0,24},{8,0},{16,8},{24,16},{1,25},{9,1},{17,9},{25,17},{2,26},{10... | collective-permute-start | bytes 1658888 | tf_op jit(solution)/shard_map/ppermute | solution.py:106
  1237.7 10.6 all-to-all-start.4
  1241.2 94.5 %all-gather.19.cloned.1.call-start = ((), (), s32[]{:S(2)}) async-start(), calls=%async_computation.20 | async-start | bytes 2875392 | tf_op jit(solution)/shard_map/all_gather | solution.py:960
  1255.2 33.7 %collective-permute-start.32 = (f32[104,768]{1,0:T(8,128)}, f32[104,768]{1,0:T(8,128)}, u32[]{:S(2)}, u32[]{:S(2)}) collective-permute-start(f32[104,768]{1,0:T(8,128)} %reduce-scatter.17.cloned.1.call-done), channel_id=1, source_target_pairs={{0,16},{8,24},{16,0},{24,8},{1,17},{9,25},{17,1},{25,9},{2,18},{10... | collective-permute-start | bytes 958472 | tf_op jit(solution)/shard_map/ppermute | solution.py:95
  1266.5 22.4 %collective-permute-start.33 = (f32[104,768]{1,0:T(8,128)}, f32[104,768]{1,0:T(8,128)}, u32[]{:S(2)}, u32[]{:S(2)}) collective-permute-start(f32[104,768]{1,0:T(8,128)} %reduce-scatter.17.cloned.1.call-done), channel_id=1, source_target_pairs={{0,8},{8,16},{16,24},{24,0},{1,9},{9,17},{17,25},{25,1},{2,10},{10... | collective-permute-start | bytes 958472 | tf_op jit(solution)/shard_map/ppermute | solution.py:95
  1268.8 20.1 %collective-permute-start.34 = (f32[104,768]{1,0:T(8,128)}, f32[104,768]{1,0:T(8,128)}, u32[]{:S(2)}, u32[]{:S(2)}) collective-permute-start(f32[104,768]{1,0:T(8,128)} %reduce-scatter.17.cloned.1.call-done), channel_id=1, source_target_pairs={{0,24},{8,0},{16,8},{24,16},{1,25},{9,1},{17,9},{25,17},{2,26},{10... | collective-permute-start | bytes 958472 | tf_op jit(solution)/shard_map/ppermute | solution.py:95
  1292.3 13.3 collective-permute-start.35
  1301.6 5.6 collective-permute-start.36
  1301.8 5.3 collective-permute-start.37
  1307.2 3.5 collective-permute-start.38
  1310.7 3.5 collective-permute-start.39
  1312.4 3.0 collective-permute-start.40
  1312.4 3.0 collective-permute-start.41
  (317 other events, 1957.6 us)
Sparse Core Ops, SparseCore 0:
  49.5 57.5 all-gather.20
  117.5 86.5 all-gather.24
  206.6 101.9 all-gather.22
  310.0 179.6 all-gather.12
  492.3 30.9 all-gather.14
  663.4 46.2 reduce-scatter.8
  712.1 180.0 reduce-scatter.10
  895.8 127.3 reduce-scatter.14
  1039.2 151.3 reduce-scatter.12
  1194.4 43.3 reduce-scatter.16
  1305.8 28.2 all-gather.18
Sparse Core Ops, SparseCore 1:
  92.2 28.2 reduce-scatter.6
  824.8 17.6 all-gather.16
